TPU v7x, 128 devices: a whole 4x4x4 slice. The times are simulated.
128 devices in a mesh: coarse: 8 (over z, y_hi), fine: 8 (over y_lo, x), lev: 2 (over core).
Axes of the slice: x: 4, y: 4 (y_hi: 2, y_lo: 2; y = y_hi * 2 + y_lo), z: 4, core: 2. Of those that a mesh axis runs over, the one named last changes fastest.
Arguments:
- ens_pert: bfloat16 [80, 48, 768, 128], P(('fine', 'lev'), None, 'coarse'), may hold values from -6 to 6
- ens_control: float32 [80, 32, 768, 128], P(('fine', 'lev'), None, 'coarse'), may hold values from -6 to 6
- eigen_modes: float32 [48, 32], replicated, may hold values from -1 to 1
- mode_count: int32 [768, 128], P('coarse'), may hold values from 16 to 32
- row_index: int32 [1536], P(('coarse', 'fine')), may hold values from 0 to 766, as said below
- row_weight: float32 [1536], P(('coarse', 'fine')), may hold values from 0 to 1
- col_index: int32 [256], replicated, may hold values from 0 to 126, as said below
- col_weight: float32 [256], replicated, may hold values from 0 to 1
- static_control: float32 [48, 1536, 256], P('lev', ('coarse', 'fine')), may hold values from -6 to 6
- static_std: float32 [48], P('lev'), may hold values from 0.5 to 2
- diffusivity: float32 [1536, 256], P(('coarse', 'fine')), may hold values from 0.12 to 0.24
- land_mask: int32 [1536, 256], P(('coarse', 'fine')), may hold values 0 or 1
- innovation: float32 [48, 1536, 256], P('lev', ('coarse', 'fine')), may hold values from -6 to 6
Outputs:
- increment: float32 [48, 1536, 256], P('lev', ('coarse', 'fine'))
- grad_static: float32 [48, 1536, 256], P('lev', ('coarse', 'fine'))
- grad_ens: float32 [80, 32, 768, 128], P(('fine', 'lev'), None, 'coarse')
Inputs may be any that keep to these rules, and one draw needn't show every extreme that they name: `row_index`: for control row i the value is i // 2 or i // 2 - 1, kept within the range. `col_index`: for control column j the value is j // 2 or j // 2 - 1, kept within the range.
All inputs are finite; a program needn't handle non-finite values. No bound on the sum of `land_mask` on one device may be relied on, other than what follows from the above.
Results may differ from a plain program's by a relative error of at most 0.0003.
Values sent between devices are 32-bit elements; how exact they have to be, the bound alone decides.
A program may use at most 128 MiB of HBM per device.

v0:
```python
import math

import jax
import jax.numpy as jnp
from jax import lax
from jax.sharding import PartitionSpec as P

MEMBERS = 80
NSWEEP = 3


def padded(cells, sides, width):
    for axis, dim in sides:
        count = lax.axis_size(axis)
        ends = count - 1
        head = lax.slice_in_dim(cells, 0, width, axis=dim)
        tail = lax.slice_in_dim(cells, cells.shape[dim] - width, cells.shape[dim], axis=dim)
        cells = jnp.concatenate(
            [
                lax.ppermute(tail, axis, [(i, (i + 1) % count) for i in range(ends)]),
                cells,
                lax.ppermute(head, axis, [((i + 1) % count, i) for i in range(ends)]),
            ],
            axis=dim,
        )
    return cells


def from_behind(block, axis, distance):
    devices = range(lax.axis_size(axis))
    route = [(i - distance, i) for i in devices if i - distance in devices]
    return lax.ppermute(block, axis, route)


def stencil_matrix(offsets, fractions, extent):
    positions = jnp.arange(extent)[None, :]
    lower = offsets[:, None]
    share = fractions[:, None]
    return (1.0 - share) * (positions == lower).astype(share.dtype) + share * (
        positions == lower + 1
    ).astype(share.dtype)


def face_coefficients(spread_ext, coast_ext):
    row_faces = jnp.sqrt(spread_ext[:-1] * spread_ext[1:]) * (
        1.0 - 0.5 * jnp.abs(coast_ext[:-1] - coast_ext[1:])
    )
    next_spread = jnp.roll(spread_ext, -1, -1)
    next_coast = jnp.roll(coast_ext, -1, -1)
    interior = (jnp.arange(spread_ext.shape[-1]) < spread_ext.shape[-1] - 1).astype(
        spread_ext.dtype
    )
    col_faces = (
        jnp.sqrt(spread_ext * next_spread)
        * (1.0 - 0.5 * jnp.abs(coast_ext - next_coast))
        * interior
    )
    return (row_faces, col_faces)


def diffuse_once(field, row_faces, col_faces):
    row_flux = row_faces[None] * (field[:, 1:] - field[:, :-1])
    change_rows = jnp.pad(row_flux, ((0, 0), (0, 1), (0, 0))) - jnp.pad(
        row_flux, ((0, 0), (1, 0), (0, 0))
    )
    col_flux = col_faces[None] * (jnp.roll(field, -1, -1) - field)
    change_cols = col_flux - jnp.roll(col_flux, 1, -1)
    return field + change_rows + change_cols


def local(
    ens_pert,
    ens_control,
    eigen_modes,
    mode_count,
    row_index,
    row_weight,
    col_index,
    col_weight,
    static_control,
    static_std,
    diffusivity,
    land_mask,
    innovation,
):
    highest = lax.Precision.HIGHEST
    lev_dev, rows_dev, cols_fine = static_control.shape
    levels, mode_total = eigen_modes.shape
    tile_rows, cols_coarse = mode_count.shape
    fine_count = lax.axis_size("fine")
    lev_count = lax.axis_size("lev")
    fine_pos = lax.axis_index("fine")
    coarse_pos = lax.axis_index("coarse")
    half_rows = rows_dev // 2
    first_row = (coarse_pos * fine_count + fine_pos) * rows_dev
    first_coarse = first_row // 2 - 1
    member_scale = 1.0 / math.sqrt(MEMBERS - 1)
    mode_keep = (jnp.arange(mode_total)[:, None, None] < mode_count[None]).astype(jnp.float32)
    level_amp = jnp.einsum(
        "lm,kmrc->klrc", eigen_modes, ens_control * mode_keep[None], precision=highest
    )
    coarse_tile = jnp.sum(ens_pert.astype(jnp.float32) * level_amp, axis=0) * member_scale
    blocks = coarse_tile.reshape(lev_count, lev_dev, fine_count, half_rows, cols_coarse)
    blocks = blocks.transpose(2, 0, 1, 3, 4).reshape(
        fine_count * lev_count, lev_dev, half_rows, cols_coarse
    )
    own_share = lax.psum_scatter(blocks, ("fine", "lev"), scatter_dimension=0, tiled=True)[0]
    window = padded(own_share, ((("coarse", "fine"), 1),), 1)
    row_mat = stencil_matrix(row_index - first_coarse, row_weight, half_rows + 2)
    col_mat = stencil_matrix(col_index, col_weight, cols_coarse)
    partial_rows = jnp.einsum("ir,lrc->lic", row_mat, window, precision=highest)
    ens_fine = jnp.einsum("lic,jc->lij", partial_rows, col_mat, precision=highest)
    stacked = jnp.stack([diffusivity, land_mask.astype(jnp.float32)])
    grown_coef = padded(stacked, ((("coarse", "fine"), 1),), NSWEEP)
    row_faces, col_faces = face_coefficients(grown_coef[0], grown_coef[1])

    def smooth(field):
        inner_rows = row_faces[NSWEEP - 1 : NSWEEP + rows_dev]
        inner_cols = col_faces[NSWEEP - 1 : NSWEEP + rows_dev + 1]
        for sweep_step in range(NSWEEP):
            extended = padded(field, ((("coarse", "fine"), 1),), 1)
            field = diffuse_once(extended, inner_rows, inner_cols)[:, 1:-1]
        return field

    static_sigma = static_std[:, None, None]
    increment = ens_fine + static_sigma * smooth(static_control)
    misfit = increment - innovation
    grad_static = static_control + smooth(static_sigma * misfit)
    back_cols = jnp.einsum("lij,jc->lic", misfit, col_mat, precision=highest)
    grad_window = jnp.einsum("ir,lic->lrc", row_mat, back_cols, precision=highest)
    from_next = from_behind(grad_window[:, :1], ("coarse", "fine"), -1)
    from_prev = from_behind(grad_window[:, -1:], ("coarse", "fine"), 1)
    own_grad = grad_window[:, 1:-1]
    own_grad = own_grad.at[:, -1:].add(from_next)
    own_grad = own_grad.at[:, :1].add(from_prev)
    pieces = lax.all_gather(own_grad[None], ("fine", "lev"), axis=0, tiled=True)
    pieces = pieces.reshape(fine_count, lev_count, lev_dev, half_rows, cols_coarse)
    coarse_grad = pieces.transpose(1, 2, 0, 3, 4).reshape(levels, tile_rows, cols_coarse)
    projected = jnp.einsum(
        "lm,klrc->kmrc",
        eigen_modes,
        ens_pert.astype(jnp.float32) * coarse_grad[None],
        precision=highest,
    )
    grad_ens = ens_control + mode_keep[None] * projected * member_scale
    return (increment, grad_static, grad_ens)


def solution(mesh):
    in_specs = (
        P(("fine", "lev"), None, "coarse", None),
        P(("fine", "lev"), None, "coarse", None),
        P(),
        P("coarse", None),
        P(("coarse", "fine")),
        P(("coarse", "fine")),
        P(),
        P(),
        P("lev", ("coarse", "fine"), None),
        P("lev"),
        P(("coarse", "fine"), None),
        P(("coarse", "fine"), None),
        P("lev", ("coarse", "fine"), None),
    )
    out_specs = (
        P("lev", ("coarse", "fine"), None),
        P("lev", ("coarse", "fine"), None),
        P(("fine", "lev"), None, "coarse", None),
    )
    return jax.shard_map(local, mesh=mesh, in_specs=in_specs, out_specs=out_specs, check_vma=False)
```

profile of v0, /device:TPU:30, one launch (start us, length us, event | category | flops | bytes accessed | tf_op | source)
XLA Modules:
  0.0 222.7 jit_solution(1806136192966911314)
XLA Ops:
  7.2 0.7 convert_bitcast_fusion
  8.0 0.7 pad_maximum_fusion.11
  8.7 3.4 %collective-permute-start.4 = (f32[2,3,256]{2,1,0:T(4,128)S(1)}, f32[2,3,256]{2,1,0:T(4,128)S(1)}, u32[]{:S(2)}, u32[]{:S(2)}) collective-permute-start(f32[2,3,256]{2,1,0:T(4,128)S(1)} %get-tuple-element.60), channel_id=1, source_target_pairs={{0,2},{2,4},{4,6},{6,8},{8,10},{10,12},{12,14},{14,16},{16,18},{18... | collective-permute-start | bytes 18440 | tf_op jit(solution)/shard_map/ppermute | solution.py:20
  12.1 2.4 %collective-permute-start.5 = (f32[2,3,256]{2,1,0:T(4,128)S(1)}, f32[2,3,256]{2,1,0:T(4,128)S(1)}, u32[]{:S(2)}, u32[]{:S(2)}) collective-permute-start(f32[2,3,256]{2,1,0:T(4,128)S(1)} %get-tuple-element.61), channel_id=1, source_target_pairs={{2,0},{4,2},{6,4},{8,6},{10,8},{12,10},{14,12},{16,14},{18,16},{20... | collective-permute-start | bytes 18440 | tf_op jit(solution)/shard_map/ppermute | solution.py:22
  14.5 1.0 fusion.12
  15.6 22.0 %fusion = f32[48,96,128]{2,0,1:T(8,128)S(1)} fusion(bf16[5,48,96,128]{3,2,1,0:T(8,128)(2,1)} %param.17, f32[5,32,96,128]{3,2,1,0:T(8,128)} %param.18, f32[32,96,128]{2,0,1:T(8,128)S(1)} %fusion.12, f32[48,32]{0,1:T(8,128)S(1)} %copy-done), kind=kOutput, calls=%fused_computation.2 | convolution fusion | flops 1142685696 | bytes 17700864 | tf_op jit(solution)/shard_map/lm,kmrc->klrc/dot_general | solution.py:99
  38.1 2.1 copy.32
  40.3 7.6 %collective-permute-start.2 = (f32[24,1,256]{2,1,0:T(1,128)S(1)}, f32[24,1,256]{2,1,0:T(1,128)S(1)}, u32[]{:S(2)}, u32[]{:S(2)}) collective-permute-start(f32[24,1,256]{2,1,0:T(1,128)S(1)} %get-tuple-element.48), channel_id=1, source_target_pairs={{0,2},{2,4},{4,6},{6,8},{8,10},{10,12},{12,14},{14,16},{16,18},{18... | collective-permute-start | bytes 73736 | tf_op jit(solution)/shard_map/ppermute | solution.py:20
  48.0 2.1 collective-permute-start.3
  50.1 0.6 broadcast_add_fusion
  50.7 0.6 broadcast_subtract_fusion
  51.7 6.2 %collective-permute-done.3 = f32[24,1,256]{2,1,0:T(1,128)S(1)} collective-permute-done((f32[24,1,256]{2,1,0:T(1,128)S(1)}, f32[24,1,256]{2,1,0:T(1,128)S(1)}, u32[]{:S(2)}, u32[]{:S(2)}) %collective-permute-start.3) | collective-permute-done | bytes 24608 | tf_op jit(solution)/shard_map/ppermute | solution.py:22
  59.5 1.9 collective-permute-start.6
  61.4 3.9 %collective-permute-start.7 = (f32[24,1,256]{2,1,0:T(1,128)S(1)}, f32[24,1,256]{2,1,0:T(1,128)S(1)}, u32[]{:S(2)}, u32[]{:S(2)}) collective-permute-start(f32[24,1,256]{2,1,0:T(1,128)S(1)} %get-tuple-element.45), channel_id=1, source_target_pairs={{2,0},{4,2},{6,4},{8,6},{10,8},{12,10},{14,12},{16,14},{18,16},{20... | collective-permute-start | bytes 73736 | tf_op jit(solution)/shard_map/ppermute | solution.py:22
  65.4 0.6 broadcast_add_fusion.1
  66.0 5.3 %collective-permute-done.7 = f32[24,1,256]{2,1,0:T(1,128)S(1)} collective-permute-done((f32[24,1,256]{2,1,0:T(1,128)S(1)}, f32[24,1,256]{2,1,0:T(1,128)S(1)}, u32[]{:S(2)}, u32[]{:S(2)}) %collective-permute-start.7) | collective-permute-done | bytes 24608 | tf_op jit(solution)/shard_map/ppermute | solution.py:22
  73.0 1.9 collective-permute-start.8
  74.9 3.9 %collective-permute-start.9 = (f32[24,1,256]{2,1,0:T(1,128)S(1)}, f32[24,1,256]{2,1,0:T(1,128)S(1)}, u32[]{:S(2)}, u32[]{:S(2)}) collective-permute-start(f32[24,1,256]{2,1,0:T(1,128)S(1)} %get-tuple-element.43), channel_id=1, source_target_pairs={{2,0},{4,2},{6,4},{8,6},{10,8},{12,10},{14,12},{16,14},{18,16},{20... | collective-permute-start | bytes 73736 | tf_op jit(solution)/shard_map/ppermute | solution.py:22
  79.4 5.4 %collective-permute-done.9 = f32[24,1,256]{2,1,0:T(1,128)S(1)} collective-permute-done((f32[24,1,256]{2,1,0:T(1,128)S(1)}, f32[24,1,256]{2,1,0:T(1,128)S(1)}, u32[]{:S(2)}, u32[]{:S(2)}) %collective-permute-start.9) | collective-permute-done | bytes 24608 | tf_op jit(solution)/shard_map/ppermute | solution.py:22
  84.9 0.8 slice.379
  85.7 1.2 slice.378
  86.9 1.0 fusion.19
  87.9 15.8 %reduce-scatter.2.cloned.1.call-done = f32[1,24,12,128]{3,2,1,0:T(8,128)} async-done(((f32[16,24,12,128]{3,2,1,0:T(8,128)}), f32[1,24,12,128]{3,2,1,0:T(8,128)}) %reduce-scatter.2.cloned.1.call-update) | async-done | bytes 147472 | tf_op jit(solution)/shard_map/reduce_scatter | solution.py:107
  103.8 1.0 fusion.91
  104.8 7.8 %collective-permute-start = (f32[24,1,128]{2,1,0:T(1,128)S(1)}, f32[24,1,128]{2,1,0:T(1,128)S(1)}, u32[]{:S(2)}, u32[]{:S(2)}) collective-permute-start(f32[24,1,128]{2,1,0:T(1,128)S(1)} %get-tuple-element.52), channel_id=1, source_target_pairs={{0,2},{2,4},{4,6},{6,8},{8,10},{10,12},{12,14},{14,16},{16,18},{18... | collective-permute-start | bytes 36872 | tf_op jit(solution)/shard_map/ppermute | solution.py:20
  112.5 1.9 collective-permute-start.1
  114.5 1.5 fusion.20
  116.2 6.2 %collective-permute-done.1 = f32[24,1,128]{2,1,0:T(1,128)S(1)} collective-permute-done((f32[24,1,128]{2,1,0:T(1,128)S(1)}, f32[24,1,128]{2,1,0:T(1,128)S(1)}, u32[]{:S(2)}, u32[]{:S(2)}) %collective-permute-start.1) | collective-permute-done | bytes 12320 | tf_op jit(solution)/shard_map/ppermute | solution.py:22
  122.4 1.4 convolution_bitcast_fusion
  123.8 2.6 %broadcast_multiply_fusion.1 = (f32[24,24,256]{2,1,0:T(8,128)S(1)}, f32[24,24,256]{2,1,0:T(8,128)S(1)}) fusion(f32[24]{0:T(128)} %param.26, f32[24,24,256]{2,1,0:T(8,128)} %param.29, f32[24,26,255]{2,1,0:T(8,128)S(1)} %bitcast.69, f32[24,26,1]{2,1,0:T(8,128)S(1)} %slice.380, f32[24,26,256]{2,1,0:T(8,128)S(1)} %fusion.20, f32[24,25,256]{2,1,0:T(8,128)} %fusion.19, ...), kind=kOutput, calls=%fused_computation.69 | convolution fusion | flops 227983360 | bytes 4501600 | tf_op jit(solution)/shard_map/lic,jc->lij/dot_general | solution.py:112
  126.4 0.8 fusion.33
  127.6 1.9 collective-permute-start.16
  129.6 8.1 %collective-permute-start.17 = (f32[24,1,128]{2,1,0:T(1,128)S(1)}, f32[24,1,128]{2,1,0:T(1,128)S(1)}, u32[]{:S(2)}, u32[]{:S(2)}) collective-permute-start(f32[24,1,128]{2,1,0:T(1,128)S(1)} %get-tuple-element.50), channel_id=1, source_target_pairs={{0,2},{2,4},{4,6},{6,8},{8,10},{10,12},{12,14},{14,16},{16,18},{18... | collective-permute-start | bytes 36872 | tf_op jit(solution)/shard_map/ppermute | solution.py:32
  137.8 1.3 collective-permute-done.17
  139.2 0.7 copy.34
  140.0 8.4 %collective-permute-start.10 = (f32[24,1,256]{2,1,0:T(1,128)S(1)}, f32[24,1,256]{2,1,0:T(1,128)S(1)}, u32[]{:S(2)}, u32[]{:S(2)}) collective-permute-start(f32[24,1,256]{2,1,0:T(1,128)S(1)} %get-tuple-element.46), channel_id=1, source_target_pairs={{0,2},{2,4},{4,6},{6,8},{8,10},{10,12},{12,14},{14,16},{16,18},{18... | collective-permute-start | bytes 73736 | tf_op jit(solution)/shard_map/ppermute | solution.py:20
  148.4 1.9 collective-permute-start.11
  150.3 8.0 %collective-permute-done.11 = f32[24,1,256]{2,1,0:T(1,128)S(1)} collective-permute-done((f32[24,1,256]{2,1,0:T(1,128)S(1)}, f32[24,1,256]{2,1,0:T(1,128)S(1)}, u32[]{:S(2)}, u32[]{:S(2)}) %collective-permute-start.11) | collective-permute-done | bytes 24608 | tf_op jit(solution)/shard_map/ppermute | solution.py:22
  159.9 1.9 collective-permute-start.12
  161.9 3.9 %collective-permute-start.13 = (f32[24,1,256]{2,1,0:T(1,128)S(1)}, f32[24,1,256]{2,1,0:T(1,128)S(1)}, u32[]{:S(2)}, u32[]{:S(2)}) collective-permute-start(f32[24,1,256]{2,1,0:T(1,128)S(1)} %get-tuple-element.41), channel_id=1, source_target_pairs={{2,0},{4,2},{6,4},{8,6},{10,8},{12,10},{14,12},{16,14},{18,16},{20... | collective-permute-start | bytes 73736 | tf_op jit(solution)/shard_map/ppermute | solution.py:22
  166.1 5.7 %collective-permute-done.13 = f32[24,1,256]{2,1,0:T(1,128)S(1)} collective-permute-done((f32[24,1,256]{2,1,0:T(1,128)S(1)}, f32[24,1,256]{2,1,0:T(1,128)S(1)}, u32[]{:S(2)}, u32[]{:S(2)}) %collective-permute-start.13) | collective-permute-done | bytes 24608 | tf_op jit(solution)/shard_map/ppermute | solution.py:22
  173.4 1.9 collective-permute-start.14
  175.3 4.1 %collective-permute-start.15 = (f32[24,1,256]{2,1,0:T(1,128)S(1)}, f32[24,1,256]{2,1,0:T(1,128)S(1)}, u32[]{:S(2)}, u32[]{:S(2)}) collective-permute-start(f32[24,1,256]{2,1,0:T(1,128)S(1)} %get-tuple-element.39), channel_id=1, source_target_pairs={{2,0},{4,2},{6,4},{8,6},{10,8},{12,10},{14,12},{16,14},{18,16},{20... | collective-permute-start | bytes 73736 | tf_op jit(solution)/shard_map/ppermute | solution.py:22
  179.5 5.7 %collective-permute-done.15 = f32[24,1,256]{2,1,0:T(1,128)S(1)} collective-permute-done((f32[24,1,256]{2,1,0:T(1,128)S(1)}, f32[24,1,256]{2,1,0:T(1,128)S(1)}, u32[]{:S(2)}, u32[]{:S(2)}) %collective-permute-start.15) | collective-permute-done | bytes 24608 | tf_op jit(solution)/shard_map/ppermute | solution.py:22
  186.3 1.3 fusion.30
  187.6 1.9 copy.35
  189.4 18.7 %fusion.3 = f32[5,32,96,128]{3,1,2,0:T(8,128)S(1)} fusion(f32[5,32,96,128]{3,2,1,0:T(8,128)} %param.18, f32[32,96,128]{2,0,1:T(8,128)S(1)} %fusion.12, f32[48,96,128]{2,0,1:T(8,128)S(1)} %bitcast.62, bf16[5,48,96,128]{3,2,1,0:T(8,128)(2,1)} %param.17, f32[48,32]{0,1:T(8,128)S(1)} %copy-done), kind=kOutput, calls=%fused_computation.6 | convolution fusion | flops 1144258560 | bytes 25565184 | tf_op jit(solution)/shard_map/lm,klrc->kmrc/dot_general | solution.py:139
  208.2 7.7 %copy.37 = f32[5,32,96,128]{3,2,1,0:T(8,128)} copy(f32[5,32,96,128]{3,1,2,0:T(8,128)S(1)} %fusion.3) | data formatting | bytes 15728640
  (127 shorter events, 10.0 us)
Async XLA Ops:
  7.2 8.4 %copy-start = (f32[48,32]{0,1:T(8,128)S(1)}, f32[48,32]{0,1:T(8,128)}, u32[]{:S(2)}) copy-start(f32[48,32]{0,1:T(8,128)} %param.19) | copy-start | bytes 18436
  7.2 96.5 %reduce-scatter.2.cloned.1.call-start = ((), (), s32[]{:S(2)}) async-start(), calls=%async_computation.1 | async-start | bytes 3342336 | tf_op jit(solution)/shard_map/reduce_scatter | solution.py:107
  8.7 42.6 %collective-permute-start.4 = (f32[2,3,256]{2,1,0:T(4,128)S(1)}, f32[2,3,256]{2,1,0:T(4,128)S(1)}, u32[]{:S(2)}, u32[]{:S(2)}) collective-permute-start(f32[2,3,256]{2,1,0:T(4,128)S(1)} %get-tuple-element.60), channel_id=1, source_target_pairs={{0,2},{2,4},{4,6},{6,8},{8,10},{10,12},{12,14},{14,16},{16,18},{18... | collective-permute-start | bytes 18440 | tf_op jit(solution)/shard_map/ppermute | solution.py:20
  12.1 39.2 %collective-permute-start.5 = (f32[2,3,256]{2,1,0:T(4,128)S(1)}, f32[2,3,256]{2,1,0:T(4,128)S(1)}, u32[]{:S(2)}, u32[]{:S(2)}) collective-permute-start(f32[2,3,256]{2,1,0:T(4,128)S(1)} %get-tuple-element.61), channel_id=1, source_target_pairs={{2,0},{4,2},{6,4},{8,6},{10,8},{12,10},{14,12},{16,14},{18,16},{20... | collective-permute-start | bytes 18440 | tf_op jit(solution)/shard_map/ppermute | solution.py:22
  37.8 2.5 %copy-start.1 = (f32[24,24,256]{2,1,0:T(8,128)S(1)}, f32[24,24,256]{2,1,0:T(8,128)}, u32[]{:S(2)}) copy-start(f32[24,24,256]{2,1,0:T(8,128)} %param.25) | copy-start | bytes 1769476
  37.8 12.3 %copy-start.13 = (s32[256]{0:T(256)S(1)}, s32[256]{0:T(256)}, u32[]{:S(2)}) copy-start(s32[256]{0:T(256)} %param.23) | copy-start | bytes 3076
  37.8 12.9 %copy-start.11 = (f32[256]{0:T(256)S(1)}, f32[256]{0:T(256)}, u32[]{:S(2)}) copy-start(f32[256]{0:T(256)} %param.24) | copy-start | bytes 3076
  37.8 13.5 %copy-start.10 = (f32[24,256]{1,0:T(8,128)S(1)}, f32[24,256]{1,0:T(8,128)}, u32[]{:S(2)}) copy-start(f32[24,256]{1,0:T(8,128)} %param.27) | copy-start | bytes 73732
  40.2 147.4 %all-gather.2.cloned.1.call-start = ((), (), s32[]{:S(2)}) async-start(), calls=%async_computation.2 | async-start | bytes 2506752 | tf_op jit(solution)/shard_map/all_gather | solution.py:136
  40.3 11.3 %collective-permute-start.2 = (f32[24,1,256]{2,1,0:T(1,128)S(1)}, f32[24,1,256]{2,1,0:T(1,128)S(1)}, u32[]{:S(2)}, u32[]{:S(2)}) collective-permute-start(f32[24,1,256]{2,1,0:T(1,128)S(1)} %get-tuple-element.48), channel_id=1, source_target_pairs={{0,2},{2,4},{4,6},{6,8},{8,10},{10,12},{12,14},{14,16},{16,18},{18... | collective-permute-start | bytes 73736 | tf_op jit(solution)/shard_map/ppermute | solution.py:20
  48.0 9.9 %collective-permute-start.3 = (f32[24,1,256]{2,1,0:T(1,128)S(1)}, f32[24,1,256]{2,1,0:T(1,128)S(1)}, u32[]{:S(2)}, u32[]{:S(2)}) collective-permute-start(f32[24,1,256]{2,1,0:T(1,128)S(1)} %get-tuple-element.49), channel_id=1, source_target_pairs={{2,0},{4,2},{6,4},{8,6},{10,8},{12,10},{14,12},{16,14},{18,16},{20... | collective-permute-start | bytes 73736 | tf_op jit(solution)/shard_map/ppermute | solution.py:22
  51.5 35.3 %copy-start.6 = (f32[25,256]{1,0:T(8,128)}, f32[25,256]{1,0:T(8,128)S(1)}, u32[]{:S(2)}) copy-start(f32[25,256]{1,0:T(8,128)S(1)} %fusion.60) | copy-start | bytes 76804
  51.7 20.2 %copy-start.4 = (f32[26,256]{1,0:T(8,128)}, f32[26,256]{1,0:T(8,128)S(1)}, u32[]{:S(2)}) copy-start(f32[26,256]{1,0:T(8,128)S(1)} %fusion.54) | copy-start | bytes 79876
  58.0 7.3 %copy-start.22 = (s32[24]{0:T(128)S(1)}, s32[24]{0:T(128)}, u32[]{:S(2)}) copy-start(s32[24]{0:T(128)} %param.21) | copy-start | bytes 292
  59.5 6.5 %collective-permute-start.6 = (f32[24,1,256]{2,1,0:T(1,128)S(1)}, f32[24,1,256]{2,1,0:T(1,128)S(1)}, u32[]{:S(2)}, u32[]{:S(2)}) collective-permute-start(f32[24,1,256]{2,1,0:T(1,128)S(1)} %get-tuple-element.44), channel_id=1, source_target_pairs={{0,2},{2,4},{4,6},{6,8},{8,10},{10,12},{12,14},{14,16},{16,18},{18... | collective-permute-start | bytes 73736 | tf_op jit(solution)/shard_map/ppermute | solution.py:20
  61.4 9.9 %collective-permute-start.7 = (f32[24,1,256]{2,1,0:T(1,128)S(1)}, f32[24,1,256]{2,1,0:T(1,128)S(1)}, u32[]{:S(2)}, u32[]{:S(2)}) collective-permute-start(f32[24,1,256]{2,1,0:T(1,128)S(1)} %get-tuple-element.45), channel_id=1, source_target_pairs={{2,0},{4,2},{6,4},{8,6},{10,8},{12,10},{14,12},{16,14},{18,16},{20... | collective-permute-start | bytes 73736 | tf_op jit(solution)/shard_map/ppermute | solution.py:22
  71.5 7.3 %copy-start.19 = (f32[24]{0:T(128)S(1)}, f32[24]{0:T(128)}, u32[]{:S(2)}) copy-start(f32[24]{0:T(128)} %param.22) | copy-start | bytes 292
  73.0 6.5 %collective-permute-start.8 = (f32[24,1,256]{2,1,0:T(1,128)S(1)}, f32[24,1,256]{2,1,0:T(1,128)S(1)}, u32[]{:S(2)}, u32[]{:S(2)}) collective-permute-start(f32[24,1,256]{2,1,0:T(1,128)S(1)} %get-tuple-element.42), channel_id=1, source_target_pairs={{0,2},{2,4},{4,6},{6,8},{8,10},{10,12},{12,14},{14,16},{16,18},{18... | collective-permute-start | bytes 73736 | tf_op jit(solution)/shard_map/ppermute | solution.py:20
  74.9 9.9 %collective-permute-start.9 = (f32[24,1,256]{2,1,0:T(1,128)S(1)}, f32[24,1,256]{2,1,0:T(1,128)S(1)}, u32[]{:S(2)}, u32[]{:S(2)}) collective-permute-start(f32[24,1,256]{2,1,0:T(1,128)S(1)} %get-tuple-element.43), channel_id=1, source_target_pairs={{2,0},{4,2},{6,4},{8,6},{10,8},{12,10},{14,12},{16,14},{18,16},{20... | collective-permute-start | bytes 73736 | tf_op jit(solution)/shard_map/ppermute | solution.py:22
  79.4 7.5 %copy-start.8 = (f32[24,1,256]{2,1,0:T(1,128)}, f32[24,1,256]{2,1,0:T(1,128)S(1)}, u32[]{:S(2)}) copy-start(f32[24,1,256]{2,1,0:T(1,128)S(1)} %collective-permute-done.8) | copy-start | bytes 73732
  84.8 2.1 copy-start.9
  103.7 22.7 %copy-start.2 = (f32[24,24,256]{2,1,0:T(8,128)S(1)}, f32[24,24,256]{2,1,0:T(8,128)}, u32[]{:S(2)}) copy-start(f32[24,24,256]{2,1,0:T(8,128)} %param.29) | copy-start | bytes 1769476
  103.7 22.7 %copy-start.12 = (f32[256]{0:T(256)S(1)}, f32[256]{0:T(256)}, u32[]{:S(2)}) copy-start(f32[256]{0:T(256)} %param.24) | copy-start | bytes 3076
  103.7 22.7 %copy-start.14 = (s32[256]{0:T(256)S(1)}, s32[256]{0:T(256)}, u32[]{:S(2)}) copy-start(s32[256]{0:T(256)} %param.23) | copy-start | bytes 3076
  103.7 22.7 %copy-start.15 = (s32[256]{0:T(256)S(1)}, s32[256]{0:T(256)}, u32[]{:S(2)}) copy-start(s32[256]{0:T(256)} %broadcast_add_fusion) | copy-start | bytes 3076
  103.7 22.7 %copy-start.16 = (f32[256]{0:T(256)S(1)}, f32[256]{0:T(256)}, u32[]{:S(2)}) copy-start(f32[256]{0:T(256)} %broadcast_subtract_fusion) | copy-start | bytes 3076
  103.7 23.5 %copy-start.17 = (s32[24]{0:T(128)S(1)}, s32[24]{0:T(128)}, u32[]{:S(2)}) copy-start(s32[24]{0:T(128)} %get-tuple-element.36) | copy-start | bytes 292
  103.7 23.5 %copy-start.18 = (s32[24]{0:T(128)S(1)}, s32[24]{0:T(128)}, u32[]{:S(2)}) copy-start(s32[24]{0:T(128)} %get-tuple-element.37) | copy-start | bytes 292
  103.7 23.5 %copy-start.20 = (f32[24]{0:T(128)S(1)}, f32[24]{0:T(128)}, u32[]{:S(2)}) copy-start(f32[24]{0:T(128)} %param.22) | copy-start | bytes 292
  103.8 23.5 %copy-start.21 = (f32[24]{0:T(128)S(1)}, f32[24]{0:T(128)}, u32[]{:S(2)}) copy-start(f32[24]{0:T(128)} %broadcast_subtract_fusion.1) | copy-start | bytes 292
  104.8 11.4 %collective-permute-start = (f32[24,1,128]{2,1,0:T(1,128)S(1)}, f32[24,1,128]{2,1,0:T(1,128)S(1)}, u32[]{:S(2)}, u32[]{:S(2)}) collective-permute-start(f32[24,1,128]{2,1,0:T(1,128)S(1)} %get-tuple-element.52), channel_id=1, source_target_pairs={{0,2},{2,4},{4,6},{6,8},{8,10},{10,12},{12,14},{14,16},{16,18},{18... | collective-permute-start | bytes 36872 | tf_op jit(solution)/shard_map/ppermute | solution.py:20
  112.5 9.8 %collective-permute-start.1 = (f32[24,1,128]{2,1,0:T(1,128)S(1)}, f32[24,1,128]{2,1,0:T(1,128)S(1)}, u32[]{:S(2)}, u32[]{:S(2)}) collective-permute-start(f32[24,1,128]{2,1,0:T(1,128)S(1)} %get-tuple-element.53), channel_id=1, source_target_pairs={{2,0},{4,2},{6,4},{8,6},{10,8},{12,10},{14,12},{16,14},{18,16},{20... | collective-permute-start | bytes 36872 | tf_op jit(solution)/shard_map/ppermute | solution.py:22
  126.3 0.9 copy-start.3
  126.3 32.4 %copy-start.5 = (f32[26,256]{1,0:T(8,128)S(1)}, f32[26,256]{1,0:T(8,128)}, u32[]{:S(2)}) copy-start(f32[26,256]{1,0:T(8,128)} %copy-done.4) | copy-start | bytes 79876
  126.4 32.9 %copy-start.7 = (f32[25,256]{1,0:T(8,128)S(1)}, f32[25,256]{1,0:T(8,128)}, u32[]{:S(2)}) copy-start(f32[25,256]{1,0:T(8,128)} %copy-done.6) | copy-start | bytes 76804
  127.6 10.1 %collective-permute-start.16 = (f32[24,1,128]{2,1,0:T(1,128)S(1)}, f32[24,1,128]{2,1,0:T(1,128)S(1)}, u32[]{:S(2)}, u32[]{:S(2)}) collective-permute-start(f32[24,1,128]{2,1,0:T(1,128)S(1)} %get-tuple-element.51), channel_id=1, source_target_pairs={{2,0},{4,2},{6,4},{8,6},{10,8},{12,10},{14,12},{16,14},{18,16},{20... | collective-permute-start | bytes 36872 | tf_op jit(solution)/shard_map/ppermute | solution.py:32
  129.6 9.5 %collective-permute-start.17 = (f32[24,1,128]{2,1,0:T(1,128)S(1)}, f32[24,1,128]{2,1,0:T(1,128)S(1)}, u32[]{:S(2)}, u32[]{:S(2)}) collective-permute-start(f32[24,1,128]{2,1,0:T(1,128)S(1)} %get-tuple-element.50), channel_id=1, source_target_pairs={{0,2},{2,4},{4,6},{6,8},{8,10},{10,12},{12,14},{14,16},{16,18},{18... | collective-permute-start | bytes 36872 | tf_op jit(solution)/shard_map/ppermute | solution.py:32
  140.0 10.4 %collective-permute-start.10 = (f32[24,1,256]{2,1,0:T(1,128)S(1)}, f32[24,1,256]{2,1,0:T(1,128)S(1)}, u32[]{:S(2)}, u32[]{:S(2)}) collective-permute-start(f32[24,1,256]{2,1,0:T(1,128)S(1)} %get-tuple-element.46), channel_id=1, source_target_pairs={{0,2},{2,4},{4,6},{6,8},{8,10},{10,12},{12,14},{14,16},{16,18},{18... | collective-permute-start | bytes 73736 | tf_op jit(solution)/shard_map/ppermute | solution.py:20
  148.4 9.9 %collective-permute-start.11 = (f32[24,1,256]{2,1,0:T(1,128)S(1)}, f32[24,1,256]{2,1,0:T(1,128)S(1)}, u32[]{:S(2)}, u32[]{:S(2)}) collective-permute-start(f32[24,1,256]{2,1,0:T(1,128)S(1)} %get-tuple-element.47), channel_id=1, source_target_pairs={{2,0},{4,2},{6,4},{8,6},{10,8},{12,10},{14,12},{16,14},{18,16},{20... | collective-permute-start | bytes 73736 | tf_op jit(solution)/shard_map/ppermute | solution.py:22
  159.9 6.2 %collective-permute-start.12 = (f32[24,1,256]{2,1,0:T(1,128)S(1)}, f32[24,1,256]{2,1,0:T(1,128)S(1)}, u32[]{:S(2)}, u32[]{:S(2)}) collective-permute-start(f32[24,1,256]{2,1,0:T(1,128)S(1)} %get-tuple-element.40), channel_id=1, source_target_pairs={{0,2},{2,4},{4,6},{6,8},{8,10},{10,12},{12,14},{14,16},{16,18},{18... | collective-permute-start | bytes 73736 | tf_op jit(solution)/shard_map/ppermute | solution.py:20
  161.9 9.9 %collective-permute-start.13 = (f32[24,1,256]{2,1,0:T(1,128)S(1)}, f32[24,1,256]{2,1,0:T(1,128)S(1)}, u32[]{:S(2)}, u32[]{:S(2)}) collective-permute-start(f32[24,1,256]{2,1,0:T(1,128)S(1)} %get-tuple-element.41), channel_id=1, source_target_pairs={{2,0},{4,2},{6,4},{8,6},{10,8},{12,10},{14,12},{16,14},{18,16},{20... | collective-permute-start | bytes 73736 | tf_op jit(solution)/shard_map/ppermute | solution.py:22
  173.4 6.2 %collective-permute-start.14 = (f32[24,1,256]{2,1,0:T(1,128)S(1)}, f32[24,1,256]{2,1,0:T(1,128)S(1)}, u32[]{:S(2)}, u32[]{:S(2)}) collective-permute-start(f32[24,1,256]{2,1,0:T(1,128)S(1)} %get-tuple-element.38), channel_id=1, source_target_pairs={{0,2},{2,4},{4,6},{6,8},{8,10},{10,12},{12,14},{14,16},{16,18},{18... | collective-permute-start | bytes 73736 | tf_op jit(solution)/shard_map/ppermute | solution.py:20
  175.3 9.9 %collective-permute-start.15 = (f32[24,1,256]{2,1,0:T(1,128)S(1)}, f32[24,1,256]{2,1,0:T(1,128)S(1)}, u32[]{:S(2)}, u32[]{:S(2)}) collective-permute-start(f32[24,1,256]{2,1,0:T(1,128)S(1)} %get-tuple-element.39), channel_id=1, source_target_pairs={{2,0},{4,2},{6,4},{8,6},{10,8},{12,10},{14,12},{16,14},{18,16},{20... | collective-permute-start | bytes 73736 | tf_op jit(solution)/shard_map/ppermute | solution.py:22
Sparse Core Ops, SparseCore 0:
  40.3 63.3 reduce-scatter.1
  140.1 34.5 all-gather.1
where the time goes:
time: 224 us; the launch traced here: 223 us
  starting transfers between devices  69.3 us (31%)
  waiting for transfers between devices  59.9 us (27%)
  matrix products  45.8 us (20%)
  local copies, waits for them, and re-layouts  19 us (8%)
  between operations  15 us (7%)
  other arithmetic  13.8 us (6%)
    ppermute x8, waiting for transfers between devices, padded(): lax.ppermute(head, axis, [((i + 1) % count, i) for i in range(ends)])  42.5 us
    ppermute x8, starting transfers between devices, padded(): lax.ppermute(tail, axis, [(i, (i + 1) % count) for i in range(ends)])  34.9 us
    ppermute x8, starting transfers between devices, padded(): lax.ppermute(head, axis, [((i + 1) % count, i) for i in range(ends)])  24.3 us
    dot_general x1, matrix products, local(): jnp.einsum('lm,kmrc->klrc', eigen_modes, ens_control * mode_keep[None], p...  22 us
    dot_general x1, matrix products, local(): jnp.einsum('lm,klrc->kmrc', eigen_modes, ens_pert.astype(jnp.float32) * c...  18.7 us
    reduce_scatter x1, waiting for transfers between devices, local(): lax.psum_scatter(blocks, ('fine', 'lev'), scatter_dimension=0, tiled=True)  15.8 us
    ppermute x2, starting transfers between devices, from_behind(): return lax.ppermute(block, axis, route)  10.1 us
    unnamed x47, local copies, waits for them, and re-layouts  7.79 us
  transfers between devices with their start and end apart: 20, of which 10 were waited for; matrix products, arithmetic and copies ran while one was open for 19% of the time, Pallas kernels for 0%

commit v1 on v0

v1 whole, which is shorter than its diff:
```python
import functools
import math

import jax
import jax.numpy as jnp
from jax import lax
from jax.experimental import pallas as pl
from jax.experimental.pallas import tpu as pltpu
from jax.sharding import PartitionSpec as P

MEMBERS = 80
NSWEEP = 3
HALO = 3
EDGE = 4
GROWN = 32
ROWS = 12
XROWS = 7
YROWS = ROWS - XROWS
YA = YROWS // 2
BLOCK = 16
F32 = jnp.float32
BF16 = jnp.bfloat16


def halves(value):
    hi = value.astype(BF16)
    return hi, (value - hi.astype(F32)).astype(BF16)


def stacked(value):
    hi, lo = halves(value)
    return jnp.concatenate([hi, hi, lo], axis=0)


def split_modes(matrix):
    hi = lax.reduce_precision(matrix, 8, 7)
    return jnp.concatenate([hi, matrix - hi, hi], axis=1).astype(BF16)


def forward_kernel(lhs_ref, count_ref, amp_ref, pert_ref, out_ref, wide_ref):
    members, modes = amp_ref.shape[:2]
    levels = pert_ref.shape[1]
    wide_ref[...] = pert_ref[...].reshape(wide_ref.shape).astype(F32)
    amps = amp_ref.reshape(members * modes * BLOCK, 128)
    lhs = lhs_ref[...]
    mode = lax.broadcasted_iota(jnp.int32, (modes, 128), 0)

    def row_pair(step, carry):
        first = step * 2
        keep = [mode < count_ref[pl.ds(first + h, 1), :] for h in range(2)]
        total = [jnp.zeros((levels, 128), F32) for _ in range(2)]
        for k in range(members):
            rhs = []
            for h in range(2):
                amp = amps[pl.ds(k * modes * BLOCK + first + h, modes, stride=BLOCK), :]
                rhs.append(stacked(jnp.where(keep[h], amp, 0.0)))
            level_amp = jnp.dot(lhs, jnp.concatenate(rhs, axis=1), preferred_element_type=F32)
            for h in range(2):
                pert = wide_ref[pl.ds(k * levels * BLOCK + first + h, levels, stride=BLOCK), :]
                total[h] = total[h] + pert * level_amp[:, h * 128 : (h + 1) * 128]
        for h in range(2):
            out_ref[0, first + h] = total[h][: levels // 2]
            out_ref[1, first + h] = total[h][levels // 2 :]
        return carry

    lax.fori_loop(0, BLOCK // 2, row_pair, 0, unroll=4)


def backward_kernel(lhs_ref, count_ref, amp_ref, pert_ref, grad_ref, out_ref, wide_ref):
    members, modes = amp_ref.shape[:2]
    levels = pert_ref.shape[1]
    wide_ref[...] = pert_ref[...].reshape(wide_ref.shape).astype(F32)
    amps = amp_ref.reshape(members * modes * BLOCK, 128)
    outs = out_ref.reshape(members * modes * BLOCK, 128)
    lhs = lhs_ref[...]
    mode = lax.broadcasted_iota(jnp.int32, (modes, 128), 0)

    def row_pair(step, carry):
        first = step * 2
        keep = [mode < count_ref[pl.ds(first + h, 1), :] for h in range(2)]
        grad = [
            jnp.concatenate([grad_ref[0, first + h], grad_ref[1, first + h]], axis=0)
            for h in range(2)
        ]
        for k in range(members):
            rhs = []
            for h in range(2):
                pert = wide_ref[pl.ds(k * levels * BLOCK + first + h, levels, stride=BLOCK), :]
                rhs.append(stacked(pert * grad[h]))
            proj = jnp.dot(lhs, jnp.concatenate(rhs, axis=1), preferred_element_type=F32)
            for h in range(2):
                at = pl.ds(k * modes * BLOCK + first + h, modes, stride=BLOCK)
                outs[at, :] = amps[at, :] + jnp.where(
                    keep[h], proj[:, h * 128 : (h + 1) * 128], 0.0
                )
        return carry

    lax.fori_loop(0, BLOCK // 2, row_pair, 0, unroll=4)


def forward(lhs, count, amp, pert):
    members, modes, rows, cols = amp.shape
    levels = pert.shape[1]
    return pl.pallas_call(
        forward_kernel,
        grid=(rows // BLOCK,),
        in_specs=[
            pl.BlockSpec(lhs.shape, lambda i: (0, 0)),
            pl.BlockSpec((BLOCK, cols), lambda i: (i, 0)),
            pl.BlockSpec((members, modes, BLOCK, cols), lambda i: (0, 0, i, 0)),
            pl.BlockSpec((members, levels, BLOCK, cols), lambda i: (0, 0, i, 0)),
        ],
        out_specs=pl.BlockSpec((2, BLOCK, levels // 2, cols), lambda i: (0, i, 0, 0)),
        out_shape=jax.ShapeDtypeStruct((2, rows, levels // 2, cols), F32),
        scratch_shapes=[pltpu.VMEM((members * levels * BLOCK, cols), F32)],
        compiler_params=pltpu.CompilerParams(vmem_limit_bytes=50 << 20),
        name="forward_modes",
    )(lhs, count, amp, pert)


def backward(lhs, count, amp, pert, grad):
    members, modes, rows, cols = amp.shape
    levels = pert.shape[1]
    return pl.pallas_call(
        backward_kernel,
        grid=(rows // BLOCK,),
        in_specs=[
            pl.BlockSpec(lhs.shape, lambda i: (0, 0)),
            pl.BlockSpec((BLOCK, cols), lambda i: (i, 0)),
            pl.BlockSpec((members, modes, BLOCK, cols), lambda i: (0, 0, i, 0)),
            pl.BlockSpec((members, levels, BLOCK, cols), lambda i: (0, 0, i, 0)),
            pl.BlockSpec((2, BLOCK, levels // 2, cols), lambda i: (0, i, 0, 0)),
        ],
        out_specs=pl.BlockSpec((members, modes, BLOCK, cols), lambda i: (0, 0, i, 0)),
        out_shape=jax.ShapeDtypeStruct(amp.shape, F32),
        scratch_shapes=[pltpu.VMEM((members * levels * BLOCK, cols), F32)],
        compiler_params=pltpu.CompilerParams(vmem_limit_bytes=50 << 20),
        name="backward_modes",
    )(lhs, count, amp, pert, grad)


def exchange_kernel(
    sizes,
    tile_ref,
    control_ref,
    innov_ref,
    std_ref,
    spread_ref,
    land_ref,
    row_index_ref,
    row_weight_ref,
    col_index_ref,
    col_weight_ref,
    inc_ref,
    grad_ref,
    coarse_ref,
    sums,
    core_in,
    x1_in,
    x2_in,
    x3_in,
    x4_in,
    yq_in,
    y1_in,
    y2_in,
    y3_in,
    window,
    field_a,
    field_b,
    misfit,
    cells,
    row_faces,
    col_faces,
    weights,
    sigma,
    col_mat,
    back,
    shares,
    planes_in,
    planes_out,
    send_sem,
    recv_sem,
    copy_sem,
    plane_sem,
):
    coarse_count, fine_count, rows_all = sizes
    xs = fine_count // 2
    coarse = lax.axis_index("coarse")
    fine = lax.axis_index("fine")
    lev = lax.axis_index("lev")
    x = lax.rem(fine, xs)
    y = fine // xs
    right, left, across = lax.rem(x + 1, xs), lax.rem(x + xs - 1, xs), lax.rem(x + 2, xs)
    other_y = 1 - y
    serial = coarse * fine_count + fine
    count = coarse_count * fine_count
    after, before = lax.rem(serial + 1, count), lax.rem(serial + count - 1, count)
    first_row = serial * 2 * ROWS

    to_core = (coarse, fine, 1 - lev)
    to_right = (coarse, y * xs + right, lev)
    to_left = (coarse, y * xs + left, lev)
    to_y = (coarse, other_y * xs + x, lev)
    to_after = (after // fine_count, lax.rem(after, fine_count), lev)
    to_before = (before // fine_count, lax.rem(before, fine_count), lev)

    barrier = pltpu.get_barrier_semaphore()
    for device in (to_core, to_right, to_left, to_y, to_after, to_before):
        pl.semaphore_signal(barrier, inc=1, device_id=device, device_id_type=pl.DeviceIdType.MESH)

    numbers = iter(range(100))
    sent = []

    def remote(src, dst, device):
        number = next(numbers)
        copy = pltpu.make_async_remote_copy(
            src_ref=src,
            dst_ref=dst,
            send_sem=send_sem.at[number],
            recv_sem=recv_sem.at[number],
            device_id=device,
            device_id_type=pl.DeviceIdType.MESH,
        )
        copy.start()
        sent.append(copy)
        return copy

    def share(ry, rx):
        return (ry * xs + rx) * ROWS

    lev_dev = control_ref.shape[0]
    own = 2 * ROWS
    lanes = [pl.ds(0, 128), pl.ds(128, 128)]
    plane_in = [
        [
            pltpu.make_async_copy(
                ref.at[:, :, lanes[side]],
                planes_in.at[number, side],
                plane_sem.at[2 * number + side],
            )
            for side in range(2)
        ]
        for number, ref in enumerate((control_ref, innov_ref))
    ]
    for pair in plane_in:
        for copy in pair:
            copy.start()

    def planes(ref, number, side):
        return ref.at[number, side].reshape(lev_dev * own, 128)

    for copy in plane_in[0]:
        copy.wait()

    def load_rows(i, carry):
        for side in range(2):
            field_a[EDGE + i, :, lanes[side]] = planes(planes_in, 0, side)[
                pl.ds(i, lev_dev, stride=own), :
            ]
        sub = lax.broadcasted_iota(jnp.int32, (8, 256), 0)
        weight = jnp.full((8, 256), row_weight_ref[i], F32)
        index = jnp.full((8, 256), row_index_ref[i], jnp.int32)
        upper = (index == (first_row + i) // 2).astype(F32)
        spread = jnp.broadcast_to(spread_ref[pl.ds(i, 1), :], (8, 256))
        land = jnp.broadcast_to(land_ref[pl.ds(i, 1), :], (8, 256)).astype(F32)
        cells[EDGE + i] = jnp.where(
            sub == 0, spread, jnp.where(sub == 1, land, jnp.where(sub == 2, weight, upper))
        )
        return carry

    lax.fori_loop(0, own, load_rows, 0, unroll=4)
    for ref in (cells, misfit):
        ref[0] = jnp.zeros(ref.shape[1:], F32)
        ref[GROWN - 1] = jnp.zeros(ref.shape[1:], F32)
    for row in (1, GROWN - 2):
        field_b[row] = jnp.zeros(field_b.shape[1:], F32)
    for lev_at in range(lev_dev):
        sigma[lev_at : lev_at + 1, :] = jnp.full((1, 256), std_ref[lev_at], F32)

    pl.semaphore_wait(barrier, 6)

    orders = [across, right, left, x]
    keep_own = pltpu.make_async_copy(tile_ref.at[lev], sums, copy_sem)
    keep_own.start()
    core_sends = []
    for rx in orders:
        for ry in (0, 1):
            rows = pl.ds(share(ry, rx), ROWS)
            core_sends.append(
                remote(tile_ref.at[1 - lev, rows], core_in.at[rows], to_core)
            )
    top, bottom = pl.ds(EDGE, HALO), pl.ds(EDGE + own - HALO, HALO)
    low, high = pl.ds(EDGE - HALO, HALO), pl.ds(EDGE + own, HALO)
    halo_sends = [
        remote(ref.at[src], ref.at[dst], device)
        for ref in (cells, field_a)
        for src, dst, device in ((top, high, to_before), (bottom, low, to_after))
    ]
    keep_own.wait()

    def x_rows(ry, rx):
        return pl.ds(share(ry, rx), XROWS)

    def y_rows(rx, part, ry=None):
        start = share(y if ry is None else ry, rx) + XROWS
        return {
            "all": pl.ds(start, YROWS),
            "a": pl.ds(start, YA),
            "b": pl.ds(start + YA, YROWS - YA),
        }[part]

    def add(rows, *terms):
        total = sums[rows]
        for term in terms:
            total = total + term[...]
        sums[rows] = total

    quarter = {}
    for number, rx in enumerate(orders):
        for ry in (0, 1):
            core_sends[2 * number + ry].wait_recv()
            rows = pl.ds(share(ry, rx), ROWS)
            add(rows, core_in.at[rows])
        quarter[number] = remote(sums.at[y_rows(rx, "all", other_y)], yq_in.at[number], to_y)
        if number == 0:
            x1 = [
                remote(sums.at[x_rows(0, across)], x1_in.at[0], to_right),
                remote(sums.at[x_rows(1, across)], x1_in.at[1], to_left),
            ]
        if number == 1:
            x2_right = remote(sums.at[x_rows(1, right)], x2_in.at[0], to_right)
        if number == 2:
            x2_left = remote(sums.at[x_rows(0, left)], x2_in.at[1], to_left)

    for copy in halo_sends[:2]:
        copy.wait_recv()

    def coefficients(e, carry):
        here, there = cells[e], cells[e + 1]
        line = first_row - EDGE + e
        inside = (line >= 0) & (line < rows_all) & (e >= 1) & (e <= GROWN - 2)
        facing = (line >= 0) & (line + 1 < rows_all)
        inside = jnp.where(inside, 1.0, 0.0).astype(F32)
        facing = jnp.where(facing, 1.0, 0.0).astype(F32)
        lane = lax.broadcasted_iota(jnp.int32, (8, 256), 1)
        spread, land = (jnp.broadcast_to(here[j : j + 1], (8, 256)) for j in (0, 1))
        spread_next, land_next = (jnp.broadcast_to(there[j : j + 1], (8, 256)) for j in (0, 1))
        row_faces[e] = (
            jnp.sqrt(spread * spread_next) * (1.0 - 0.5 * jnp.abs(land - land_next)) * facing
        )
        spread_right, land_right = (pltpu.roll(v, 255, 1) for v in (spread, land))
        col_faces[e] = jnp.where(
            lane < 255,
            jnp.sqrt(spread * spread_right) * (1.0 - 0.5 * jnp.abs(land - land_right)),
            0.0,
        )
        weight, upper = (jnp.broadcast_to(here[j : j + 1, :128], (8, 128)) for j in (2, 3))
        upper_on = upper > 0.5
        weights[0, e] = jnp.where(upper_on, 0.0, 1.0 - weight) * inside
        weights[1, e] = jnp.where(upper_on, 1.0 - weight, weight) * inside
        weights[2, e] = jnp.where(upper_on, weight, 0.0) * inside
        return carry

    lax.fori_loop(0, GROWN - 1, coefficients, 0, unroll=4)
    for j in range(3):
        weights[j, GROWN - 1] = jnp.zeros((8, 128), F32)
    col = lax.broadcasted_iota(jnp.int32, (128, 256), 0)
    col_at, col_w = col_index_ref[...], col_weight_ref[...]
    matrix = jnp.where(col == col_at, 1.0 - col_w, jnp.where(col == col_at + 1, col_w, 0.0))
    hi, lo = halves(matrix)
    col_mat[0], col_mat[1] = hi, lo

    for rx_copy, rows, slot, device, x3_slot in (
        (x1[0], x_rows(0, right), 0, to_right, 0),
        (x1[1], x_rows(1, left), 1, to_left, 1),
    ):
        rx_copy.wait_recv()
        add(rows, x1_in.at[slot])
        if slot == 0:
            x3_right = remote(sums.at[rows], x3_in.at[0], device)
        else:
            x3_left = remote(sums.at[rows], x3_in.at[1], device)

    for number, rx in enumerate(orders):
        quarter[number].wait_recv()
        add(y_rows(rx, "all"), yq_in.at[number])
        if number == 0:
            y1 = [
                remote(sums.at[y_rows(rx, "a")], y1_in.at[0, pl.ds(0, YA)], to_right),
                remote(sums.at[y_rows(rx, "b")], y1_in.at[1], to_left),
            ]
        if number == 1:
            y2_right = remote(sums.at[y_rows(rx, "b")], y2_in.at[0], to_right)
        if number == 2:
            y2_left = remote(sums.at[y_rows(rx, "a")], y2_in.at[1, pl.ds(0, YA)], to_left)

    def sweep(src, dst):
        def rows_of_four(step, carry):
            e = EDGE - 2 + 4 * step
            down = row_faces[pl.ds(e - 1, 5)]
            side = col_faces[pl.ds(e, 4)]
            for tile in range(lev_dev // 8):
                at = pl.ds(8 * tile, 8)
                v = src[pl.ds(e - 1, 6), at, :]
                mid = v[1:5]
                flux = down * (v[1:] - v[:-1])
                cross = side * (pltpu.roll(mid, 255, 2) - mid)
                dst[pl.ds(e, 4), at, :] = (
                    mid + (flux[1:] - flux[:-1]) + (cross - pltpu.roll(cross, 1, 2))
                )
            return carry

        lax.fori_loop(0, 7, rows_of_four, 0)

    for copy in halo_sends[2:]:
        copy.wait_recv()
        copy.wait_send()
    sweep(field_a, field_b)

    for copy, slot in ((y1[0], 0), (y1[1], 1)):
        copy.wait_recv()
    a_rows, b_rows = y_rows(right, "a"), y_rows(left, "b")
    add(a_rows, y1_in.at[0, pl.ds(0, YA)])
    y3_right = remote(sums.at[a_rows], y3_in.at[0, pl.ds(0, YA)], to_right)
    add(b_rows, y1_in.at[1])
    y3_left = remote(sums.at[b_rows], y3_in.at[1], to_left)

    sweep(field_b, field_a)
    sweep(field_a, field_b)

    def static_part(i, carry):
        for side in range(2):
            cols = lanes[side]
            misfit[EDGE + i, :, cols] = (
                sigma[:, cols] * field_b[EDGE + i, :, cols]
                - planes(planes_in, 1, side)[pl.ds(i, lev_dev, stride=own), :]
            )
        return carry

    for copy in plane_in[1]:
        copy.wait()

    lax.fori_loop(0, own, static_part, 0, unroll=4)
    misfit_sends = [
        remote(misfit.at[top], misfit.at[high], to_before),
        remote(misfit.at[bottom], misfit.at[low], to_after),
    ]

    for copy in (x2_right, x2_left, x3_right, x3_left):
        copy.wait_recv()
    rows = x_rows(other_y, x)
    add(rows, x3_in.at[other_y], x2_in.at[y])
    x4 = remote(sums.at[rows], x4_in, to_y)
    add(x_rows(y, x), x3_in.at[y], x2_in.at[other_y])
    for copy in (y2_right, y2_left, y3_right, y3_left):
        copy.wait_recv()
    mine = share(y, x)
    window[pl.ds(HALO + XROWS, YA)] = (
        sums[y_rows(x, "a")] + y3_in[0, :YA] + y2_in[1, :YA]
    )
    window[pl.ds(HALO + XROWS + YA, YROWS - YA)] = sums[y_rows(x, "b")] + y3_in[1] + y2_in[0]
    window_after = remote(
        window.at[pl.ds(ROWS, HALO)], window.at[pl.ds(0, HALO)], to_after
    )
    x4.wait_recv()
    window[pl.ds(HALO, XROWS)] = sums[pl.ds(mine, XROWS)] + x4_in[...]
    window_before = remote(
        window.at[pl.ds(HALO, HALO)], window.at[pl.ds(HALO + ROWS, HALO)], to_before
    )
    for copy in misfit_sends + [window_after, window_before]:
        copy.wait_recv()
    for copy in misfit_sends:
        copy.wait_send()

    def dot_split(lhs, which):
        hi, lo = halves(lhs)
        c_hi, c_lo = col_mat[0], col_mat[1]
        dims = (((1,), (which,)), ((), ()))
        dot = functools.partial(lax.dot_general, dimension_numbers=dims, preferred_element_type=F32)
        return dot(hi, c_hi) + (dot(lo, c_hi) + dot(hi, c_lo))

    span = 8

    def interpolate(step, carry):
        e0 = step * span
        lines = []
        for pair in range(span // 2):
            t = step * (span // 2) + pair + 1
            w = [window[t + d].reshape(lev_dev // 8, 8, 128) for d in (-1, 0, 1)]
            for h in range(2):
                e = e0 + 2 * pair + h
                line = weights[0, e] * w[0] + weights[1, e] * w[1] + weights[2, e] * w[2]
                lines.append(line.reshape(lev_dev, 128))
        fine_part = dot_split(jnp.concatenate(lines, axis=0), 0)
        at = pl.ds(e0, span)
        total = misfit[at] + fine_part.reshape(span, lev_dev, 256)
        misfit[at] = total
        back[at] = dot_split(total.reshape(span * lev_dev, 256), 1).reshape(span, lev_dev, 128)
        return carry

    lax.fori_loop(0, GROWN // span, interpolate, 0)

    def adjoint(r, carry):
        e = 2 * r + 2
        total = jnp.zeros((lev_dev // 8, 8, 128), F32)
        for j in range(6):
            total = total + weights[2 - j // 2, e + j] * back[e + j].reshape(lev_dev // 8, 8, 128)
        shares[lev, mine + r] = total.reshape(lev_dev, 128)
        return carry

    lax.fori_loop(0, ROWS, adjoint, 0, unroll=4)

    def to_all(rows, device):
        return remote(shares.at[lev, rows], shares.at[lev, rows], device)

    def x_part(ry, rx):
        return pl.ds(share(ry, rx), XROWS)

    pair_first = to_all(x_part(y, x), to_y)
    ring_y = [to_all(y_rows(x, "all"), to_right), to_all(y_rows(x, "all"), to_left)]
    ring_own = [to_all(x_part(y, x), to_right), to_all(x_part(y, x), to_left)]
    core = [to_all(pl.ds(mine, ROWS), to_core)]
    pair_y = [to_all(y_rows(x, "all"), to_y)]

    def scaled(e, carry):
        at = pl.ds(e * 2 + 1, 2)
        field_a[at] = sigma[...] * misfit[at]
        return carry

    lax.fori_loop(0, (GROWN - 2) // 2, scaled, 0)

    pair_first.wait_recv()
    ring_other = [to_all(x_part(other_y, x), to_right), to_all(x_part(other_y, x), to_left)]
    core.append(to_all(x_part(other_y, x), to_core))
    for copy in ring_y:
        copy.wait_recv()
    on_y = [
        to_all(y_rows(left, "a"), to_right),
        to_all(y_rows(right, "b"), to_left),
    ]
    for rx in (left, right):
        pair_y.append(to_all(y_rows(rx, "all"), to_y))
        core.append(to_all(y_rows(rx, "all"), to_core))

    sweep(field_a, field_b)

    for copy in ring_own + ring_other:
        copy.wait_recv()
    on_x = [to_all(x_part(0, left), to_right), to_all(x_part(1, right), to_left)]
    for rx in (left, right):
        for ry in (0, 1):
            core.append(to_all(x_part(ry, rx), to_core))
    for copy in on_y:
        copy.wait_recv()
    pair_y.append(to_all(y_rows(across, "all"), to_y))
    core.append(to_all(y_rows(across, "all"), to_core))

    sweep(field_b, field_a)
    sweep(field_a, field_b)

    def finish(i, carry):
        at = pl.ds(i, lev_dev, stride=own)
        for side in range(2):
            for number, value in ((0, field_b), (1, misfit)):
                planes(planes_out, number, side)[at, :] = (
                    planes(planes_in, number, side)[at, :] + value[EDGE + i, :, lanes[side]]
                )
        return carry

    lax.fori_loop(0, own, finish, 0, unroll=4)
    plane_out = [
        pltpu.make_async_copy(
            planes_out.at[number, side],
            ref.at[:, :, lanes[side]],
            plane_sem.at[2 * number + side],
        )
        for number, ref in enumerate((grad_ref, inc_ref))
        for side in range(2)
    ]
    for copy in plane_out:
        copy.start()

    for copy in on_x:
        copy.wait_recv()
    for ry in (0, 1):
        core.append(to_all(x_part(ry, across), to_core))
    for rx, copy in zip((x, left, right, across), pair_y):
        copy.wait_recv()
        core.append(to_all(y_rows(rx, "all", other_y), to_core))
    for copy in core:
        copy.wait_recv()
    out = pltpu.make_async_copy(shares, coarse_ref, copy_sem)
    out.start()
    waited = halo_sends[2:] + misfit_sends
    for copy in sent:
        if not any(copy is done for done in waited):
            copy.wait_send()
    out.wait()
    for copy in plane_out:
        copy.wait()


def exchange(sizes, tile, control, innov, std, spread, land, row_index, row_weight, col_index, col_weight):
    lev_dev, own, cols_fine = control.shape
    vmem = pl.BlockSpec(memory_space=pltpu.VMEM)
    smem = pl.BlockSpec(memory_space=pltpu.SMEM)
    anywhere = pl.BlockSpec(memory_space=pl.ANY)
    cell = (lev_dev, 128)
    row = (lev_dev, cols_fine)
    return pl.pallas_call(
        functools.partial(exchange_kernel, sizes),
        in_specs=[anywhere, anywhere, anywhere, smem, vmem, vmem, smem, smem, vmem, vmem],
        out_specs=[anywhere, anywhere, anywhere],
        out_shape=[
            jax.ShapeDtypeStruct(control.shape, F32),
            jax.ShapeDtypeStruct(control.shape, F32),
            jax.ShapeDtypeStruct(tile.shape, F32),
        ],
        scratch_shapes=[
            pltpu.VMEM(tile.shape[1:], F32),
            pltpu.VMEM(tile.shape[1:], F32),
            pltpu.VMEM((2, XROWS) + cell, F32),
            pltpu.VMEM((2, XROWS) + cell, F32),
            pltpu.VMEM((2, XROWS) + cell, F32),
            pltpu.VMEM((XROWS,) + cell, F32),
            pltpu.VMEM((4, YROWS) + cell, F32),
            pltpu.VMEM((2, YROWS - YA) + cell, F32),
            pltpu.VMEM((2, YROWS - YA) + cell, F32),
            pltpu.VMEM((2, YROWS - YA) + cell, F32),
            pltpu.VMEM((ROWS + 2 * HALO,) + cell, F32),
            pltpu.VMEM((GROWN,) + row, F32),
            pltpu.VMEM((GROWN,) + row, F32),
            pltpu.VMEM((GROWN,) + row, F32),
            pltpu.VMEM((GROWN, 8, cols_fine), F32),
            pltpu.VMEM((GROWN, 8, cols_fine), F32),
            pltpu.VMEM((GROWN, 8, cols_fine), F32),
            pltpu.VMEM((3, GROWN, 8, 128), F32),
            pltpu.VMEM(row, F32),
            pltpu.VMEM((2, 128, cols_fine), BF16),
            pltpu.VMEM((GROWN,) + cell, F32),
            pltpu.VMEM(tile.shape, F32),
            pltpu.VMEM((2, 2, lev_dev, own, 128), F32),
            pltpu.VMEM((2, 2, lev_dev, own, 128), F32),
            pltpu.SemaphoreType.DMA((80,)),
            pltpu.SemaphoreType.DMA((80,)),
            pltpu.SemaphoreType.DMA,
            pltpu.SemaphoreType.DMA((4,)),
        ],
        compiler_params=pltpu.CompilerParams(
            collective_id=0, has_side_effects=True, vmem_limit_bytes=50 << 20
        ),
        name="exchange",
    )(
        tile,
        control,
        innov,
        std,
        spread,
        land,
        row_index,
        row_weight,
        col_index.reshape(1, cols_fine),
        col_weight.reshape(1, cols_fine),
    )


def local(
    ens_pert,
    ens_control,
    eigen_modes,
    mode_count,
    row_index,
    row_weight,
    col_index,
    col_weight,
    static_control,
    static_std,
    diffusivity,
    land_mask,
    innovation,
):
    sizes = (
        lax.axis_size("coarse"),
        lax.axis_size("fine"),
        lax.axis_size("coarse") * lax.axis_size("fine") * row_index.shape[0],
    )
    scaled = eigen_modes * (1.0 / math.sqrt(MEMBERS - 1))
    tile = forward(split_modes(scaled), mode_count, ens_control, ens_pert)
    increment, grad_static, coarse_grad = exchange(
        sizes,
        tile,
        static_control,
        innovation,
        static_std,
        diffusivity,
        land_mask,
        row_index,
        row_weight,
        col_index,
        col_weight,
    )
    grad_ens = backward(split_modes(scaled.T), mode_count, ens_control, ens_pert, coarse_grad)
    return increment, grad_static, grad_ens


def solution(mesh):
    in_specs = (
        P(("fine", "lev"), None, "coarse", None),
        P(("fine", "lev"), None, "coarse", None),
        P(),
        P("coarse", None),
        P(("coarse", "fine")),
        P(("coarse", "fine")),
        P(),
        P(),
        P("lev", ("coarse", "fine"), None),
        P("lev"),
        P(("coarse", "fine"), None),
        P(("coarse", "fine"), None),
        P("lev", ("coarse", "fine"), None),
    )
    out_specs = (
        P("lev", ("coarse", "fine"), None),
        P("lev", ("coarse", "fine"), None),
        P(("fine", "lev"), None, "coarse", None),
    )
    return jax.shard_map(local, mesh=mesh, in_specs=in_specs, out_specs=out_specs, check_vma=False)
```

time: 224 us -> 83.2 us (0.37)
  the two profiles are of different devices: /device:TPU:30 before, /device:TPU:1 now
where the time goes in v1:
time: 83.2 us; the launch traced here: 82.6 us
  Pallas kernels  74.6 us (90%)
  local copies, waits for them, and re-layouts  5.63 us (7%)
  other arithmetic  1.55 us (2%)
    pallas_call x1, Pallas kernels, exchange(): pl.pallas_call(functools.partial(exchange_kernel, sizes), in_specs=[anywh...  50.4 us
    pallas_call x1, Pallas kernels, backward(): pl.pallas_call(backward_kernel, grid=(rows // BLOCK,), in_specs=[pl.Block...  14 us
    pallas_call x1, Pallas kernels, forward(): pl.pallas_call(forward_kernel, grid=(rows // BLOCK,), in_specs=[pl.BlockS...  10.3 us
    unnamed x28, local copies, waits for them, and re-layouts  5.55 us

profile of v1, /device:TPU:1, one launch (start us, length us, event | category | flops | bytes accessed | tf_op | source)
XLA Modules:
  0.0 82.6 jit_solution(4361420658471707709)
XLA Ops:
  0.6 0.7 fusion.1
  1.4 0.1 pad_maximum_fusion.1.lhs_ref
  1.4 0.7 fusion
  2.2 0.1 copy.16.lhs_ref
  2.3 0.0 copy-start.4
  2.3 0.8 copy-done.4
  3.1 0.0 copy-start.2
  3.1 0.0 copy-start.3
  3.1 0.0 copy-start.6
  3.1 0.0 copy-start.7
  3.1 0.0 copy-start.8
  3.1 0.0 copy-start.9
  3.1 0.0 copy-start.10
  3.1 0.0 copy-start.11
  3.1 0.0 copy-start.12
  3.1 0.0 copy-start.5
  3.2 10.3 %forward_modes.1.tile_ref = f32[2,96,24,128]{3,2,1,0:T(8,128)S(1)} custom-call(bf16[48,96]{1,0:T(8,128)(2,1)S(1)} %copy.16.lhs_ref, s32[96,128]{1,0:T(8,128)S(1)} %copy-done.4, f32[5,32,96,128]{3,2,1,0:T(8,128)} %amp_ref.3, bf16[5,48,96,128]{3,2,1,0:T(8,128)(2,1)} %pert_ref.3), custom_call_target="tpu_custom_call" | custom-call | tf_op jit(solution)/shard_map/forward_modes/pallas_call | solution.py:104
  13.5 0.0 copy-start
  13.5 1.4 %copy-done = f32[2,96,24,128]{3,2,1,0:T(8,128)} copy-done((f32[2,96,24,128]{3,2,1,0:T(8,128)}, f32[2,96,24,128]{3,2,1,0:T(8,128)S(1)}, u32[]{:S(2)}) %copy-start) | copy-done | bytes 2359320
  14.9 0.0 copy-done.2
  14.9 0.0 copy-done.3
  14.9 0.0 copy-done.6
  14.9 0.0 copy-done.7
  14.9 0.0 copy-done.8
  14.9 0.0 copy-done.9
  14.9 0.0 copy-done.10
  14.9 0.0 copy-done.11
  14.9 0.0 copy-done.12
  14.9 50.4 %exchange.1 = (f32[24,24,256]{2,1,0:T(8,128)S(1)}, f32[24,24,256]{2,1,0:T(8,128)S(1)}, f32[2,96,24,128]{3,2,1,0:T(8,128)}) custom-call(f32[2,96,24,128]{3,2,1,0:T(8,128)} %copy-done, f32[24,24,256]{2,1,0:T(8,128)S(1)} %copy-done.2, f32[24,24,256]{2,1,0:T(8,128)S(1)} %copy-done.3, f32[24]{0:T(128)S(1)} %copy-done.10, f32[24,256]{1,0:T(8,128)S(1)} %copy-done.6, ...), custom_call_target="tpu_custom_call" | custom-call | tf_op jit(solution)/shard_map/exchange/pallas_call | solution.py:610
  65.3 0.0 copy-done.5
  65.3 0.0 copy-start.1
  65.3 1.7 %copy-done.1 = f32[2,96,24,128]{3,2,1,0:T(8,128)S(1)} copy-done((f32[2,96,24,128]{3,2,1,0:T(8,128)S(1)}, f32[2,96,24,128]{3,2,1,0:T(8,128)}, u32[]{:S(2)}) %copy-start.1) | copy-done | bytes 2359320
  67.0 14.0 %backward_modes.1 = f32[5,32,96,128]{3,2,1,0:T(8,128)} custom-call(bf16[32,144]{1,0:T(8,128)(2,1)S(1)} %pad_maximum_fusion.1.lhs_ref, s32[96,128]{1,0:T(8,128)S(1)} %copy-done.5, f32[5,32,96,128]{3,2,1,0:T(8,128)} %amp_ref.3, bf16[5,48,96,128]{3,2,1,0:T(8,128)(2,1)} %pert_ref.3, f32[2,96,24,128]{3,2,1,0:T(8,128)S(1)} %copy-done.1), custom_call_target="tpu_custom_call" | custom-call | tf_op jit(solution)/shard_map/backward_modes/pallas_call | solution.py:124
  80.9 0.8 copy.19
  81.8 0.8 copy.20
  (1 shorter events, 0.0 us)
Async XLA Ops:
  2.3 0.8 copy-start.4
  3.1 11.8 %copy-start.2 = (f32[24,24,256]{2,1,0:T(8,128)S(1)}, f32[24,24,256]{2,1,0:T(8,128)}, u32[]{:S(2)}) copy-start(f32[24,24,256]{2,1,0:T(8,128)} %control_ref.1) | copy-start | bytes 1769476
  3.1 11.8 %copy-start.3 = (f32[24,24,256]{2,1,0:T(8,128)S(1)}, f32[24,24,256]{2,1,0:T(8,128)}, u32[]{:S(2)}) copy-start(f32[24,24,256]{2,1,0:T(8,128)} %innov_ref.1) | copy-start | bytes 1769476
  3.1 11.8 %copy-start.6 = (f32[24,256]{1,0:T(8,128)S(1)}, f32[24,256]{1,0:T(8,128)}, u32[]{:S(2)}) copy-start(f32[24,256]{1,0:T(8,128)} %spread_ref.1) | copy-start | bytes 73732
  3.1 11.8 %copy-start.7 = (s32[24,256]{1,0:T(8,128)S(1)}, s32[24,256]{1,0:T(8,128)}, u32[]{:S(2)}) copy-start(s32[24,256]{1,0:T(8,128)} %land_ref.1) | copy-start | bytes 73732
  3.1 11.8 %copy-start.8 = (s32[256]{0:T(256)S(1)}, s32[256]{0:T(256)}, u32[]{:S(2)}) copy-start(s32[256]{0:T(256)} %param.19) | copy-start | bytes 3076
  3.1 11.8 %copy-start.9 = (f32[256]{0:T(256)S(1)}, f32[256]{0:T(256)}, u32[]{:S(2)}) copy-start(f32[256]{0:T(256)} %param.20) | copy-start | bytes 3076
  3.1 11.8 %copy-start.10 = (f32[24]{0:T(128)S(1)}, f32[24]{0:T(128)}, u32[]{:S(2)}) copy-start(f32[24]{0:T(128)} %std_ref.1) | copy-start | bytes 292
  3.1 11.8 %copy-start.11 = (s32[24]{0:T(128)S(1)}, s32[24]{0:T(128)}, u32[]{:S(2)}) copy-start(s32[24]{0:T(128)} %row_index_ref.1) | copy-start | bytes 292
  3.1 11.8 %copy-start.12 = (f32[24]{0:T(128)S(1)}, f32[24]{0:T(128)}, u32[]{:S(2)}) copy-start(f32[24]{0:T(128)} %row_weight_ref.1) | copy-start | bytes 292
  3.1 62.1 %copy-start.5 = (s32[96,128]{1,0:T(8,128)S(1)}, s32[96,128]{1,0:T(8,128)}, u32[]{:S(2)}) copy-start(s32[96,128]{1,0:T(8,128)} %count_ref.3) | copy-start | bytes 147460
  13.5 1.4 %copy-start = (f32[2,96,24,128]{3,2,1,0:T(8,128)}, f32[2,96,24,128]{3,2,1,0:T(8,128)S(1)}, u32[]{:S(2)}) copy-start(f32[2,96,24,128]{3,2,1,0:T(8,128)S(1)} %forward_modes.1.tile_ref) | copy-start | bytes 7077892
  65.3 1.7 %copy-start.1 = (f32[2,96,24,128]{3,2,1,0:T(8,128)S(1)}, f32[2,96,24,128]{3,2,1,0:T(8,128)}, u32[]{:S(2)}) copy-start(f32[2,96,24,128]{3,2,1,0:T(8,128)} %get-tuple-element.8.grad_ref) | copy-start | bytes 7077892

commit v2 on v1

--- a/solution.py
+++ b/solution.py
@@ -14,10 +14,11 @@
 EDGE = 4
 GROWN = 32
 ROWS = 12
-XROWS = 7
+XROWS = 6
 YROWS = ROWS - XROWS
 YA = YROWS // 2
-BLOCK = 16
+PITCH = 104
+PIECE = 24
 F32 = jnp.float32
 BF16 = jnp.bfloat16
 
@@ -37,111 +38,100 @@
     return jnp.concatenate([hi, matrix - hi, hi], axis=1).astype(BF16)
 
 
-def forward_kernel(lhs_ref, count_ref, amp_ref, pert_ref, out_ref, wide_ref):
+def backward_kernel(
+    lhs_ref,
+    count_ref,
+    amp_ref,
+    wide_ref,
+    grad_ref,
+    planes_ref,
+    out_ref,
+    grad_static_ref,
+    inc_ref,
+    result,
+    out_sem,
+    plane_sem,
+):
     members, modes = amp_ref.shape[:2]
-    levels = pert_ref.shape[1]
-    wide_ref[...] = pert_ref[...].reshape(wide_ref.shape).astype(F32)
-    amps = amp_ref.reshape(members * modes * BLOCK, 128)
+    levels = wide_ref.shape[1]
+    rows = out_ref.shape[2]
+    plane_out = [
+        pltpu.make_async_copy(
+            planes_ref.at[number, side],
+            ref.at[:, :, pl.ds(128 * side, 128)],
+            plane_sem.at[2 * number + side],
+        )
+        for number, ref in enumerate((grad_static_ref, inc_ref))
+        for side in range(2)
+    ]
+    for copy in plane_out:
+        copy.start()
+    amps = amp_ref.reshape(members * modes * PITCH, 128)
+    perts = wide_ref.reshape(members * levels * PITCH, 128)
+    outs = result.reshape(members * modes * PITCH, 128)
     lhs = lhs_ref[...]
     mode = lax.broadcasted_iota(jnp.int32, (modes, 128), 0)
-
-    def row_pair(step, carry):
-        first = step * 2
-        keep = [mode < count_ref[pl.ds(first + h, 1), :] for h in range(2)]
-        total = [jnp.zeros((levels, 128), F32) for _ in range(2)]
-        for k in range(members):
-            rhs = []
-            for h in range(2):
-                amp = amps[pl.ds(k * modes * BLOCK + first + h, modes, stride=BLOCK), :]
-                rhs.append(stacked(jnp.where(keep[h], amp, 0.0)))
-            level_amp = jnp.dot(lhs, jnp.concatenate(rhs, axis=1), preferred_element_type=F32)
-            for h in range(2):
-                pert = wide_ref[pl.ds(k * levels * BLOCK + first + h, levels, stride=BLOCK), :]
-                total[h] = total[h] + pert * level_amp[:, h * 128 : (h + 1) * 128]
-        for h in range(2):
-            out_ref[0, first + h] = total[h][: levels // 2]
-            out_ref[1, first + h] = total[h][levels // 2 :]
-        return carry
-
-    lax.fori_loop(0, BLOCK // 2, row_pair, 0, unroll=4)
-
-
-def backward_kernel(lhs_ref, count_ref, amp_ref, pert_ref, grad_ref, out_ref, wide_ref):
-    members, modes = amp_ref.shape[:2]
-    levels = pert_ref.shape[1]
-    wide_ref[...] = pert_ref[...].reshape(wide_ref.shape).astype(F32)
-    amps = amp_ref.reshape(members * modes * BLOCK, 128)
-    outs = out_ref.reshape(members * modes * BLOCK, 128)
-    lhs = lhs_ref[...]
-    mode = lax.broadcasted_iota(jnp.int32, (modes, 128), 0)
-
-    def row_pair(step, carry):
-        first = step * 2
-        keep = [mode < count_ref[pl.ds(first + h, 1), :] for h in range(2)]
-        grad = [
-            jnp.concatenate([grad_ref[0, first + h], grad_ref[1, first + h]], axis=0)
-            for h in range(2)
-        ]
-        for k in range(members):
-            rhs = []
-            for h in range(2):
-                pert = wide_ref[pl.ds(k * levels * BLOCK + first + h, levels, stride=BLOCK), :]
-                rhs.append(stacked(pert * grad[h]))
-            proj = jnp.dot(lhs, jnp.concatenate(rhs, axis=1), preferred_element_type=F32)
-            for h in range(2):
-                at = pl.ds(k * modes * BLOCK + first + h, modes, stride=BLOCK)
-                outs[at, :] = amps[at, :] + jnp.where(
-                    keep[h], proj[:, h * 128 : (h + 1) * 128], 0.0
-                )
-        return carry
-
-    lax.fori_loop(0, BLOCK // 2, row_pair, 0, unroll=4)
-
-
-def forward(lhs, count, amp, pert):
-    members, modes, rows, cols = amp.shape
-    levels = pert.shape[1]
-    return pl.pallas_call(
-        forward_kernel,
-        grid=(rows // BLOCK,),
-        in_specs=[
-            pl.BlockSpec(lhs.shape, lambda i: (0, 0)),
-            pl.BlockSpec((BLOCK, cols), lambda i: (i, 0)),
-            pl.BlockSpec((members, modes, BLOCK, cols), lambda i: (0, 0, i, 0)),
-            pl.BlockSpec((members, levels, BLOCK, cols), lambda i: (0, 0, i, 0)),
-        ],
-        out_specs=pl.BlockSpec((2, BLOCK, levels // 2, cols), lambda i: (0, i, 0, 0)),
-        out_shape=jax.ShapeDtypeStruct((2, rows, levels // 2, cols), F32),
-        scratch_shapes=[pltpu.VMEM((members * levels * BLOCK, cols), F32)],
-        compiler_params=pltpu.CompilerParams(vmem_limit_bytes=50 << 20),
-        name="forward_modes",
-    )(lhs, count, amp, pert)
-
-
-def backward(lhs, count, amp, pert, grad):
-    members, modes, rows, cols = amp.shape
-    levels = pert.shape[1]
+    pieces = []
+    for piece in range(rows // PIECE):
+
+        def row_pair(step, carry):
+            first = piece * PIECE + step * 2
+            keep = [mode < count_ref[pl.ds(first + h, 1), :] for h in range(2)]
+            grad = [
+                jnp.concatenate([grad_ref[0, first + h], grad_ref[1, first + h]], axis=0)
+                for h in range(2)
+            ]
+            for k in range(members):
+                rhs = []
+                for h in range(2):
+                    pert = perts[pl.ds(k * levels * PITCH + first + h, levels, stride=PITCH), :]
+                    rhs.append(stacked(pert * grad[h]))
+                proj = jnp.dot(lhs, jnp.concatenate(rhs, axis=1), preferred_element_type=F32)
+                for h in range(2):
+                    at = pl.ds(k * modes * PITCH + first + h, modes, stride=PITCH)
+                    outs[at, :] = amps[at, :] + jnp.where(
+                        keep[h], proj[:, h * 128 : (h + 1) * 128], 0.0
+                    )
+            return carry
+
+        lax.fori_loop(0, PIECE // 2, row_pair, 0, unroll=4)
+        at = pl.ds(piece * PIECE, PIECE)
+        copy = pltpu.make_async_copy(
+            result.at[:, :, at, :], out_ref.at[:, :, at, :], out_sem.at[piece]
+        )
+        copy.start()
+        pieces.append(copy)
+    for copy in plane_out + pieces:
+        copy.wait()
+
+
+def backward(lhs, count, amp, wide, grad, planes, rows):
+    members, modes, _, cols = amp.shape
+    lev_dev, own = planes.shape[2:4]
+    vmem = pl.BlockSpec(memory_space=pltpu.VMEM)
+    anywhere = pl.BlockSpec(memory_space=pl.ANY)
+    field = jax.ShapeDtypeStruct((lev_dev, own, 2 * cols), F32)
     return pl.pallas_call(
         backward_kernel,
-        grid=(rows // BLOCK,),
-        in_specs=[
-            pl.BlockSpec(lhs.shape, lambda i: (0, 0)),
-            pl.BlockSpec((BLOCK, cols), lambda i: (i, 0)),
-            pl.BlockSpec((members, modes, BLOCK, cols), lambda i: (0, 0, i, 0)),
-            pl.BlockSpec((members, levels, BLOCK, cols), lambda i: (0, 0, i, 0)),
-            pl.BlockSpec((2, BLOCK, levels // 2, cols), lambda i: (0, i, 0, 0)),
+        in_specs=[vmem] * 6,
+        out_specs=[anywhere] * 3,
+        out_shape=[jax.ShapeDtypeStruct((members, modes, rows, cols), F32), field, field],
+        scratch_shapes=[
+            pltpu.VMEM(amp.shape, F32),
+            pltpu.SemaphoreType.DMA((rows // PIECE,)),
+            pltpu.SemaphoreType.DMA((4,)),
         ],
-        out_specs=pl.BlockSpec((members, modes, BLOCK, cols), lambda i: (0, 0, i, 0)),
-        out_shape=jax.ShapeDtypeStruct(amp.shape, F32),
-        scratch_shapes=[pltpu.VMEM((members * levels * BLOCK, cols), F32)],
-        compiler_params=pltpu.CompilerParams(vmem_limit_bytes=50 << 20),
+        compiler_params=pltpu.CompilerParams(vmem_limit_bytes=12 << 20),
         name="backward_modes",
-    )(lhs, count, amp, pert, grad)
+    )(lhs, count, amp, wide, grad, planes)
 
 
 def exchange_kernel(
     sizes,
-    tile_ref,
+    lhs_ref,
+    count_ref,
+    amp_ref,
+    pert_ref,
     control_ref,
     innov_ref,
     std_ref,
@@ -151,10 +141,12 @@
     row_weight_ref,
     col_index_ref,
     col_weight_ref,
-    inc_ref,
-    grad_ref,
-    coarse_ref,
-    sums,
+    amp_out,
+    wide,
+    shares,
+    planes_out,
+    tile,
+    narrow,
     core_in,
     x1_in,
     x2_in,
@@ -175,12 +167,10 @@
     sigma,
     col_mat,
     back,
-    shares,
     planes_in,
-    planes_out,
     send_sem,
     recv_sem,
-    copy_sem,
+    load_sem,
     plane_sem,
 ):
     coarse_count, fine_count, rows_all = sizes
@@ -196,6 +186,9 @@
     count = coarse_count * fine_count
     after, before = lax.rem(serial + 1, count), lax.rem(serial + count - 1, count)
     first_row = serial * 2 * ROWS
+    members, modes = amp_ref.shape[:2]
+    levels = pert_ref.shape[1]
+    sums = tile.at[lev]
 
     to_core = (coarse, fine, 1 - lev)
     to_right = (coarse, y * xs + right, lev)
@@ -242,9 +235,25 @@
         ]
         for number, ref in enumerate((control_ref, innov_ref))
     ]
-    for pair in plane_in:
-        for copy in pair:
-            copy.start()
+    for copy in plane_in[0]:
+        copy.start()
+    pert_in = []
+    for k in range(members):
+        copy = pltpu.make_async_copy(pert_ref.at[k], narrow.at[k], load_sem.at[k])
+        copy.start()
+        pert_in.append(copy)
+    amp_in = []
+    for number, (part, ry) in enumerate(
+        ((across // 2, 0), (across // 2, 1), (1 - across // 2, 0), (1 - across // 2, 1))
+    ):
+        at = pl.ds(pl.multiple_of(ry * xs * ROWS + part * PIECE, PIECE), PIECE)
+        copy = pltpu.make_async_copy(
+            amp_ref.at[:, :, at, :], amp_out.at[:, :, at, :], load_sem.at[members + number]
+        )
+        copy.start()
+        amp_in.append(copy)
+    for copy in plane_in[1]:
+        copy.start()
 
     def planes(ref, number, side):
         return ref.at[number, side].reshape(lev_dev * own, 128)
@@ -279,16 +288,6 @@
 
     pl.semaphore_wait(barrier, 6)
 
-    orders = [across, right, left, x]
-    keep_own = pltpu.make_async_copy(tile_ref.at[lev], sums, copy_sem)
-    keep_own.start()
-    core_sends = []
-    for rx in orders:
-        for ry in (0, 1):
-            rows = pl.ds(share(ry, rx), ROWS)
-            core_sends.append(
-                remote(tile_ref.at[1 - lev, rows], core_in.at[rows], to_core)
-            )
     top, bottom = pl.ds(EDGE, HALO), pl.ds(EDGE + own - HALO, HALO)
     low, high = pl.ds(EDGE - HALO, HALO), pl.ds(EDGE + own, HALO)
     halo_sends = [
@@ -296,7 +295,6 @@
         for ref in (cells, field_a)
         for src, dst, device in ((top, high, to_before), (bottom, low, to_after))
     ]
-    keep_own.wait()
 
     def x_rows(ry, rx):
         return pl.ds(share(ry, rx), XROWS)
@@ -315,22 +313,14 @@
             total = total + term[...]
         sums[rows] = total
 
-    quarter = {}
-    for number, rx in enumerate(orders):
-        for ry in (0, 1):
-            core_sends[2 * number + ry].wait_recv()
-            rows = pl.ds(share(ry, rx), ROWS)
-            add(rows, core_in.at[rows])
-        quarter[number] = remote(sums.at[y_rows(rx, "all", other_y)], yq_in.at[number], to_y)
-        if number == 0:
-            x1 = [
-                remote(sums.at[x_rows(0, across)], x1_in.at[0], to_right),
-                remote(sums.at[x_rows(1, across)], x1_in.at[1], to_left),
-            ]
-        if number == 1:
-            x2_right = remote(sums.at[x_rows(1, right)], x2_in.at[0], to_right)
-        if number == 2:
-            x2_left = remote(sums.at[x_rows(0, left)], x2_in.at[1], to_left)
+    for k in range(members):
+        pert_in[k].wait()
+
+        def widen(level, carry):
+            wide[k, level, pl.ds(0, pert_ref.shape[2])] = narrow[k, level].astype(F32)
+            return carry
+
+        lax.fori_loop(0, levels, widen, 0, unroll=4)
 
     for copy in halo_sends[:2]:
         copy.wait_recv()
@@ -370,29 +360,89 @@
     hi, lo = halves(matrix)
     col_mat[0], col_mat[1] = hi, lo
 
-    for rx_copy, rows, slot, device, x3_slot in (
-        (x1[0], x_rows(0, right), 0, to_right, 0),
-        (x1[1], x_rows(1, left), 1, to_left, 1),
-    ):
-        rx_copy.wait_recv()
-        add(rows, x1_in.at[slot])
-        if slot == 0:
-            x3_right = remote(sums.at[rows], x3_in.at[0], device)
-        else:
-            x3_left = remote(sums.at[rows], x3_in.at[1], device)
-
-    for number, rx in enumerate(orders):
-        quarter[number].wait_recv()
-        add(y_rows(rx, "all"), yq_in.at[number])
-        if number == 0:
-            y1 = [
-                remote(sums.at[y_rows(rx, "a")], y1_in.at[0, pl.ds(0, YA)], to_right),
-                remote(sums.at[y_rows(rx, "b")], y1_in.at[1], to_left),
-            ]
-        if number == 1:
-            y2_right = remote(sums.at[y_rows(rx, "b")], y2_in.at[0], to_right)
-        if number == 2:
-            y2_left = remote(sums.at[y_rows(rx, "a")], y2_in.at[1, pl.ds(0, YA)], to_left)
+    amps = amp_out.reshape(members * modes * PITCH, 128)
+    perts = wide.reshape(members * levels * PITCH, 128)
+    lhs = lhs_ref[...]
+    mode = lax.broadcasted_iota(jnp.int32, (modes, 128), 0)
+
+    def contract(start):
+        def row_pair(step, carry):
+            first = start + step * 2
+            keep = [mode < count_ref[pl.ds(first + h, 1), :] for h in range(2)]
+            total = [jnp.zeros((levels, 128), F32) for _ in range(2)]
+            for k in range(members):
+                rhs = []
+                for h in range(2):
+                    amp = amps[pl.ds(k * modes * PITCH + first + h, modes, stride=PITCH), :]
+                    rhs.append(stacked(jnp.where(keep[h], amp, 0.0)))
+                level_amp = jnp.dot(lhs, jnp.concatenate(rhs, axis=1), preferred_element_type=F32)
+                for h in range(2):
+                    pert = perts[pl.ds(k * levels * PITCH + first + h, levels, stride=PITCH), :]
+                    total[h] = total[h] + pert * level_amp[:, h * 128 : (h + 1) * 128]
+            for h in range(2):
+                tile[0, first + h] = total[h][: levels // 2]
+                tile[1, first + h] = total[h][levels // 2 :]
+            return carry
+
+        lax.fori_loop(0, ROWS // 2, row_pair, 0, unroll=3)
+
+    order = [(0, across), (1, across), (0, right), (1, right), (1, left), (0, left), (other_y, x), (y, x)]
+    core_sends = []
+
+    def produce(number):
+        start = share(*order[number])
+        contract(start)
+        rows = pl.ds(start, ROWS)
+        core_sends.append(remote(tile.at[1 - lev, rows], core_in.at[rows], to_core))
+
+    def settle(number):
+        core_sends[number].wait_recv()
+        rows = pl.ds(share(*order[number]), ROWS)
+        add(rows, core_in.at[rows])
+
+    def pass_y(rx, number):
+        return remote(sums.at[y_rows(rx, "all", other_y)], yq_in.at[number], to_y)
+
+    for copy in amp_in[:2]:
+        copy.wait()
+    produce(0)
+    produce(1)
+    for copy in amp_in[2:]:
+        copy.wait()
+    produce(2)
+    settle(0)
+    x1_right = remote(sums.at[x_rows(0, across)], x1_in.at[0], to_right)
+    produce(3)
+    settle(1)
+    x1_left = remote(sums.at[x_rows(1, across)], x1_in.at[1], to_left)
+    q_across = pass_y(across, 0)
+    produce(4)
+    settle(2)
+    produce(5)
+    settle(3)
+    x2_right = remote(sums.at[x_rows(1, right)], x2_in.at[0], to_right)
+    q_right = pass_y(right, 1)
+    produce(6)
+    settle(4)
+    x1_right.wait_recv()
+    add(x_rows(0, right), x1_in.at[0])
+    x3_right = remote(sums.at[x_rows(0, right)], x3_in.at[0], to_right)
+    x1_left.wait_recv()
+    add(x_rows(1, left), x1_in.at[1])
+    x3_left = remote(sums.at[x_rows(1, left)], x3_in.at[1], to_left)
+    produce(7)
+    settle(5)
+    x2_left = remote(sums.at[x_rows(0, left)], x2_in.at[1], to_left)
+    q_left = pass_y(left, 2)
+    settle(6)
+    q_own = pass_y(x, 3)
+    q_across.wait_recv()
+    add(y_rows(across, "all"), yq_in.at[0])
+    y1_right = remote(sums.at[y_rows(across, "a")], y1_in.at[0, pl.ds(0, YA)], to_right)
+    y1_left = remote(sums.at[y_rows(across, "b")], y1_in.at[1], to_left)
+    q_right.wait_recv()
+    add(y_rows(right, "all"), yq_in.at[1])
+    y2_right = remote(sums.at[y_rows(right, "b")], y2_in.at[0], to_right)
 
     def sweep(src, dst):
         def rows_of_four(step, carry):
@@ -417,8 +467,12 @@
         copy.wait_send()
     sweep(field_a, field_b)
 
-    for copy, slot in ((y1[0], 0), (y1[1], 1)):
-        copy.wait_recv()
+    settle(7)
+    q_left.wait_recv()
+    add(y_rows(left, "all"), yq_in.at[2])
+    y2_left = remote(sums.at[y_rows(left, "a")], y2_in.at[1, pl.ds(0, YA)], to_left)
+    y1_right.wait_recv()
+    y1_left.wait_recv()
     a_rows, b_rows = y_rows(right, "a"), y_rows(left, "b")
     add(a_rows, y1_in.at[0, pl.ds(0, YA)])
     y3_right = remote(sums.at[a_rows], y3_in.at[0, pl.ds(0, YA)], to_right)
@@ -426,6 +480,14 @@
     y3_left = remote(sums.at[b_rows], y3_in.at[1], to_left)
 
     sweep(field_b, field_a)
+
+    for copy in (x2_right, x2_left, x3_right, x3_left):
+        copy.wait_recv()
+    rows = x_rows(other_y, x)
+    add(rows, x3_in.at[other_y], x2_in.at[y])
+    x4 = remote(sums.at[rows], x4_in, to_y)
+    add(x_rows(y, x), x3_in.at[y], x2_in.at[other_y])
+
     sweep(field_a, field_b)
 
     def static_part(i, carry):
@@ -446,12 +508,8 @@
         remote(misfit.at[bottom], misfit.at[low], to_after),
     ]
 
-    for copy in (x2_right, x2_left, x3_right, x3_left):
-        copy.wait_recv()
-    rows = x_rows(other_y, x)
-    add(rows, x3_in.at[other_y], x2_in.at[y])
-    x4 = remote(sums.at[rows], x4_in, to_y)
-    add(x_rows(y, x), x3_in.at[y], x2_in.at[other_y])
+    q_own.wait_recv()
+    add(y_rows(x, "all"), yq_in.at[3])
     for copy in (y2_right, y2_left, y3_right, y3_left):
         copy.wait_recv()
     mine = share(y, x)
@@ -568,18 +626,6 @@
         return carry
 
     lax.fori_loop(0, own, finish, 0, unroll=4)
-    plane_out = [
-        pltpu.make_async_copy(
-            planes_out.at[number, side],
-            ref.at[:, :, lanes[side]],
-            plane_sem.at[2 * number + side],
-        )
-        for number, ref in enumerate((grad_ref, inc_ref))
-        for side in range(2)
-    ]
-    for copy in plane_out:
-        copy.start()
-
     for copy in on_x:
         copy.wait_recv()
     for ry in (0, 1):
@@ -589,36 +635,36 @@
         core.append(to_all(y_rows(rx, "all", other_y), to_core))
     for copy in core:
         copy.wait_recv()
-    out = pltpu.make_async_copy(shares, coarse_ref, copy_sem)
-    out.start()
     waited = halo_sends[2:] + misfit_sends
     for copy in sent:
         if not any(copy is done for done in waited):
             copy.wait_send()
-    out.wait()
-    for copy in plane_out:
-        copy.wait()
-
-
-def exchange(sizes, tile, control, innov, std, spread, land, row_index, row_weight, col_index, col_weight):
+
+
+def exchange(sizes, lhs, count, amp, pert, control, innov, std, spread, land, row_index, row_weight, col_index, col_weight):
+    members, modes, rows, cols = amp.shape
+    levels = pert.shape[1]
     lev_dev, own, cols_fine = control.shape
     vmem = pl.BlockSpec(memory_space=pltpu.VMEM)
     smem = pl.BlockSpec(memory_space=pltpu.SMEM)
     anywhere = pl.BlockSpec(memory_space=pl.ANY)
     cell = (lev_dev, 128)
     row = (lev_dev, cols_fine)
+    tile = (2, rows) + cell
     return pl.pallas_call(
         functools.partial(exchange_kernel, sizes),
-        in_specs=[anywhere, anywhere, anywhere, smem, vmem, vmem, smem, smem, vmem, vmem],
-        out_specs=[anywhere, anywhere, anywhere],
+        in_specs=[vmem, vmem, anywhere, anywhere, anywhere, anywhere, smem, vmem, vmem, smem, smem, vmem, vmem],
+        out_specs=[vmem] * 4,
         out_shape=[
-            jax.ShapeDtypeStruct(control.shape, F32),
-            jax.ShapeDtypeStruct(control.shape, F32),
-            jax.ShapeDtypeStruct(tile.shape, F32),
+            pltpu.VMEM((members, modes, PITCH, cols), F32),
+            pltpu.VMEM((members, levels, PITCH, cols), F32),
+            pltpu.VMEM(tile, F32),
+            pltpu.VMEM((2, 2, lev_dev, own, 128), F32),
         ],
         scratch_shapes=[
-            pltpu.VMEM(tile.shape[1:], F32),
-            pltpu.VMEM(tile.shape[1:], F32),
+            pltpu.VMEM(tile, F32),
+            pltpu.VMEM(pert.shape, BF16),
+            pltpu.VMEM((rows,) + cell, F32),
             pltpu.VMEM((2, XROWS) + cell, F32),
             pltpu.VMEM((2, XROWS) + cell, F32),
             pltpu.VMEM((2, XROWS) + cell, F32),
@@ -638,20 +684,21 @@
             pltpu.VMEM(row, F32),
             pltpu.VMEM((2, 128, cols_fine), BF16),
             pltpu.VMEM((GROWN,) + cell, F32),
-            pltpu.VMEM(tile.shape, F32),
-            pltpu.VMEM((2, 2, lev_dev, own, 128), F32),
             pltpu.VMEM((2, 2, lev_dev, own, 128), F32),
             pltpu.SemaphoreType.DMA((80,)),
             pltpu.SemaphoreType.DMA((80,)),
-            pltpu.SemaphoreType.DMA,
+            pltpu.SemaphoreType.DMA((members + 4,)),
             pltpu.SemaphoreType.DMA((4,)),
         ],
         compiler_params=pltpu.CompilerParams(
-            collective_id=0, has_side_effects=True, vmem_limit_bytes=50 << 20
+            collective_id=0, has_side_effects=True, vmem_limit_bytes=24 << 20
         ),
         name="exchange",
     )(
-        tile,
+        lhs,
+        count,
+        amp,
+        pert,
         control,
         innov,
         std,
@@ -685,10 +732,12 @@
         lax.axis_size("coarse") * lax.axis_size("fine") * row_index.shape[0],
     )
     scaled = eigen_modes * (1.0 / math.sqrt(MEMBERS - 1))
-    tile = forward(split_modes(scaled), mode_count, ens_control, ens_pert)
-    increment, grad_static, coarse_grad = exchange(
+    amp, wide, coarse_grad, planes = exchange(
         sizes,
-        tile,
+        split_modes(scaled),
+        mode_count,
+        ens_control,
+        ens_pert,
         static_control,
         innovation,
         static_std,
@@ -699,7 +748,9 @@
         col_index,
         col_weight,
     )
-    grad_ens = backward(split_modes(scaled.T), mode_count, ens_control, ens_pert, coarse_grad)
+    grad_ens, grad_static, increment = backward(
+        split_modes(scaled.T), mode_count, amp, wide, coarse_grad, planes, mode_count.shape[0]
+    )
     return increment, grad_static, grad_ens
 
 

time: 83.2 us -> 72.8 us (0.87)
  Pallas kernels: 74.6 us -> 62.3 us
  local copies, waits for them, and re-layouts: 5.63 us -> 7.81 us
    pallas_call x3 -> x2, Pallas kernels: 74.6 us -> 62.3 us  [the longest x1 55 us: exchange(): pl.pallas_call(functools.partial(exchange_kernel, sizes), in_specs=[vmem,...]
    unnamed x28 -> x20, local copies, waits for them, and re-layouts: 5.55 us -> 7.73 us
where the time goes in v2:
time: 72.8 us; the launch traced here: 72.3 us
  Pallas kernels  62.3 us (86%)
  local copies, waits for them, and re-layouts  7.81 us (11%)
  other arithmetic  1.55 us (2%)
    pallas_call x1, Pallas kernels, exchange(): pl.pallas_call(functools.partial(exchange_kernel, sizes), in_specs=[vmem,...  55 us
    unnamed x20, local copies, waits for them, and re-layouts  7.73 us
    pallas_call x1, Pallas kernels, backward(): pl.pallas_call(backward_kernel, in_specs=[vmem] * 6, out_specs=[anywhere]...  7.29 us

profile of v2, /device:TPU:1, one launch (start us, length us, event | category | flops | bytes accessed | tf_op | source)
XLA Modules:
  0.0 72.3 jit_solution(15181368606024685896)
XLA Ops:
  0.6 0.7 %fusion = (bf16[32,48]{1,0:T(8,128)(2,1)S(1)}, bf16[32,48]{1,0:T(8,128)(2,1)S(1)}) fusion(f32[48,32]{0,1:T(8,128)} %param.15), kind=kLoop, calls=%fused_computation.5 | loop fusion | flops 7680 | bytes 12288 | tf_op jit(solution)/shard_map/convert.4
  1.4 0.1 pad_maximum_fusion.1.lhs_ref
  1.4 0.7 %fusion.1 = (bf16[48,32]{0,1:T(8,128)(2,1)S(1)}, bf16[48,32]{0,1:T(8,128)(2,1)S(1)}) fusion(f32[48,32]{0,1:T(8,128)} %param.15), kind=kLoop, calls=%fused_computation.6 | loop fusion | flops 7680 | bytes 12288 | tf_op jit(solution)/shard_map/convert.1
  2.2 0.1 copy.16.lhs_ref
  2.3 0.0 copy-start
  2.3 1.1 %copy-done = f32[24,24,256]{2,1,0:T(8,128)S(1)} copy-done((f32[24,24,256]{2,1,0:T(8,128)S(1)}, f32[24,24,256]{2,1,0:T(8,128)}, u32[]{:S(2)}) %copy-start) | copy-done | bytes 589848
  3.3 0.0 copy-start.1
  3.3 1.1 %copy-done.1 = f32[24,24,256]{2,1,0:T(8,128)S(1)} copy-done((f32[24,24,256]{2,1,0:T(8,128)S(1)}, f32[24,24,256]{2,1,0:T(8,128)}, u32[]{:S(2)}) %copy-start.1) | copy-done | bytes 589848
  4.4 0.0 copy-start.2
  4.4 0.8 %copy-done.2 = s32[96,128]{1,0:T(8,128)S(1)} copy-done((s32[96,128]{1,0:T(8,128)S(1)}, s32[96,128]{1,0:T(8,128)}, u32[]{:S(2)}) %copy-start.2) | copy-done | bytes 49176
  5.2 0.0 copy-start.3
  5.2 0.7 %copy-done.3 = f32[24,256]{1,0:T(8,128)S(1)} copy-done((f32[24,256]{1,0:T(8,128)S(1)}, f32[24,256]{1,0:T(8,128)}, u32[]{:S(2)}) %copy-start.3) | copy-done | bytes 24600
  5.9 0.0 copy-start.4
  5.9 0.7 %copy-done.4 = s32[24,256]{1,0:T(8,128)S(1)} copy-done((s32[24,256]{1,0:T(8,128)S(1)}, s32[24,256]{1,0:T(8,128)}, u32[]{:S(2)}) %copy-start.4) | copy-done | bytes 24600
  6.7 0.0 copy-start.5
  6.7 0.7 copy-done.5
  7.4 0.0 copy-start.6
  7.4 0.7 copy-done.6
  8.0 0.0 copy-start.7
  8.0 0.7 copy-done.7
  8.7 0.0 copy-start.8
  8.7 0.7 copy-done.8
  9.4 0.0 copy-start.9
  9.4 0.7 copy-done.9
  10.0 55.0 %exchange.1 = (f32[5,32,104,128]{3,2,1,0:T(8,128)S(1)}, f32[5,48,104,128]{3,2,1,0:T(8,128)S(1)}, f32[2,96,24,128]{3,2,1,0:T(8,128)S(1)}, f32[2,2,24,24,128]{4,3,2,1,0:T(8,128)S(1)}) custom-call(bf16[48,96]{1,0:T(8,128)(2,1)S(1)} %copy.16.lhs_ref, s32[96,128]{1,0:T(8,128)S(1)} %copy-done.2, f32[5,32,96,128]{3,2,1,0:T(8,128)} %amp_ref.1, ...), custom_call_target="tpu_custom_call" | custom-call | tf_op jit(solution)/shard_map/exchange/pallas_call | solution.py:654
  65.0 7.3 %backward_modes.1 = (f32[5,32,96,128]{3,2,1,0:T(8,128)}, f32[24,24,256]{2,1,0:T(8,128)}, f32[24,24,256]{2,1,0:T(8,128)}) custom-call(bf16[32,144]{1,0:T(8,128)(2,1)S(1)} %pad_maximum_fusion.1.lhs_ref, s32[96,128]{1,0:T(8,128)S(1)} %copy-done.2, f32[5,32,104,128]{3,2,1,0:T(8,128)S(1)} %get-tuple-element.10.amp_ref, ...), custom_call_target="tpu_custom_call" | custom-call | tf_op jit(solution)/shard_map/backward_modes/pallas_call | solution.py:114
  (1 shorter events, 0.0 us)
Async XLA Ops:
  2.3 1.1 %copy-start = (f32[24,24,256]{2,1,0:T(8,128)S(1)}, f32[24,24,256]{2,1,0:T(8,128)}, u32[]{:S(2)}) copy-start(f32[24,24,256]{2,1,0:T(8,128)} %control_ref.1) | copy-start | bytes 1769476
  3.3 1.1 %copy-start.1 = (f32[24,24,256]{2,1,0:T(8,128)S(1)}, f32[24,24,256]{2,1,0:T(8,128)}, u32[]{:S(2)}) copy-start(f32[24,24,256]{2,1,0:T(8,128)} %innov_ref.1) | copy-start | bytes 1769476
  4.4 0.8 %copy-start.2 = (s32[96,128]{1,0:T(8,128)S(1)}, s32[96,128]{1,0:T(8,128)}, u32[]{:S(2)}) copy-start(s32[96,128]{1,0:T(8,128)} %count_ref.3) | copy-start | bytes 147460
  5.2 0.7 %copy-start.3 = (f32[24,256]{1,0:T(8,128)S(1)}, f32[24,256]{1,0:T(8,128)}, u32[]{:S(2)}) copy-start(f32[24,256]{1,0:T(8,128)} %spread_ref.1) | copy-start | bytes 73732
  5.9 0.7 %copy-start.4 = (s32[24,256]{1,0:T(8,128)S(1)}, s32[24,256]{1,0:T(8,128)}, u32[]{:S(2)}) copy-start(s32[24,256]{1,0:T(8,128)} %land_ref.1) | copy-start | bytes 73732
  6.7 0.7 copy-start.5
  7.4 0.7 copy-start.6
  8.0 0.7 copy-start.7
  8.7 0.7 copy-start.8
  9.4 0.7 copy-start.9

commit v3 on v2

--- a/solution.py
+++ b/solution.py
@@ -35,7 +35,10 @@
 
 def split_modes(matrix):
     hi = lax.reduce_precision(matrix, 8, 7)
-    return jnp.concatenate([hi, matrix - hi, hi], axis=1).astype(BF16)
+    lo = matrix - hi
+    wide = jnp.concatenate([hi, lo, hi], axis=1).astype(BF16)
+    tall = jnp.concatenate([hi, lo, hi], axis=0).astype(BF16)
+    return tall.T, wide
 
 
 def backward_kernel(
@@ -129,22 +132,23 @@
 def exchange_kernel(
     sizes,
     lhs_ref,
-    count_ref,
+    count_in,
     amp_ref,
     pert_ref,
     control_ref,
     innov_ref,
-    std_ref,
-    spread_ref,
-    land_ref,
-    row_index_ref,
-    row_weight_ref,
-    col_index_ref,
-    col_weight_ref,
+    std_in,
+    spread_in,
+    land_in,
+    row_index_in,
+    row_weight_in,
+    col_index_in,
+    col_weight_in,
     amp_out,
     wide,
     shares,
     planes_out,
+    count_ref,
     tile,
     narrow,
     core_in,
@@ -168,10 +172,18 @@
     col_mat,
     back,
     planes_in,
+    std_ref,
+    spread_ref,
+    land_ref,
+    row_index_ref,
+    row_weight_ref,
+    col_index_ref,
+    col_weight_ref,
     send_sem,
     recv_sem,
     load_sem,
     plane_sem,
+    small_sem,
 ):
     coarse_count, fine_count, rows_all = sizes
     xs = fine_count // 2
@@ -235,30 +247,50 @@
         ]
         for number, ref in enumerate((control_ref, innov_ref))
     ]
-    for copy in plane_in[0]:
+    small_in = [
+        pltpu.make_async_copy(src, dst, small_sem.at[number])
+        for number, (src, dst) in enumerate(
+            (
+                (spread_in, spread_ref),
+                (land_in, land_ref),
+                (row_index_in, row_index_ref),
+                (row_weight_in, row_weight_ref),
+                (std_in, std_ref),
+                (col_index_in, col_index_ref),
+                (col_weight_in, col_weight_ref),
+                (count_in, count_ref),
+            )
+        )
+    ]
+    for copy in small_in + plane_in[0]:
         copy.start()
-    pert_in = []
-    for k in range(members):
-        copy = pltpu.make_async_copy(pert_ref.at[k], narrow.at[k], load_sem.at[k])
-        copy.start()
-        pert_in.append(copy)
-    amp_in = []
-    for number, (part, ry) in enumerate(
-        ((across // 2, 0), (across // 2, 1), (1 - across // 2, 0), (1 - across // 2, 1))
-    ):
-        at = pl.ds(pl.multiple_of(ry * xs * ROWS + part * PIECE, PIECE), PIECE)
-        copy = pltpu.make_async_copy(
-            amp_ref.at[:, :, at, :], amp_out.at[:, :, at, :], load_sem.at[members + number]
-        )
-        copy.start()
-        amp_in.append(copy)
+    half_rows = xs * ROWS
+    pert_in, amp_in = [], []
+    for half, ry in enumerate((other_y, y)):
+        at = pl.ds(pl.multiple_of(ry * half_rows, 16), half_rows)
+        for k in range(members):
+            copy = pltpu.make_async_copy(
+                pert_ref.at[k, :, at, :], narrow.at[k, :, at, :], load_sem.at[half * members + k]
+            )
+            copy.start()
+            pert_in.append(copy)
+        for part in (0, 1):
+            column = lax.rem(across // 2 + part, 2)
+            at = pl.ds(pl.multiple_of(ry * half_rows + column * PIECE, PIECE), PIECE)
+            copy = pltpu.make_async_copy(
+                amp_ref.at[:, :, at, :],
+                amp_out.at[:, :, at, :],
+                load_sem.at[2 * members + 2 * half + part],
+            )
+            copy.start()
+            amp_in.append(copy)
     for copy in plane_in[1]:
         copy.start()
 
     def planes(ref, number, side):
         return ref.at[number, side].reshape(lev_dev * own, 128)
 
-    for copy in plane_in[0]:
+    for copy in small_in + plane_in[0]:
         copy.wait()
 
     def load_rows(i, carry):
@@ -313,14 +345,18 @@
             total = total + term[...]
         sums[rows] = total
 
-    for k in range(members):
-        pert_in[k].wait()
-
-        def widen(level, carry):
-            wide[k, level, pl.ds(0, pert_ref.shape[2])] = narrow[k, level].astype(F32)
-            return carry
-
-        lax.fori_loop(0, levels, widen, 0, unroll=4)
+    def widen(half):
+        at = pl.ds(pl.multiple_of((other_y, y)[half] * half_rows, 16), half_rows)
+        for k in range(members):
+            pert_in[half * members + k].wait()
+
+            def widen_level(level, carry):
+                wide[k, level, at] = narrow[k, level, at].astype(F32)
+                return carry
+
+            lax.fori_loop(0, levels, widen_level, 0, unroll=8)
+
+    widen(0)
 
     for copy in halo_sends[:2]:
         copy.wait_recv()
@@ -386,7 +422,16 @@
 
         lax.fori_loop(0, ROWS // 2, row_pair, 0, unroll=3)
 
-    order = [(0, across), (1, across), (0, right), (1, right), (1, left), (0, left), (other_y, x), (y, x)]
+    order = [
+        (other_y, across),
+        (other_y, right),
+        (other_y, left),
+        (other_y, x),
+        (y, across),
+        (y, left),
+        (y, right),
+        (y, x),
+    ]
     core_sends = []
 
     def produce(number):
@@ -403,48 +448,53 @@
     def pass_y(rx, number):
         return remote(sums.at[y_rows(rx, "all", other_y)], yq_in.at[number], to_y)
 
-    for copy in amp_in[:2]:
-        copy.wait()
+    amp_in[0].wait()
     produce(0)
+    amp_in[1].wait()
     produce(1)
-    for copy in amp_in[2:]:
-        copy.wait()
     produce(2)
+    produce(3)
     settle(0)
-    x1_right = remote(sums.at[x_rows(0, across)], x1_in.at[0], to_right)
-    produce(3)
+    x1_right = remote(sums.at[x_rows(other_y, across)], x1_in.at[0], to_right)
+    q_across = pass_y(across, 0)
+    widen(1)
     settle(1)
-    x1_left = remote(sums.at[x_rows(1, across)], x1_in.at[1], to_left)
-    q_across = pass_y(across, 0)
+    q_right = pass_y(right, 1)
+    amp_in[2].wait()
     produce(4)
     settle(2)
+    x2_left = remote(sums.at[x_rows(other_y, left)], x2_in.at[1], to_left)
+    q_left = pass_y(left, 2)
+    amp_in[3].wait()
     produce(5)
     settle(3)
-    x2_right = remote(sums.at[x_rows(1, right)], x2_in.at[0], to_right)
-    q_right = pass_y(right, 1)
+    q_own = pass_y(x, 3)
+    settle(4)
+    x1_left = remote(sums.at[x_rows(y, across)], x1_in.at[1], to_left)
     produce(6)
-    settle(4)
     x1_right.wait_recv()
-    add(x_rows(0, right), x1_in.at[0])
-    x3_right = remote(sums.at[x_rows(0, right)], x3_in.at[0], to_right)
-    x1_left.wait_recv()
-    add(x_rows(1, left), x1_in.at[1])
-    x3_left = remote(sums.at[x_rows(1, left)], x3_in.at[1], to_left)
-    produce(7)
-    settle(5)
-    x2_left = remote(sums.at[x_rows(0, left)], x2_in.at[1], to_left)
-    q_left = pass_y(left, 2)
-    settle(6)
-    q_own = pass_y(x, 3)
+    add(x_rows(other_y, right), x1_in.at[0])
+    x3_right = remote(sums.at[x_rows(other_y, right)], x3_in.at[0], to_right)
     q_across.wait_recv()
     add(y_rows(across, "all"), yq_in.at[0])
     y1_right = remote(sums.at[y_rows(across, "a")], y1_in.at[0, pl.ds(0, YA)], to_right)
     y1_left = remote(sums.at[y_rows(across, "b")], y1_in.at[1], to_left)
+    settle(5)
+    produce(7)
+    settle(6)
+    x2_right = remote(sums.at[x_rows(y, right)], x2_in.at[0], to_right)
     q_right.wait_recv()
     add(y_rows(right, "all"), yq_in.at[1])
     y2_right = remote(sums.at[y_rows(right, "b")], y2_in.at[0], to_right)
-
-    def sweep(src, dst):
+    q_left.wait_recv()
+    add(y_rows(left, "all"), yq_in.at[2])
+    y2_left = remote(sums.at[y_rows(left, "a")], y2_in.at[1, pl.ds(0, YA)], to_left)
+    x1_left.wait_recv()
+    add(x_rows(y, left), x1_in.at[1])
+    x3_left = remote(sums.at[x_rows(y, left)], x3_in.at[1], to_left)
+    settle(7)
+
+    def sweep(src, dst, first=0, last=7):
         def rows_of_four(step, carry):
             e = EDGE - 2 + 4 * step
             down = row_faces[pl.ds(e - 1, 5)]
@@ -460,17 +510,13 @@
                 )
             return carry
 
-        lax.fori_loop(0, 7, rows_of_four, 0)
+        lax.fori_loop(first, last, rows_of_four, 0)
 
     for copy in halo_sends[2:]:
         copy.wait_recv()
         copy.wait_send()
     sweep(field_a, field_b)
 
-    settle(7)
-    q_left.wait_recv()
-    add(y_rows(left, "all"), yq_in.at[2])
-    y2_left = remote(sums.at[y_rows(left, "a")], y2_in.at[1, pl.ds(0, YA)], to_left)
     y1_right.wait_recv()
     y1_left.wait_recv()
     a_rows, b_rows = y_rows(right, "a"), y_rows(left, "b")
@@ -479,15 +525,13 @@
     add(b_rows, y1_in.at[1])
     y3_left = remote(sums.at[b_rows], y3_in.at[1], to_left)
 
+    x3_right.wait_recv()
+    x2_left.wait_recv()
+    rows = x_rows(other_y, x)
+    add(rows, x3_in.at[0], x2_in.at[1])
+    x4 = remote(sums.at[rows], x4_in, to_y)
+
     sweep(field_b, field_a)
-
-    for copy in (x2_right, x2_left, x3_right, x3_left):
-        copy.wait_recv()
-    rows = x_rows(other_y, x)
-    add(rows, x3_in.at[other_y], x2_in.at[y])
-    x4 = remote(sums.at[rows], x4_in, to_y)
-    add(x_rows(y, x), x3_in.at[y], x2_in.at[other_y])
-
     sweep(field_a, field_b)
 
     def static_part(i, carry):
@@ -508,6 +552,9 @@
         remote(misfit.at[bottom], misfit.at[low], to_after),
     ]
 
+    x3_left.wait_recv()
+    x2_right.wait_recv()
+    add(x_rows(y, x), x3_in.at[1], x2_in.at[0])
     q_own.wait_recv()
     add(y_rows(x, "all"), yq_in.at[3])
     for copy in (y2_right, y2_left, y3_right, y3_left):
@@ -553,6 +600,7 @@
         at = pl.ds(e0, span)
         total = misfit[at] + fine_part.reshape(span, lev_dev, 256)
         misfit[at] = total
+        field_a[at] = sigma[...] * total
         back[at] = dot_split(total.reshape(span * lev_dev, 256), 1).reshape(span, lev_dev, 128)
         return carry
 
@@ -580,13 +628,8 @@
     core = [to_all(pl.ds(mine, ROWS), to_core)]
     pair_y = [to_all(y_rows(x, "all"), to_y)]
 
-    def scaled(e, carry):
-        at = pl.ds(e * 2 + 1, 2)
-        field_a[at] = sigma[...] * misfit[at]
-        return carry
-
-    lax.fori_loop(0, (GROWN - 2) // 2, scaled, 0)
-
+    sweep(field_a, field_b)
+    sweep(field_b, field_a, 0, 3)
     pair_first.wait_recv()
     ring_other = [to_all(x_part(other_y, x), to_right), to_all(x_part(other_y, x), to_left)]
     core.append(to_all(x_part(other_y, x), to_core))
@@ -600,21 +643,23 @@
         pair_y.append(to_all(y_rows(rx, "all"), to_y))
         core.append(to_all(y_rows(rx, "all"), to_core))
 
-    sweep(field_a, field_b)
-
-    for copy in ring_own + ring_other:
-        copy.wait_recv()
-    on_x = [to_all(x_part(0, left), to_right), to_all(x_part(1, right), to_left)]
+    sweep(field_b, field_a, 3, 7)
+    for copy in ring_own:
+        copy.wait_recv()
+    on_x = [to_all(x_part(y, right), to_left)]
     for rx in (left, right):
-        for ry in (0, 1):
-            core.append(to_all(x_part(ry, rx), to_core))
+        core.append(to_all(x_part(y, rx), to_core))
+    sweep(field_a, field_b, 0, 3)
     for copy in on_y:
         copy.wait_recv()
     pair_y.append(to_all(y_rows(across, "all"), to_y))
     core.append(to_all(y_rows(across, "all"), to_core))
-
-    sweep(field_b, field_a)
-    sweep(field_a, field_b)
+    sweep(field_a, field_b, 3, 7)
+    for copy in ring_other:
+        copy.wait_recv()
+    on_x.append(to_all(x_part(other_y, left), to_right))
+    for rx in (left, right):
+        core.append(to_all(x_part(other_y, rx), to_core))
 
     def finish(i, carry):
         at = pl.ds(i, lev_dev, stride=own)
@@ -626,13 +671,15 @@
         return carry
 
     lax.fori_loop(0, own, finish, 0, unroll=4)
-    for copy in on_x:
-        copy.wait_recv()
-    for ry in (0, 1):
-        core.append(to_all(x_part(ry, across), to_core))
-    for rx, copy in zip((x, left, right, across), pair_y):
+    for rx, copy in zip((x, left, right), pair_y):
         copy.wait_recv()
         core.append(to_all(y_rows(rx, "all", other_y), to_core))
+    on_x[0].wait_recv()
+    core.append(to_all(x_part(y, across), to_core))
+    pair_y[3].wait_recv()
+    core.append(to_all(y_rows(across, "all", other_y), to_core))
+    on_x[1].wait_recv()
+    core.append(to_all(x_part(other_y, across), to_core))
     for copy in core:
         copy.wait_recv()
     waited = halo_sends[2:] + misfit_sends
@@ -646,20 +693,20 @@
     levels = pert.shape[1]
     lev_dev, own, cols_fine = control.shape
     vmem = pl.BlockSpec(memory_space=pltpu.VMEM)
-    smem = pl.BlockSpec(memory_space=pltpu.SMEM)
     anywhere = pl.BlockSpec(memory_space=pl.ANY)
     cell = (lev_dev, 128)
     row = (lev_dev, cols_fine)
     tile = (2, rows) + cell
     return pl.pallas_call(
         functools.partial(exchange_kernel, sizes),
-        in_specs=[vmem, vmem, anywhere, anywhere, anywhere, anywhere, smem, vmem, vmem, smem, smem, vmem, vmem],
-        out_specs=[vmem] * 4,
+        in_specs=[vmem] + [anywhere] * 12,
+        out_specs=[vmem] * 5,
         out_shape=[
             pltpu.VMEM((members, modes, PITCH, cols), F32),
             pltpu.VMEM((members, levels, PITCH, cols), F32),
             pltpu.VMEM(tile, F32),
             pltpu.VMEM((2, 2, lev_dev, own, 128), F32),
+            pltpu.VMEM(count.shape, jnp.int32),
         ],
         scratch_shapes=[
             pltpu.VMEM(tile, F32),
@@ -685,10 +732,18 @@
             pltpu.VMEM((2, 128, cols_fine), BF16),
             pltpu.VMEM((GROWN,) + cell, F32),
             pltpu.VMEM((2, 2, lev_dev, own, 128), F32),
+            pltpu.SMEM(std.shape, F32),
+            pltpu.VMEM(spread.shape, F32),
+            pltpu.VMEM(land.shape, jnp.int32),
+            pltpu.SMEM(row_index.shape, jnp.int32),
+            pltpu.SMEM(row_weight.shape, F32),
+            pltpu.VMEM((1, cols_fine), jnp.int32),
+            pltpu.VMEM((1, cols_fine), F32),
             pltpu.SemaphoreType.DMA((80,)),
             pltpu.SemaphoreType.DMA((80,)),
-            pltpu.SemaphoreType.DMA((members + 4,)),
+            pltpu.SemaphoreType.DMA((2 * members + 4,)),
             pltpu.SemaphoreType.DMA((4,)),
+            pltpu.SemaphoreType.DMA((8,)),
         ],
         compiler_params=pltpu.CompilerParams(
             collective_id=0, has_side_effects=True, vmem_limit_bytes=24 << 20
@@ -696,18 +751,23 @@
         name="exchange",
     )(
         lhs,
-        count,
-        amp,
-        pert,
-        control,
-        innov,
-        std,
-        spread,
-        land,
-        row_index,
-        row_weight,
-        col_index.reshape(1, cols_fine),
-        col_weight.reshape(1, cols_fine),
+        *(
+            pltpu.with_memory_space_constraint(operand, pltpu.HBM)
+            for operand in (
+                count,
+                amp,
+                pert,
+                control,
+                innov,
+                std,
+                spread,
+                land,
+                row_index,
+                row_weight,
+                col_index.reshape(1, cols_fine),
+                col_weight.reshape(1, cols_fine),
+            )
+        ),
     )
 
 
@@ -732,9 +792,10 @@
         lax.axis_size("coarse") * lax.axis_size("fine") * row_index.shape[0],
     )
     scaled = eigen_modes * (1.0 / math.sqrt(MEMBERS - 1))
-    amp, wide, coarse_grad, planes = exchange(
+    tall, across = split_modes(scaled.T)
+    amp, wide, coarse_grad, planes, count = exchange(
         sizes,
-        split_modes(scaled),
+        tall,
         mode_count,
         ens_control,
         ens_pert,
@@ -749,7 +810,7 @@
         col_weight,
     )
     grad_ens, grad_static, increment = backward(
-        split_modes(scaled.T), mode_count, amp, wide, coarse_grad, planes, mode_count.shape[0]
+        across, count, amp, wide, coarse_grad, planes, mode_count.shape[0]
     )
     return increment, grad_static, grad_ens
 

time: 72.8 us -> 62.1 us (0.85)
  local copies, waits for them, and re-layouts: 7.81 us -> 0.08 us
  Pallas kernels: 62.3 us -> 60.4 us
  other arithmetic: 1.55 us -> 0.82 us
    unnamed x20 -> x0, local copies, waits for them, and re-layouts: 7.73 us -> none
    pallas_call x1, Pallas kernels: 55 us -> 53.1 us  [exchange(): pl.pallas_call(functools.partial(exchange_kernel, sizes), in_specs=[vmem]...]
where the time goes in v3:
time: 62.1 us; the launch traced here: 62 us
  Pallas kernels  60.4 us (97%)
  other arithmetic  0.82 us (1%)
  between operations  0.65 us (1%)
    pallas_call x1, Pallas kernels, exchange(): pl.pallas_call(functools.partial(exchange_kernel, sizes), in_specs=[vmem]...  53.1 us
    pallas_call x1, Pallas kernels, backward(): pl.pallas_call(backward_kernel, in_specs=[vmem] * 6, out_specs=[anywhere]...  7.37 us

profile of v3, /device:TPU:1, one launch (start us, length us, event | category | flops | bytes accessed | tf_op | source)
XLA Modules:
  0.0 62.0 jit_solution(13925147599961894669)
XLA Ops:
  0.6 0.7 %fusion = (bf16[32,48]{1,0:T(8,128)(2,1)S(1)}, bf16[32,48]{1,0:T(8,128)(2,1)S(1)}) fusion(f32[48,32]{0,1:T(8,128)} %param.15), kind=kLoop, calls=%fused_computation.3 | loop fusion | flops 7680 | bytes 12288 | tf_op jit(solution)/shard_map/convert.4
  1.4 0.1 pad_maximum_fusion.lhs_ref
  1.5 0.1 copy.16.lhs_ref
  1.5 53.1 %exchange.1 = (f32[5,32,104,128]{3,2,1,0:T(8,128)S(1)}, f32[5,48,104,128]{3,2,1,0:T(8,128)S(1)}, f32[2,96,24,128]{3,2,1,0:T(8,128)S(1)}, f32[2,2,24,24,128]{4,3,2,1,0:T(8,128)S(1)}, s32[96,128]{1,0:T(8,128)S(1)}) custom-call(bf16[48,96]{1,0:T(8,128)(2,1)S(1)} %copy.16.lhs_ref, s32[96,128]{1,0:T(8,128)} %count_in.1, f32[5,32,96,128]{3,2,1,0:T(8,128)} %amp_ref.1, ...), custom_call_target="tpu_custom_call" | custom-call | tf_op jit(solution)/shard_map/exchange/pallas_call | solution.py:700
  54.6 7.4 %backward_modes.1 = (f32[5,32,96,128]{3,2,1,0:T(8,128)}, f32[24,24,256]{2,1,0:T(8,128)}, f32[24,24,256]{2,1,0:T(8,128)}) custom-call(bf16[32,144]{1,0:T(8,128)(2,1)S(1)} %pad_maximum_fusion.lhs_ref, s32[96,128]{1,0:T(8,128)S(1)} %get-tuple-element.11.count_ref, f32[5,32,104,128]{3,2,1,0:T(8,128)S(1)} %get-tuple-element.12.amp_ref, ...), custom_call_target="tpu_custom_call" | custom-call | tf_op jit(solution)/shard_map/backward_modes/pallas_call | solution.py:117
  (1 shorter events, 0.0 us)

commit v4 on v3

--- a/solution.py
+++ b/solution.py
@@ -14,9 +14,8 @@
 EDGE = 4
 GROWN = 32
 ROWS = 12
-XROWS = 6
+XROWS = 5
 YROWS = ROWS - XROWS
-YA = YROWS // 2
 PITCH = 104
 PIECE = 24
 F32 = jnp.float32
@@ -152,14 +151,10 @@
     tile,
     narrow,
     core_in,
-    x1_in,
-    x2_in,
-    x3_in,
-    x4_in,
-    yq_in,
-    y1_in,
-    y2_in,
-    y3_in,
+    x_in,
+    pair_x_in,
+    pair_y_in,
+    y_in,
     window,
     field_a,
     field_b,
@@ -205,12 +200,13 @@
     to_core = (coarse, fine, 1 - lev)
     to_right = (coarse, y * xs + right, lev)
     to_left = (coarse, y * xs + left, lev)
+    to_across = (coarse, y * xs + across, lev)
     to_y = (coarse, other_y * xs + x, lev)
     to_after = (after // fine_count, lax.rem(after, fine_count), lev)
     to_before = (before // fine_count, lax.rem(before, fine_count), lev)
 
     barrier = pltpu.get_barrier_semaphore()
-    for device in (to_core, to_right, to_left, to_y, to_after, to_before):
+    for device in (to_core, to_right, to_left, to_across, to_y, to_after, to_before):
         pl.semaphore_signal(barrier, inc=1, device_id=device, device_id_type=pl.DeviceIdType.MESH)
 
     numbers = iter(range(100))
@@ -235,7 +231,34 @@
 
     lev_dev = control_ref.shape[0]
     own = 2 * ROWS
+    half_rows = xs * ROWS
     lanes = [pl.ds(0, 128), pl.ds(128, 128)]
+
+    count_load = pltpu.make_async_copy(count_in, count_ref, small_sem.at[7])
+    count_load.start()
+    pert_in, amp_in = [], []
+
+    def load_half(half):
+        at = pl.ds(pl.multiple_of((other_y, y)[half] * half_rows, 16), half_rows)
+        for k in range(members):
+            copy = pltpu.make_async_copy(
+                pert_ref.at[k, :, at, :], narrow.at[k, :, at, :], load_sem.at[half * members + k]
+            )
+            copy.start()
+            pert_in.append(copy)
+        for part in (0, 1):
+            column = lax.rem(across // 2 + part, 2)
+            start = (other_y, y)[half] * half_rows + column * PIECE
+            at = pl.ds(pl.multiple_of(start, PIECE), PIECE)
+            copy = pltpu.make_async_copy(
+                amp_ref.at[:, :, at, :],
+                amp_out.at[:, :, at, :],
+                load_sem.at[2 * members + 2 * half + part],
+            )
+            copy.start()
+            amp_in.append(copy)
+
+    load_half(0)
     plane_in = [
         [
             pltpu.make_async_copy(
@@ -258,37 +281,119 @@
                 (std_in, std_ref),
                 (col_index_in, col_index_ref),
                 (col_weight_in, col_weight_ref),
-                (count_in, count_ref),
             )
         )
     ]
     for copy in small_in + plane_in[0]:
         copy.start()
-    half_rows = xs * ROWS
-    pert_in, amp_in = [], []
-    for half, ry in enumerate((other_y, y)):
-        at = pl.ds(pl.multiple_of(ry * half_rows, 16), half_rows)
-        for k in range(members):
-            copy = pltpu.make_async_copy(
-                pert_ref.at[k, :, at, :], narrow.at[k, :, at, :], load_sem.at[half * members + k]
-            )
-            copy.start()
-            pert_in.append(copy)
-        for part in (0, 1):
-            column = lax.rem(across // 2 + part, 2)
-            at = pl.ds(pl.multiple_of(ry * half_rows + column * PIECE, PIECE), PIECE)
-            copy = pltpu.make_async_copy(
-                amp_ref.at[:, :, at, :],
-                amp_out.at[:, :, at, :],
-                load_sem.at[2 * members + 2 * half + part],
-            )
-            copy.start()
-            amp_in.append(copy)
+    load_half(1)
     for copy in plane_in[1]:
         copy.start()
 
     def planes(ref, number, side):
         return ref.at[number, side].reshape(lev_dev * own, 128)
+
+    def widen(half):
+        at = pl.ds(pl.multiple_of((other_y, y)[half] * half_rows, 16), half_rows)
+        for k in range(members):
+            pert_in[half * members + k].wait()
+
+            def widen_level(level, carry):
+                wide[k, level, at] = narrow[k, level, at].astype(F32)
+                return carry
+
+            lax.fori_loop(0, levels, widen_level, 0, unroll=8)
+
+    def x_rows(ry, rx):
+        return pl.ds(share(ry, rx), XROWS)
+
+    def y_rows(ry, rx):
+        return pl.ds(share(ry, rx) + XROWS, YROWS)
+
+    def add(rows, *terms):
+        total = sums[rows]
+        for term in terms:
+            total = total + term[...]
+        sums[rows] = total
+
+    amps = amp_out.reshape(members * modes * PITCH, 128)
+    perts = wide.reshape(members * levels * PITCH, 128)
+    lhs = lhs_ref[...]
+    mode = lax.broadcasted_iota(jnp.int32, (modes, 128), 0)
+
+    def contract(start):
+        def row_pair(step, carry):
+            first = start + step * 2
+            keep = [mode < count_ref[pl.ds(first + h, 1), :] for h in range(2)]
+            total = [jnp.zeros((levels, 128), F32) for _ in range(2)]
+            for k in range(members):
+                rhs = []
+                for h in range(2):
+                    amp = amps[pl.ds(k * modes * PITCH + first + h, modes, stride=PITCH), :]
+                    rhs.append(stacked(jnp.where(keep[h], amp, 0.0)))
+                level_amp = jnp.dot(lhs, jnp.concatenate(rhs, axis=1), preferred_element_type=F32)
+                for h in range(2):
+                    pert = perts[pl.ds(k * levels * PITCH + first + h, levels, stride=PITCH), :]
+                    total[h] = total[h] + pert * level_amp[:, h * 128 : (h + 1) * 128]
+            for h in range(2):
+                tile[0, first + h] = total[h][: levels // 2]
+                tile[1, first + h] = total[h][levels // 2 :]
+            return carry
+
+        lax.fori_loop(0, ROWS // 2, row_pair, 0, unroll=3)
+
+    order = [(ry, rx) for ry in (other_y, y) for rx in (across, right, left, x)]
+    ring = ((across, to_across), (right, to_right), (left, to_left))
+    origins = (across, left, right)
+    core_sends = []
+    to_ring = [[], []]
+    to_pair = []
+    to_own = []
+
+    def produce(number):
+        contract(share(*order[number]))
+
+    def send_core(number):
+        rows = pl.ds(share(*order[number]), ROWS)
+        core_sends.append(remote(tile.at[1 - lev, rows], core_in.at[rows], to_core))
+
+    def settle(number):
+        core_sends[number].wait_recv()
+        rows = pl.ds(share(*order[number]), ROWS)
+        add(rows, core_in.at[rows])
+        half, place = number // 4, number % 4
+        if place < 3:
+            rx, device = ring[place]
+            to_ring[half].append(
+                remote(sums.at[x_rows(*order[number])], x_in.at[half, place], device)
+            )
+        if half == 0:
+            rx = order[number][1]
+            to_pair.append(remote(sums.at[y_rows(other_y, rx)], pair_y_in.at[place], to_y))
+
+    def settle_pair(place):
+        to_pair[place].wait_recv()
+        rx = order[place][1]
+        add(y_rows(y, rx), pair_y_in.at[place])
+        if place < 3:
+            to_own.append(remote(sums.at[y_rows(y, rx)], y_in.at[place], ring[place][1]))
+
+    count_load.wait()
+    widen(0)
+    amp_in[0].wait()
+    produce(0)
+    pl.semaphore_wait(barrier, 7)
+    send_core(0)
+    amp_in[1].wait()
+    produce(1)
+    send_core(1)
+    produce(2)
+    send_core(2)
+    settle(0)
+    produce(3)
+    send_core(3)
+    settle(1)
+    settle(2)
 
     for copy in small_in + plane_in[0]:
         copy.wait()
@@ -310,6 +415,36 @@
         return carry
 
     lax.fori_loop(0, own, load_rows, 0, unroll=4)
+    top, bottom = pl.ds(EDGE, HALO), pl.ds(EDGE + own - HALO, HALO)
+    low, high = pl.ds(EDGE - HALO, HALO), pl.ds(EDGE + own, HALO)
+    halo_sends = [
+        remote(ref.at[src], ref.at[dst], device)
+        for ref in (cells, field_a)
+        for src, dst, device in ((top, high, to_before), (bottom, low, to_after))
+    ]
+    settle(3)
+
+    widen(1)
+    amp_in[2].wait()
+    produce(4)
+    send_core(4)
+    amp_in[3].wait()
+    produce(5)
+    send_core(5)
+    settle(4)
+    settle_pair(0)
+    produce(6)
+    send_core(6)
+    settle(5)
+    produce(7)
+    send_core(7)
+    settle(6)
+    settle_pair(1)
+    for copy in to_ring[0]:
+        copy.wait_recv()
+    add(x_rows(other_y, x), x_in.at[0, 0], x_in.at[0, 1], x_in.at[0, 2])
+    pair_x = remote(sums.at[x_rows(other_y, x)], pair_x_in, to_y)
+
     for ref in (cells, misfit):
         ref[0] = jnp.zeros(ref.shape[1:], F32)
         ref[GROWN - 1] = jnp.zeros(ref.shape[1:], F32)
@@ -317,47 +452,6 @@
         field_b[row] = jnp.zeros(field_b.shape[1:], F32)
     for lev_at in range(lev_dev):
         sigma[lev_at : lev_at + 1, :] = jnp.full((1, 256), std_ref[lev_at], F32)
-
-    pl.semaphore_wait(barrier, 6)
-
-    top, bottom = pl.ds(EDGE, HALO), pl.ds(EDGE + own - HALO, HALO)
-    low, high = pl.ds(EDGE - HALO, HALO), pl.ds(EDGE + own, HALO)
-    halo_sends = [
-        remote(ref.at[src], ref.at[dst], device)
-        for ref in (cells, field_a)
-        for src, dst, device in ((top, high, to_before), (bottom, low, to_after))
-    ]
-
-    def x_rows(ry, rx):
-        return pl.ds(share(ry, rx), XROWS)
-
-    def y_rows(rx, part, ry=None):
-        start = share(y if ry is None else ry, rx) + XROWS
-        return {
-            "all": pl.ds(start, YROWS),
-            "a": pl.ds(start, YA),
-            "b": pl.ds(start + YA, YROWS - YA),
-        }[part]
-
-    def add(rows, *terms):
-        total = sums[rows]
-        for term in terms:
-            total = total + term[...]
-        sums[rows] = total
-
-    def widen(half):
-        at = pl.ds(pl.multiple_of((other_y, y)[half] * half_rows, 16), half_rows)
-        for k in range(members):
-            pert_in[half * members + k].wait()
-
-            def widen_level(level, carry):
-                wide[k, level, at] = narrow[k, level, at].astype(F32)
-                return carry
-
-            lax.fori_loop(0, levels, widen_level, 0, unroll=8)
-
-    widen(0)
-
     for copy in halo_sends[:2]:
         copy.wait_recv()
 
@@ -396,111 +490,13 @@
     hi, lo = halves(matrix)
     col_mat[0], col_mat[1] = hi, lo
 
-    amps = amp_out.reshape(members * modes * PITCH, 128)
-    perts = wide.reshape(members * levels * PITCH, 128)
-    lhs = lhs_ref[...]
-    mode = lax.broadcasted_iota(jnp.int32, (modes, 128), 0)
-
-    def contract(start):
-        def row_pair(step, carry):
-            first = start + step * 2
-            keep = [mode < count_ref[pl.ds(first + h, 1), :] for h in range(2)]
-            total = [jnp.zeros((levels, 128), F32) for _ in range(2)]
-            for k in range(members):
-                rhs = []
-                for h in range(2):
-                    amp = amps[pl.ds(k * modes * PITCH + first + h, modes, stride=PITCH), :]
-                    rhs.append(stacked(jnp.where(keep[h], amp, 0.0)))
-                level_amp = jnp.dot(lhs, jnp.concatenate(rhs, axis=1), preferred_element_type=F32)
-                for h in range(2):
-                    pert = perts[pl.ds(k * levels * PITCH + first + h, levels, stride=PITCH), :]
-                    total[h] = total[h] + pert * level_amp[:, h * 128 : (h + 1) * 128]
-            for h in range(2):
-                tile[0, first + h] = total[h][: levels // 2]
-                tile[1, first + h] = total[h][levels // 2 :]
-            return carry
-
-        lax.fori_loop(0, ROWS // 2, row_pair, 0, unroll=3)
-
-    order = [
-        (other_y, across),
-        (other_y, right),
-        (other_y, left),
-        (other_y, x),
-        (y, across),
-        (y, left),
-        (y, right),
-        (y, x),
-    ]
-    core_sends = []
-
-    def produce(number):
-        start = share(*order[number])
-        contract(start)
-        rows = pl.ds(start, ROWS)
-        core_sends.append(remote(tile.at[1 - lev, rows], core_in.at[rows], to_core))
-
-    def settle(number):
-        core_sends[number].wait_recv()
-        rows = pl.ds(share(*order[number]), ROWS)
-        add(rows, core_in.at[rows])
-
-    def pass_y(rx, number):
-        return remote(sums.at[y_rows(rx, "all", other_y)], yq_in.at[number], to_y)
-
-    amp_in[0].wait()
-    produce(0)
-    amp_in[1].wait()
-    produce(1)
-    produce(2)
-    produce(3)
-    settle(0)
-    x1_right = remote(sums.at[x_rows(other_y, across)], x1_in.at[0], to_right)
-    q_across = pass_y(across, 0)
-    widen(1)
-    settle(1)
-    q_right = pass_y(right, 1)
-    amp_in[2].wait()
-    produce(4)
-    settle(2)
-    x2_left = remote(sums.at[x_rows(other_y, left)], x2_in.at[1], to_left)
-    q_left = pass_y(left, 2)
-    amp_in[3].wait()
-    produce(5)
-    settle(3)
-    q_own = pass_y(x, 3)
-    settle(4)
-    x1_left = remote(sums.at[x_rows(y, across)], x1_in.at[1], to_left)
-    produce(6)
-    x1_right.wait_recv()
-    add(x_rows(other_y, right), x1_in.at[0])
-    x3_right = remote(sums.at[x_rows(other_y, right)], x3_in.at[0], to_right)
-    q_across.wait_recv()
-    add(y_rows(across, "all"), yq_in.at[0])
-    y1_right = remote(sums.at[y_rows(across, "a")], y1_in.at[0, pl.ds(0, YA)], to_right)
-    y1_left = remote(sums.at[y_rows(across, "b")], y1_in.at[1], to_left)
-    settle(5)
-    produce(7)
-    settle(6)
-    x2_right = remote(sums.at[x_rows(y, right)], x2_in.at[0], to_right)
-    q_right.wait_recv()
-    add(y_rows(right, "all"), yq_in.at[1])
-    y2_right = remote(sums.at[y_rows(right, "b")], y2_in.at[0], to_right)
-    q_left.wait_recv()
-    add(y_rows(left, "all"), yq_in.at[2])
-    y2_left = remote(sums.at[y_rows(left, "a")], y2_in.at[1, pl.ds(0, YA)], to_left)
-    x1_left.wait_recv()
-    add(x_rows(y, left), x1_in.at[1])
-    x3_left = remote(sums.at[x_rows(y, left)], x3_in.at[1], to_left)
-    settle(7)
-
     def sweep(src, dst, first=0, last=7):
         def rows_of_four(step, carry):
             e = EDGE - 2 + 4 * step
             down = row_faces[pl.ds(e - 1, 5)]
             side = col_faces[pl.ds(e, 4)]
-            for tile in range(lev_dev // 8):
-                at = pl.ds(8 * tile, 8)
+            for tile_at in range(lev_dev // 8):
+                at = pl.ds(8 * tile_at, 8)
                 v = src[pl.ds(e - 1, 6), at, :]
                 mid = v[1:5]
                 flux = down * (v[1:] - v[:-1])
@@ -512,27 +508,29 @@
 
         lax.fori_loop(first, last, rows_of_four, 0)
 
+    settle_pair(2)
+    settle(7)
     for copy in halo_sends[2:]:
         copy.wait_recv()
         copy.wait_send()
     sweep(field_a, field_b)
-
-    y1_right.wait_recv()
-    y1_left.wait_recv()
-    a_rows, b_rows = y_rows(right, "a"), y_rows(left, "b")
-    add(a_rows, y1_in.at[0, pl.ds(0, YA)])
-    y3_right = remote(sums.at[a_rows], y3_in.at[0, pl.ds(0, YA)], to_right)
-    add(b_rows, y1_in.at[1])
-    y3_left = remote(sums.at[b_rows], y3_in.at[1], to_left)
-
-    x3_right.wait_recv()
-    x2_left.wait_recv()
-    rows = x_rows(other_y, x)
-    add(rows, x3_in.at[0], x2_in.at[1])
-    x4 = remote(sums.at[rows], x4_in, to_y)
-
     sweep(field_b, field_a)
+    settle_pair(3)
+    for copy in to_ring[1]:
+        copy.wait_recv()
+    add(x_rows(y, x), x_in.at[1, 0], x_in.at[1, 1], x_in.at[1, 2])
     sweep(field_a, field_b)
+
+    for copy in to_own:
+        copy.wait_recv()
+    mine = share(y, x)
+    window[pl.ds(HALO + XROWS, YROWS)] = sums[y_rows(y, x)] + y_in[0] + (y_in[1] + y_in[2])
+    pair_x.wait_recv()
+    window[pl.ds(HALO, XROWS)] = sums[x_rows(y, x)] + pair_x_in[...]
+    halo_again = [
+        remote(window.at[pl.ds(ROWS, HALO)], window.at[pl.ds(0, HALO)], to_after),
+        remote(window.at[pl.ds(HALO, HALO)], window.at[pl.ds(HALO + ROWS, HALO)], to_before),
+    ]
 
     def static_part(i, carry):
         for side in range(2):
@@ -545,37 +543,11 @@
 
     for copy in plane_in[1]:
         copy.wait()
-
     lax.fori_loop(0, own, static_part, 0, unroll=4)
-    misfit_sends = [
+    halo_again += [
         remote(misfit.at[top], misfit.at[high], to_before),
         remote(misfit.at[bottom], misfit.at[low], to_after),
     ]
-
-    x3_left.wait_recv()
-    x2_right.wait_recv()
-    add(x_rows(y, x), x3_in.at[1], x2_in.at[0])
-    q_own.wait_recv()
-    add(y_rows(x, "all"), yq_in.at[3])
-    for copy in (y2_right, y2_left, y3_right, y3_left):
-        copy.wait_recv()
-    mine = share(y, x)
-    window[pl.ds(HALO + XROWS, YA)] = (
-        sums[y_rows(x, "a")] + y3_in[0, :YA] + y2_in[1, :YA]
-    )
-    window[pl.ds(HALO + XROWS + YA, YROWS - YA)] = sums[y_rows(x, "b")] + y3_in[1] + y2_in[0]
-    window_after = remote(
-        window.at[pl.ds(ROWS, HALO)], window.at[pl.ds(0, HALO)], to_after
-    )
-    x4.wait_recv()
-    window[pl.ds(HALO, XROWS)] = sums[pl.ds(mine, XROWS)] + x4_in[...]
-    window_before = remote(
-        window.at[pl.ds(HALO, HALO)], window.at[pl.ds(HALO + ROWS, HALO)], to_before
-    )
-    for copy in misfit_sends + [window_after, window_before]:
-        copy.wait_recv()
-    for copy in misfit_sends:
-        copy.wait_send()
 
     def dot_split(lhs, which):
         hi, lo = halves(lhs)
@@ -604,7 +576,13 @@
         back[at] = dot_split(total.reshape(span * lev_dev, 256), 1).reshape(span, lev_dev, 128)
         return carry
 
-    lax.fori_loop(0, GROWN // span, interpolate, 0)
+    lax.fori_loop(1, 3, interpolate, 0)
+    for copy in halo_again:
+        copy.wait_recv()
+    for copy in halo_again[2:]:
+        copy.wait_send()
+    interpolate(0, 0)
+    interpolate(3, 0)
 
     def adjoint(r, carry):
         e = 2 * r + 2
@@ -619,47 +597,32 @@
     def to_all(rows, device):
         return remote(shares.at[lev, rows], shares.at[lev, rows], device)
 
-    def x_part(ry, rx):
-        return pl.ds(share(ry, rx), XROWS)
-
-    pair_first = to_all(x_part(y, x), to_y)
-    ring_y = [to_all(y_rows(x, "all"), to_right), to_all(y_rows(x, "all"), to_left)]
-    ring_own = [to_all(x_part(y, x), to_right), to_all(x_part(y, x), to_left)]
+    def to_ring_of(rows):
+        return [to_all(rows, device) for _, device in ring]
+
+    pair_first = to_all(x_rows(y, x), to_y)
+    ring_y = to_ring_of(y_rows(y, x))
+    pair_y = [to_all(y_rows(y, x), to_y)]
+    ring_own = to_ring_of(x_rows(y, x))
     core = [to_all(pl.ds(mine, ROWS), to_core)]
-    pair_y = [to_all(y_rows(x, "all"), to_y)]
 
     sweep(field_a, field_b)
     sweep(field_b, field_a, 0, 3)
     pair_first.wait_recv()
-    ring_other = [to_all(x_part(other_y, x), to_right), to_all(x_part(other_y, x), to_left)]
-    core.append(to_all(x_part(other_y, x), to_core))
-    for copy in ring_y:
-        copy.wait_recv()
-    on_y = [
-        to_all(y_rows(left, "a"), to_right),
-        to_all(y_rows(right, "b"), to_left),
-    ]
-    for rx in (left, right):
-        pair_y.append(to_all(y_rows(rx, "all"), to_y))
-        core.append(to_all(y_rows(rx, "all"), to_core))
-
+    ring_other = to_ring_of(x_rows(other_y, x))
+    core.append(to_all(x_rows(other_y, x), to_core))
+    for copy, rx in zip(ring_y, origins):
+        copy.wait_recv()
+        pair_y.append(to_all(y_rows(y, rx), to_y))
+        core.append(to_all(y_rows(y, rx), to_core))
     sweep(field_b, field_a, 3, 7)
-    for copy in ring_own:
-        copy.wait_recv()
-    on_x = [to_all(x_part(y, right), to_left)]
-    for rx in (left, right):
-        core.append(to_all(x_part(y, rx), to_core))
     sweep(field_a, field_b, 0, 3)
-    for copy in on_y:
-        copy.wait_recv()
-    pair_y.append(to_all(y_rows(across, "all"), to_y))
-    core.append(to_all(y_rows(across, "all"), to_core))
+    for copy, rx in zip(ring_own, origins):
+        copy.wait_recv()
+        core.append(to_all(x_rows(y, rx), to_core))
+    pair_y[0].wait_recv()
+    core.append(to_all(y_rows(other_y, x), to_core))
     sweep(field_a, field_b, 3, 7)
-    for copy in ring_other:
-        copy.wait_recv()
-    on_x.append(to_all(x_part(other_y, left), to_right))
-    for rx in (left, right):
-        core.append(to_all(x_part(other_y, rx), to_core))
 
     def finish(i, carry):
         at = pl.ds(i, lev_dev, stride=own)
@@ -671,18 +634,15 @@
         return carry
 
     lax.fori_loop(0, own, finish, 0, unroll=4)
-    for rx, copy in zip((x, left, right), pair_y):
-        copy.wait_recv()
-        core.append(to_all(y_rows(rx, "all", other_y), to_core))
-    on_x[0].wait_recv()
-    core.append(to_all(x_part(y, across), to_core))
-    pair_y[3].wait_recv()
-    core.append(to_all(y_rows(across, "all", other_y), to_core))
-    on_x[1].wait_recv()
-    core.append(to_all(x_part(other_y, across), to_core))
+    for copy, rx in zip(pair_y[1:], origins):
+        copy.wait_recv()
+        core.append(to_all(y_rows(other_y, rx), to_core))
+    for copy, rx in zip(ring_other, origins):
+        copy.wait_recv()
+        core.append(to_all(x_rows(other_y, rx), to_core))
     for copy in core:
         copy.wait_recv()
-    waited = halo_sends[2:] + misfit_sends
+    waited = halo_sends[2:] + halo_again[2:]
     for copy in sent:
         if not any(copy is done for done in waited):
             copy.wait_send()
@@ -712,14 +672,10 @@
             pltpu.VMEM(tile, F32),
             pltpu.VMEM(pert.shape, BF16),
             pltpu.VMEM((rows,) + cell, F32),
-            pltpu.VMEM((2, XROWS) + cell, F32),
-            pltpu.VMEM((2, XROWS) + cell, F32),
-            pltpu.VMEM((2, XROWS) + cell, F32),
+            pltpu.VMEM((2, 3, XROWS) + cell, F32),
             pltpu.VMEM((XROWS,) + cell, F32),
             pltpu.VMEM((4, YROWS) + cell, F32),
-            pltpu.VMEM((2, YROWS - YA) + cell, F32),
-            pltpu.VMEM((2, YROWS - YA) + cell, F32),
-            pltpu.VMEM((2, YROWS - YA) + cell, F32),
+            pltpu.VMEM((3, YROWS) + cell, F32),
             pltpu.VMEM((ROWS + 2 * HALO,) + cell, F32),
             pltpu.VMEM((GROWN,) + row, F32),
             pltpu.VMEM((GROWN,) + row, F32),

time: 62.1 us -> 55.7 us (0.90)
  Pallas kernels: 60.4 us -> 54 us
    pallas_call x1, Pallas kernels: 53.1 us -> 46.7 us  [exchange(): pl.pallas_call(functools.partial(exchange_kernel, sizes), in_specs=[vmem]...]
where the time goes in v4:
time: 55.7 us; the launch traced here: 55.6 us
  Pallas kernels  54 us (97%)
  other arithmetic  0.82 us (1%)
  between operations  0.65 us (1%)
    pallas_call x1, Pallas kernels, exchange(): pl.pallas_call(functools.partial(exchange_kernel, sizes), in_specs=[vmem]...  46.7 us
    pallas_call x1, Pallas kernels, backward(): pl.pallas_call(backward_kernel, in_specs=[vmem] * 6, out_specs=[anywhere]...  7.37 us

profile of v4, /device:TPU:1, one launch (start us, length us, event | category | flops | bytes accessed | tf_op | source)
XLA Modules:
  0.0 55.6 jit_solution(15963350129678482447)
XLA Ops:
  0.6 0.7 %fusion = (bf16[32,48]{1,0:T(8,128)(2,1)S(1)}, bf16[32,48]{1,0:T(8,128)(2,1)S(1)}) fusion(f32[48,32]{0,1:T(8,128)} %param.15), kind=kLoop, calls=%fused_computation.3 | loop fusion | flops 7680 | bytes 12288 | tf_op jit(solution)/shard_map/convert.4
  1.4 0.1 pad_maximum_fusion.lhs_ref
  1.5 0.1 copy.16.lhs_ref
  1.5 46.7 %exchange.1 = (f32[5,32,104,128]{3,2,1,0:T(8,128)S(1)}, f32[5,48,104,128]{3,2,1,0:T(8,128)S(1)}, f32[2,96,24,128]{3,2,1,0:T(8,128)S(1)}, f32[2,2,24,24,128]{4,3,2,1,0:T(8,128)S(1)}, s32[96,128]{1,0:T(8,128)S(1)}) custom-call(bf16[48,96]{1,0:T(8,128)(2,1)S(1)} %copy.16.lhs_ref, s32[96,128]{1,0:T(8,128)} %count_in.1, f32[5,32,96,128]{3,2,1,0:T(8,128)} %amp_ref.1, ...), custom_call_target="tpu_custom_call" | custom-call | tf_op jit(solution)/shard_map/exchange/pallas_call | solution.py:660
  48.2 7.4 %backward_modes.1 = (f32[5,32,96,128]{3,2,1,0:T(8,128)}, f32[24,24,256]{2,1,0:T(8,128)}, f32[24,24,256]{2,1,0:T(8,128)}) custom-call(bf16[32,144]{1,0:T(8,128)(2,1)S(1)} %pad_maximum_fusion.lhs_ref, s32[96,128]{1,0:T(8,128)S(1)} %get-tuple-element.11.count_ref, f32[5,32,104,128]{3,2,1,0:T(8,128)S(1)} %get-tuple-element.12.amp_ref, ...), custom_call_target="tpu_custom_call" | custom-call | tf_op jit(solution)/shard_map/backward_modes/pallas_call | solution.py:116
  (1 shorter events, 0.0 us)

commit v5 on v4

--- a/solution.py
+++ b/solution.py
@@ -162,6 +162,7 @@
     cells,
     row_faces,
     col_faces,
+    centre,
     weights,
     sigma,
     col_mat,
@@ -344,7 +345,7 @@
 
     order = [(ry, rx) for ry in (other_y, y) for rx in (across, right, left, x)]
     ring = ((across, to_across), (right, to_right), (left, to_left))
-    origins = (across, left, right)
+    origins = (left, right, across)
     core_sends = []
     to_ring = [[], []]
     to_pair = []
@@ -414,7 +415,7 @@
         )
         return carry
 
-    lax.fori_loop(0, own, load_rows, 0, unroll=4)
+    lax.fori_loop(0, own, load_rows, 0, unroll=8)
     top, bottom = pl.ds(EDGE, HALO), pl.ds(EDGE + own - HALO, HALO)
     low, high = pl.ds(EDGE - HALO, HALO), pl.ds(EDGE + own, HALO)
     halo_sends = [
@@ -465,15 +466,20 @@
         lane = lax.broadcasted_iota(jnp.int32, (8, 256), 1)
         spread, land = (jnp.broadcast_to(here[j : j + 1], (8, 256)) for j in (0, 1))
         spread_next, land_next = (jnp.broadcast_to(there[j : j + 1], (8, 256)) for j in (0, 1))
-        row_faces[e] = (
+        row_face = (
             jnp.sqrt(spread * spread_next) * (1.0 - 0.5 * jnp.abs(land - land_next)) * facing
         )
+        row_faces[e] = row_face
         spread_right, land_right = (pltpu.roll(v, 255, 1) for v in (spread, land))
-        col_faces[e] = jnp.where(
+        col_face = jnp.where(
             lane < 255,
             jnp.sqrt(spread * spread_right) * (1.0 - 0.5 * jnp.abs(land - land_right)),
             0.0,
         )
+        col_before = pltpu.roll(col_face, 1, 1)
+        col_faces[0, e] = col_face
+        col_faces[1, e] = col_before
+        centre[e] = 1.0 - (row_face + col_face + col_before)
         weight, upper = (jnp.broadcast_to(here[j : j + 1, :128], (8, 128)) for j in (2, 3))
         upper_on = upper > 0.5
         weights[0, e] = jnp.where(upper_on, 0.0, 1.0 - weight) * inside
@@ -482,6 +488,8 @@
         return carry
 
     lax.fori_loop(0, GROWN - 1, coefficients, 0, unroll=4)
+    inner = pl.ds(1, GROWN - 2)
+    centre[inner] = centre[inner] - row_faces[pl.ds(0, GROWN - 2)]
     for j in range(3):
         weights[j, GROWN - 1] = jnp.zeros((8, 128), F32)
     col = lax.broadcasted_iota(jnp.int32, (128, 256), 0)
@@ -493,16 +501,19 @@
     def sweep(src, dst, first=0, last=7):
         def rows_of_four(step, carry):
             e = EDGE - 2 + 4 * step
+            at_four = pl.ds(e, 4)
             down = row_faces[pl.ds(e - 1, 5)]
-            side = col_faces[pl.ds(e, 4)]
+            to_right_face, to_left_face = col_faces[0, at_four], col_faces[1, at_four]
+            keep = centre[at_four]
             for tile_at in range(lev_dev // 8):
                 at = pl.ds(8 * tile_at, 8)
                 v = src[pl.ds(e - 1, 6), at, :]
                 mid = v[1:5]
-                flux = down * (v[1:] - v[:-1])
-                cross = side * (pltpu.roll(mid, 255, 2) - mid)
-                dst[pl.ds(e, 4), at, :] = (
-                    mid + (flux[1:] - flux[:-1]) + (cross - pltpu.roll(cross, 1, 2))
+                dst[at_four, at, :] = (
+                    keep * mid
+                    + (down[1:] * v[2:] + down[:-1] * v[:-2])
+                    + to_right_face * pltpu.roll(mid, 255, 2)
+                    + to_left_face * pltpu.roll(mid, 1, 2)
                 )
             return carry
 
@@ -520,17 +531,6 @@
         copy.wait_recv()
     add(x_rows(y, x), x_in.at[1, 0], x_in.at[1, 1], x_in.at[1, 2])
     sweep(field_a, field_b)
-
-    for copy in to_own:
-        copy.wait_recv()
-    mine = share(y, x)
-    window[pl.ds(HALO + XROWS, YROWS)] = sums[y_rows(y, x)] + y_in[0] + (y_in[1] + y_in[2])
-    pair_x.wait_recv()
-    window[pl.ds(HALO, XROWS)] = sums[x_rows(y, x)] + pair_x_in[...]
-    halo_again = [
-        remote(window.at[pl.ds(ROWS, HALO)], window.at[pl.ds(0, HALO)], to_after),
-        remote(window.at[pl.ds(HALO, HALO)], window.at[pl.ds(HALO + ROWS, HALO)], to_before),
-    ]
 
     def static_part(i, carry):
         for side in range(2):
@@ -543,10 +543,21 @@
 
     for copy in plane_in[1]:
         copy.wait()
-    lax.fori_loop(0, own, static_part, 0, unroll=4)
-    halo_again += [
+    lax.fori_loop(0, own, static_part, 0, unroll=8)
+    halo_again = [
         remote(misfit.at[top], misfit.at[high], to_before),
         remote(misfit.at[bottom], misfit.at[low], to_after),
+    ]
+
+    for copy in to_own:
+        copy.wait_recv()
+    mine = share(y, x)
+    window[pl.ds(HALO + XROWS, YROWS)] = sums[y_rows(y, x)] + y_in[0] + (y_in[1] + y_in[2])
+    pair_x.wait_recv()
+    window[pl.ds(HALO, XROWS)] = sums[x_rows(y, x)] + pair_x_in[...]
+    halo_again += [
+        remote(window.at[pl.ds(ROWS, HALO)], window.at[pl.ds(0, HALO)], to_after),
+        remote(window.at[pl.ds(HALO, HALO)], window.at[pl.ds(HALO + ROWS, HALO)], to_before),
     ]
 
     def dot_split(lhs, which):
@@ -576,10 +587,10 @@
         back[at] = dot_split(total.reshape(span * lev_dev, 256), 1).reshape(span, lev_dev, 128)
         return carry
 
-    lax.fori_loop(1, 3, interpolate, 0)
+    lax.fori_loop(1, 3, interpolate, 0, unroll=2)
     for copy in halo_again:
         copy.wait_recv()
-    for copy in halo_again[2:]:
+    for copy in halo_again[:2]:
         copy.wait_send()
     interpolate(0, 0)
     interpolate(3, 0)
@@ -592,13 +603,13 @@
         shares[lev, mine + r] = total.reshape(lev_dev, 128)
         return carry
 
-    lax.fori_loop(0, ROWS, adjoint, 0, unroll=4)
+    lax.fori_loop(0, ROWS, adjoint, 0, unroll=12)
 
     def to_all(rows, device):
         return remote(shares.at[lev, rows], shares.at[lev, rows], device)
 
     def to_ring_of(rows):
-        return [to_all(rows, device) for _, device in ring]
+        return [to_all(rows, device) for device in (to_right, to_left, to_across)]
 
     pair_first = to_all(x_rows(y, x), to_y)
     ring_y = to_ring_of(y_rows(y, x))
@@ -633,7 +644,7 @@
                 )
         return carry
 
-    lax.fori_loop(0, own, finish, 0, unroll=4)
+    lax.fori_loop(0, own, finish, 0, unroll=8)
     for copy, rx in zip(pair_y[1:], origins):
         copy.wait_recv()
         core.append(to_all(y_rows(other_y, rx), to_core))
@@ -642,7 +653,7 @@
         core.append(to_all(x_rows(other_y, rx), to_core))
     for copy in core:
         copy.wait_recv()
-    waited = halo_sends[2:] + halo_again[2:]
+    waited = halo_sends[2:] + halo_again[:2]
     for copy in sent:
         if not any(copy is done for done in waited):
             copy.wait_send()
@@ -682,6 +693,7 @@
             pltpu.VMEM((GROWN,) + row, F32),
             pltpu.VMEM((GROWN, 8, cols_fine), F32),
             pltpu.VMEM((GROWN, 8, cols_fine), F32),
+            pltpu.VMEM((2, GROWN, 8, cols_fine), F32),
             pltpu.VMEM((GROWN, 8, cols_fine), F32),
             pltpu.VMEM((3, GROWN, 8, 128), F32),
             pltpu.VMEM(row, F32),

time: 55.7 us -> 54.8 us (0.984)
  Pallas kernels: 54 us -> 53.1 us
    pallas_call x1, Pallas kernels: 46.7 us -> 45.8 us  [exchange(): pl.pallas_call(functools.partial(exchange_kernel, sizes), in_specs=[vmem]...]
where the time goes in v5:
time: 54.8 us; the launch traced here: 54.7 us
  Pallas kernels  53.1 us (97%)
  other arithmetic  0.82 us (1%)
  between operations  0.65 us (1%)
    pallas_call x1, Pallas kernels, exchange(): pl.pallas_call(functools.partial(exchange_kernel, sizes), in_specs=[vmem]...  45.8 us
    pallas_call x1, Pallas kernels, backward(): pl.pallas_call(backward_kernel, in_specs=[vmem] * 6, out_specs=[anywhere]...  7.37 us

profile of v5, /device:TPU:1, one launch (start us, length us, event | category | flops | bytes accessed | tf_op | source)
XLA Modules:
  0.0 54.7 jit_solution(7423046522728279648)
XLA Ops:
  0.6 0.7 %fusion = (bf16[32,48]{1,0:T(8,128)(2,1)S(1)}, bf16[32,48]{1,0:T(8,128)(2,1)S(1)}) fusion(f32[48,32]{0,1:T(8,128)} %param.15), kind=kLoop, calls=%fused_computation.3 | loop fusion | flops 7680 | bytes 12288 | tf_op jit(solution)/shard_map/convert.4
  1.4 0.1 pad_maximum_fusion.lhs_ref
  1.5 0.1 copy.16.lhs_ref
  1.5 45.8 %exchange.1 = (f32[5,32,104,128]{3,2,1,0:T(8,128)S(1)}, f32[5,48,104,128]{3,2,1,0:T(8,128)S(1)}, f32[2,96,24,128]{3,2,1,0:T(8,128)S(1)}, f32[2,2,24,24,128]{4,3,2,1,0:T(8,128)S(1)}, s32[96,128]{1,0:T(8,128)S(1)}) custom-call(bf16[48,96]{1,0:T(8,128)(2,1)S(1)} %copy.16.lhs_ref, s32[96,128]{1,0:T(8,128)} %count_in.1, f32[5,32,96,128]{3,2,1,0:T(8,128)} %amp_ref.1, ...), custom_call_target="tpu_custom_call" | custom-call | tf_op jit(solution)/shard_map/exchange/pallas_call | solution.py:671
  47.3 7.4 %backward_modes.1 = (f32[5,32,96,128]{3,2,1,0:T(8,128)}, f32[24,24,256]{2,1,0:T(8,128)}, f32[24,24,256]{2,1,0:T(8,128)}) custom-call(bf16[32,144]{1,0:T(8,128)(2,1)S(1)} %pad_maximum_fusion.lhs_ref, s32[96,128]{1,0:T(8,128)S(1)} %get-tuple-element.11.count_ref, f32[5,32,104,128]{3,2,1,0:T(8,128)S(1)} %get-tuple-element.12.amp_ref, ...), custom_call_target="tpu_custom_call" | custom-call | tf_op jit(solution)/shard_map/backward_modes/pallas_call | solution.py:116
  (1 shorter events, 0.0 us)

commit v6 on v5

--- a/solution.py
+++ b/solution.py
@@ -17,6 +17,7 @@
 XROWS = 5
 YROWS = ROWS - XROWS
 PITCH = 104
+HALF_PITCH = 56
 PIECE = 24
 F32 = jnp.float32
 BF16 = jnp.bfloat16
@@ -32,12 +33,23 @@
     return jnp.concatenate([hi, hi, lo], axis=0)
 
 
-def split_modes(matrix):
-    hi = lax.reduce_precision(matrix, 8, 7)
-    lo = matrix - hi
-    wide = jnp.concatenate([hi, lo, hi], axis=1).astype(BF16)
-    tall = jnp.concatenate([hi, lo, hi], axis=0).astype(BF16)
-    return tall.T, wide
+def project_row_pair(lhs, keep_from, amps, perts, outs, grad_ref, sizes, first, out_first):
+    members, modes, levels = sizes
+    mode = lax.broadcasted_iota(jnp.int32, (modes, 128), 0)
+    keep = [mode < keep_from[pl.ds(first + h, 1), :] for h in range(2)]
+    grad = [
+        jnp.concatenate([grad_ref[0, first + h], grad_ref[1, first + h]], axis=0) for h in range(2)
+    ]
+    for k in range(members):
+        rhs = []
+        for h in range(2):
+            pert = perts[pl.ds(k * levels * PITCH + first + h, levels, stride=PITCH), :]
+            rhs.append(stacked(pert * grad[h]))
+        proj = jnp.dot(lhs, jnp.concatenate(rhs, axis=1), preferred_element_type=F32)
+        for h in range(2):
+            amp = amps[pl.ds(k * modes * PITCH + first + h, modes, stride=PITCH), :]
+            at = pl.ds(k * modes * HALF_PITCH + out_first + h, modes, stride=HALF_PITCH)
+            outs[at, :] = amp + jnp.where(keep[h], proj[:, h * 128 : (h + 1) * 128], 0.0)
 
 
 def backward_kernel(
@@ -47,6 +59,7 @@
     wide_ref,
     grad_ref,
     planes_ref,
+    done_ref,
     out_ref,
     grad_static_ref,
     inc_ref,
@@ -56,8 +69,15 @@
 ):
     members, modes = amp_ref.shape[:2]
     levels = wide_ref.shape[1]
-    rows = out_ref.shape[2]
-    plane_out = [
+    half_rows = out_ref.shape[2] // 2
+    y = lax.axis_index("fine") // (lax.axis_size("fine") // 2)
+    at = pl.ds(pl.multiple_of(y * half_rows, 8), half_rows)
+    copies = [
+        pltpu.make_async_copy(
+            done_ref.at[:, :, pl.ds(0, half_rows), :], out_ref.at[:, :, at, :], out_sem.at[0]
+        )
+    ]
+    copies += [
         pltpu.make_async_copy(
             planes_ref.at[number, side],
             ref.at[:, :, pl.ds(128 * side, 128)],
@@ -66,48 +86,35 @@
         for number, ref in enumerate((grad_static_ref, inc_ref))
         for side in range(2)
     ]
-    for copy in plane_out:
+    for copy in copies:
         copy.start()
     amps = amp_ref.reshape(members * modes * PITCH, 128)
     perts = wide_ref.reshape(members * levels * PITCH, 128)
-    outs = result.reshape(members * modes * PITCH, 128)
+    outs = result.reshape(members * modes * HALF_PITCH, 128)
     lhs = lhs_ref[...]
-    mode = lax.broadcasted_iota(jnp.int32, (modes, 128), 0)
-    pieces = []
-    for piece in range(rows // PIECE):
+    base = (1 - y) * half_rows
+    for piece in range(half_rows // PIECE):
 
         def row_pair(step, carry):
-            first = piece * PIECE + step * 2
-            keep = [mode < count_ref[pl.ds(first + h, 1), :] for h in range(2)]
-            grad = [
-                jnp.concatenate([grad_ref[0, first + h], grad_ref[1, first + h]], axis=0)
-                for h in range(2)
-            ]
-            for k in range(members):
-                rhs = []
-                for h in range(2):
-                    pert = perts[pl.ds(k * levels * PITCH + first + h, levels, stride=PITCH), :]
-                    rhs.append(stacked(pert * grad[h]))
-                proj = jnp.dot(lhs, jnp.concatenate(rhs, axis=1), preferred_element_type=F32)
-                for h in range(2):
-                    at = pl.ds(k * modes * PITCH + first + h, modes, stride=PITCH)
-                    outs[at, :] = amps[at, :] + jnp.where(
-                        keep[h], proj[:, h * 128 : (h + 1) * 128], 0.0
-                    )
+            row = piece * PIECE + step * 2
+            project_row_pair(
+                lhs, count_ref, amps, perts, outs, grad_ref, (members, modes, levels), base + row, row
+            )
             return carry
 
         lax.fori_loop(0, PIECE // 2, row_pair, 0, unroll=4)
-        at = pl.ds(piece * PIECE, PIECE)
         copy = pltpu.make_async_copy(
-            result.at[:, :, at, :], out_ref.at[:, :, at, :], out_sem.at[piece]
+            result.at[:, :, pl.ds(piece * PIECE, PIECE), :],
+            out_ref.at[:, :, pl.ds(pl.multiple_of(base + piece * PIECE, 8), PIECE), :],
+            out_sem.at[1 + piece],
         )
         copy.start()
-        pieces.append(copy)
-    for copy in plane_out + pieces:
+        copies.append(copy)
+    for copy in copies:
         copy.wait()
 
 
-def backward(lhs, count, amp, wide, grad, planes, rows):
+def backward(lhs, count, amp, wide, grad, planes, done, rows):
     members, modes, _, cols = amp.shape
     lev_dev, own = planes.shape[2:4]
     vmem = pl.BlockSpec(memory_space=pltpu.VMEM)
@@ -115,22 +122,22 @@
     field = jax.ShapeDtypeStruct((lev_dev, own, 2 * cols), F32)
     return pl.pallas_call(
         backward_kernel,
-        in_specs=[vmem] * 6,
+        in_specs=[vmem] * 7,
         out_specs=[anywhere] * 3,
         out_shape=[jax.ShapeDtypeStruct((members, modes, rows, cols), F32), field, field],
         scratch_shapes=[
-            pltpu.VMEM(amp.shape, F32),
-            pltpu.SemaphoreType.DMA((rows // PIECE,)),
+            pltpu.VMEM(done.shape, F32),
+            pltpu.SemaphoreType.DMA((1 + rows // (2 * PIECE),)),
             pltpu.SemaphoreType.DMA((4,)),
         ],
-        compiler_params=pltpu.CompilerParams(vmem_limit_bytes=12 << 20),
+        compiler_params=pltpu.CompilerParams(vmem_limit_bytes=6 << 20),
         name="backward_modes",
-    )(lhs, count, amp, wide, grad, planes)
+    )(lhs, count, amp, wide, grad, planes, done)
 
 
 def exchange_kernel(
     sizes,
-    lhs_ref,
+    modes_in,
     count_in,
     amp_ref,
     pert_ref,
@@ -148,6 +155,9 @@
     shares,
     planes_out,
     count_ref,
+    back_lhs_ref,
+    done,
+    modes_ref,
     tile,
     narrow,
     core_in,
@@ -237,6 +247,8 @@
 
     count_load = pltpu.make_async_copy(count_in, count_ref, small_sem.at[7])
     count_load.start()
+    modes_load = pltpu.make_async_copy(modes_in, modes_ref, small_sem.at[8])
+    modes_load.start()
     pert_in, amp_in = [], []
 
     def load_half(half):
@@ -319,7 +331,13 @@
 
     amps = amp_out.reshape(members * modes * PITCH, 128)
     perts = wide.reshape(members * levels * PITCH, 128)
-    lhs = lhs_ref[...]
+    modes_load.wait()
+    scaled = modes_ref[...] * (1.0 / math.sqrt(MEMBERS - 1))
+    scaled_hi = scaled.astype(BF16).astype(F32)
+    scaled_lo = scaled - scaled_hi
+    lhs = jnp.concatenate([scaled_hi, scaled_lo, scaled_hi], axis=0).T.astype(BF16)
+    back_lhs = jnp.concatenate([scaled_hi, scaled_lo, scaled_hi], axis=1).astype(BF16)
+    back_lhs_ref[...] = back_lhs
     mode = lax.broadcasted_iota(jnp.int32, (modes, 128), 0)
 
     def contract(start):
@@ -617,23 +635,58 @@
     ring_own = to_ring_of(x_rows(y, x))
     core = [to_all(pl.ds(mine, ROWS), to_core)]
 
+    dones = done.reshape(members * modes * HALF_PITCH, 128)
+
+    def project(rx):
+        def row_pair(step, carry):
+            row = rx * ROWS + step * 2
+            project_row_pair(
+                back_lhs,
+                count_ref,
+                amps,
+                perts,
+                dones,
+                shares,
+                (members, modes, levels),
+                y * half_rows + row,
+                row,
+            )
+            return carry
+
+        lax.fori_loop(0, ROWS // 2, row_pair, 0, unroll=3)
+
     sweep(field_a, field_b)
+    core[0].wait_recv()
+    project(x)
     sweep(field_b, field_a, 0, 3)
     pair_first.wait_recv()
     ring_other = to_ring_of(x_rows(other_y, x))
     core.append(to_all(x_rows(other_y, x), to_core))
+    core_y, core_x = [], []
     for copy, rx in zip(ring_y, origins):
         copy.wait_recv()
         pair_y.append(to_all(y_rows(y, rx), to_y))
-        core.append(to_all(y_rows(y, rx), to_core))
+        core_y.append(to_all(y_rows(y, rx), to_core))
     sweep(field_b, field_a, 3, 7)
     sweep(field_a, field_b, 0, 3)
     for copy, rx in zip(ring_own, origins):
         copy.wait_recv()
-        core.append(to_all(x_rows(y, rx), to_core))
+        core_x.append(to_all(x_rows(y, rx), to_core))
     pair_y[0].wait_recv()
     core.append(to_all(y_rows(other_y, x), to_core))
     sweep(field_a, field_b, 3, 7)
+
+    def project_origin(number):
+        core_x[number].wait_recv()
+        core_y[number].wait_recv()
+        project(origins[number])
+
+    def pass_on(number):
+        pair_y[1 + number].wait_recv()
+        core.append(to_all(y_rows(other_y, origins[number]), to_core))
+
+    project_origin(0)
+    pass_on(0)
 
     def finish(i, carry):
         at = pl.ds(i, lev_dev, stride=own)
@@ -645,13 +698,14 @@
         return carry
 
     lax.fori_loop(0, own, finish, 0, unroll=8)
-    for copy, rx in zip(pair_y[1:], origins):
-        copy.wait_recv()
-        core.append(to_all(y_rows(other_y, rx), to_core))
+    project_origin(1)
+    pass_on(1)
+    project_origin(2)
+    pass_on(2)
     for copy, rx in zip(ring_other, origins):
         copy.wait_recv()
         core.append(to_all(x_rows(other_y, rx), to_core))
-    for copy in core:
+    for copy in core[1:]:
         copy.wait_recv()
     waited = halo_sends[2:] + halo_again[:2]
     for copy in sent:
@@ -659,7 +713,7 @@
             copy.wait_send()
 
 
-def exchange(sizes, lhs, count, amp, pert, control, innov, std, spread, land, row_index, row_weight, col_index, col_weight):
+def exchange(sizes, modes_t, count, amp, pert, control, innov, std, spread, land, row_index, row_weight, col_index, col_weight):
     members, modes, rows, cols = amp.shape
     levels = pert.shape[1]
     lev_dev, own, cols_fine = control.shape
@@ -670,16 +724,19 @@
     tile = (2, rows) + cell
     return pl.pallas_call(
         functools.partial(exchange_kernel, sizes),
-        in_specs=[vmem] + [anywhere] * 12,
-        out_specs=[vmem] * 5,
+        in_specs=[anywhere] * 13,
+        out_specs=[vmem] * 7,
         out_shape=[
             pltpu.VMEM((members, modes, PITCH, cols), F32),
             pltpu.VMEM((members, levels, PITCH, cols), F32),
             pltpu.VMEM(tile, F32),
             pltpu.VMEM((2, 2, lev_dev, own, 128), F32),
             pltpu.VMEM(count.shape, jnp.int32),
+            pltpu.VMEM((modes, 3 * levels), BF16),
+            pltpu.VMEM((members, modes, HALF_PITCH, cols), F32),
         ],
         scratch_shapes=[
+            pltpu.VMEM(modes_t.shape, F32),
             pltpu.VMEM(tile, F32),
             pltpu.VMEM(pert.shape, BF16),
             pltpu.VMEM((rows,) + cell, F32),
@@ -711,17 +768,17 @@
             pltpu.SemaphoreType.DMA((80,)),
             pltpu.SemaphoreType.DMA((2 * members + 4,)),
             pltpu.SemaphoreType.DMA((4,)),
-            pltpu.SemaphoreType.DMA((8,)),
+            pltpu.SemaphoreType.DMA((9,)),
         ],
         compiler_params=pltpu.CompilerParams(
-            collective_id=0, has_side_effects=True, vmem_limit_bytes=24 << 20
+            collective_id=0, has_side_effects=True, vmem_limit_bytes=18 << 20
         ),
         name="exchange",
     )(
-        lhs,
         *(
             pltpu.with_memory_space_constraint(operand, pltpu.HBM)
             for operand in (
+                modes_t,
                 count,
                 amp,
                 pert,
@@ -759,11 +816,9 @@
         lax.axis_size("fine"),
         lax.axis_size("coarse") * lax.axis_size("fine") * row_index.shape[0],
     )
-    scaled = eigen_modes * (1.0 / math.sqrt(MEMBERS - 1))
-    tall, across = split_modes(scaled.T)
-    amp, wide, coarse_grad, planes, count = exchange(
+    amp, wide, coarse_grad, planes, count, back_lhs, done = exchange(
         sizes,
-        tall,
+        eigen_modes.T,
         mode_count,
         ens_control,
         ens_pert,
@@ -778,7 +833,7 @@
         col_weight,
     )
     grad_ens, grad_static, increment = backward(
-        across, count, amp, wide, coarse_grad, planes, mode_count.shape[0]
+        back_lhs, count, amp, wide, coarse_grad, planes, done, mode_count.shape[0]
     )
     return increment, grad_static, grad_ens
 

time: 54.8 us -> 52 us (0.949)
  the two profiles are of different devices: /device:TPU:1 before, /device:TPU:5 now
where the time goes in v6:
time: 52 us; the launch traced here: 51.9 us
  Pallas kernels  51.2 us (98%)
  between operations  0.64 us (1%)
    pallas_call x1, Pallas kernels, exchange(): pl.pallas_call(functools.partial(exchange_kernel, sizes), in_specs=[anywh...  46.9 us
    pallas_call x1, Pallas kernels, backward(): pl.pallas_call(backward_kernel, in_specs=[vmem] * 7, out_specs=[anywhere]...  4.39 us

profile of v6, /device:TPU:5, one launch (start us, length us, event | category | flops | bytes accessed | tf_op | source)
XLA Modules:
  0.0 51.9 jit_solution(8900553799286770782)
XLA Ops:
  0.6 46.9 %exchange.1 = (f32[5,32,104,128]{3,2,1,0:T(8,128)S(1)}, f32[5,48,104,128]{3,2,1,0:T(8,128)S(1)}, f32[2,96,24,128]{3,2,1,0:T(8,128)S(1)}, f32[2,2,24,24,128]{4,3,...) custom-call(f32[32,48]{1,0:T(8,128)} %bitcast.3, ...), custom_call_target="tpu_custom_call" | custom-call | tf_op jit(solution)/shard_map/exchange/pallas_call | solution.py:725
  47.5 4.4 %backward_modes.1 = (f32[5,32,96,128]{3,2,1,0:T(8,128)}, f32[24,24,256]{2,1,0:T(8,128)}, f32[24,24,256]{2,1,0:T(8,128)}) custom-call(bf16[32,144]{1,0:T(8,128)(2,1)S(1)} %get-tuple-element.13.lhs_ref, s32[96,128]{1,0:T(8,128)S(1)} %get-tuple-element.14.count_ref, f32[5,32,104,128]{3,2,1,0:T(8,128)S(1)} %get-tuple-element.15.amp_ref, ...), custom_call_target="tpu_custom_call" | custom-call | tf_op jit(solution)/shard_map/backward_modes/pallas_call | solution.py:123

commit v7 on v6

--- a/solution.py
+++ b/solution.py
@@ -505,7 +505,9 @@
         weights[2, e] = jnp.where(upper_on, weight, 0.0) * inside
         return carry
 
-    lax.fori_loop(0, GROWN - 1, coefficients, 0, unroll=4)
+    lax.fori_loop(0, 15, coefficients, 0, unroll=5)
+    settle_pair(2)
+    lax.fori_loop(15, GROWN - 1, coefficients, 0, unroll=4)
     inner = pl.ds(1, GROWN - 2)
     centre[inner] = centre[inner] - row_faces[pl.ds(0, GROWN - 2)]
     for j in range(3):
@@ -537,7 +539,6 @@
 
         lax.fori_loop(first, last, rows_of_four, 0)
 
-    settle_pair(2)
     settle(7)
     for copy in halo_sends[2:]:
         copy.wait_recv()
@@ -655,38 +656,37 @@
 
         lax.fori_loop(0, ROWS // 2, row_pair, 0, unroll=3)
 
-    sweep(field_a, field_b)
-    core[0].wait_recv()
-    project(x)
-    sweep(field_b, field_a, 0, 3)
-    pair_first.wait_recv()
-    ring_other = to_ring_of(x_rows(other_y, x))
-    core.append(to_all(x_rows(other_y, x), to_core))
     core_y, core_x = [], []
-    for copy, rx in zip(ring_y, origins):
-        copy.wait_recv()
-        pair_y.append(to_all(y_rows(y, rx), to_y))
-        core_y.append(to_all(y_rows(y, rx), to_core))
-    sweep(field_b, field_a, 3, 7)
-    sweep(field_a, field_b, 0, 3)
-    for copy, rx in zip(ring_own, origins):
-        copy.wait_recv()
-        core_x.append(to_all(x_rows(y, rx), to_core))
-    pair_y[0].wait_recv()
-    core.append(to_all(y_rows(other_y, x), to_core))
-    sweep(field_a, field_b, 3, 7)
+
+    def share_y(number):
+        ring_y[number].wait_recv()
+        rows = y_rows(y, origins[number])
+        pair_y.append(to_all(rows, to_y))
+        core_y.append(to_all(rows, to_core))
+
+    def share_x(number):
+        ring_own[number].wait_recv()
+        core_x.append(to_all(x_rows(y, origins[number]), to_core))
+
+    def pass_on(number):
+        pair_y[number].wait_recv()
+        core.append(to_all(y_rows(other_y, (x, *origins)[number]), to_core))
 
     def project_origin(number):
         core_x[number].wait_recv()
         core_y[number].wait_recv()
         project(origins[number])
 
-    def pass_on(number):
-        pair_y[1 + number].wait_recv()
-        core.append(to_all(y_rows(other_y, origins[number]), to_core))
-
-    project_origin(0)
-    pass_on(0)
+    sweep(field_a, field_b)
+    core[0].wait_recv()
+    project(x)
+    sweep(field_b, field_a)
+    pair_first.wait_recv()
+    ring_other = to_ring_of(x_rows(other_y, x))
+    core.append(to_all(x_rows(other_y, x), to_core))
+    share_y(0)
+    share_y(1)
+    sweep(field_a, field_b)
 
     def finish(i, carry):
         at = pl.ds(i, lev_dev, stride=own)
@@ -698,13 +698,20 @@
         return carry
 
     lax.fori_loop(0, own, finish, 0, unroll=8)
+    share_y(2)
+    share_x(0)
+    share_x(1)
+    pass_on(0)
+    project_origin(0)
+    share_x(2)
+    pass_on(1)
     project_origin(1)
-    pass_on(1)
-    project_origin(2)
     pass_on(2)
+    pass_on(3)
     for copy, rx in zip(ring_other, origins):
         copy.wait_recv()
         core.append(to_all(x_rows(other_y, rx), to_core))
+    project_origin(2)
     for copy in core[1:]:
         copy.wait_recv()
     waited = halo_sends[2:] + halo_again[:2]

time: 52 us -> 50.9 us (0.979)
  the two profiles are of different devices: /device:TPU:5 before, /device:TPU:1 now
where the time goes in v7:
time: 50.9 us; the launch traced here: 50.8 us
  Pallas kernels  50.1 us (98%)
  between operations  0.64 us (1%)
    pallas_call x1, Pallas kernels, exchange(): pl.pallas_call(functools.partial(exchange_kernel, sizes), in_specs=[anywh...  45.7 us
    pallas_call x1, Pallas kernels, backward(): pl.pallas_call(backward_kernel, in_specs=[vmem] * 7, out_specs=[anywhere]...  4.39 us

profile of v7, /device:TPU:1, one launch (start us, length us, event | category | flops | bytes accessed | tf_op | source)
XLA Modules:
  0.0 50.8 jit_solution(6066637350640031328)
XLA Ops:
  0.6 45.7 %exchange.1 = (f32[5,32,104,128]{3,2,1,0:T(8,128)S(1)}, f32[5,48,104,128]{3,2,1,0:T(8,128)S(1)}, f32[2,96,24,128]{3,2,1,0:T(8,128)S(1)}, f32[2,2,24,24,128]{4,3,...) custom-call(f32[32,48]{1,0:T(8,128)} %bitcast.3, ...), custom_call_target="tpu_custom_call" | custom-call | tf_op jit(solution)/shard_map/exchange/pallas_call | solution.py:732
  46.4 4.4 %backward_modes.1 = (f32[5,32,96,128]{3,2,1,0:T(8,128)}, f32[24,24,256]{2,1,0:T(8,128)}, f32[24,24,256]{2,1,0:T(8,128)}) custom-call(bf16[32,144]{1,0:T(8,128)(2,1)S(1)} %get-tuple-element.13.lhs_ref, s32[96,128]{1,0:T(8,128)S(1)} %get-tuple-element.14.count_ref, f32[5,32,104,128]{3,2,1,0:T(8,128)S(1)} %get-tuple-element.15.amp_ref, ...), custom_call_target="tpu_custom_call" | custom-call | tf_op jit(solution)/shard_map/backward_modes/pallas_call | solution.py:123

commit v8 on v7

--- a/solution.py
+++ b/solution.py
@@ -271,18 +271,6 @@
             copy.start()
             amp_in.append(copy)
 
-    load_half(0)
-    plane_in = [
-        [
-            pltpu.make_async_copy(
-                ref.at[:, :, lanes[side]],
-                planes_in.at[number, side],
-                plane_sem.at[2 * number + side],
-            )
-            for side in range(2)
-        ]
-        for number, ref in enumerate((control_ref, innov_ref))
-    ]
     small_in = [
         pltpu.make_async_copy(src, dst, small_sem.at[number])
         for number, (src, dst) in enumerate(
@@ -297,7 +285,21 @@
             )
         )
     ]
-    for copy in small_in + plane_in[0]:
+    for copy in small_in:
+        copy.start()
+    load_half(0)
+    plane_in = [
+        [
+            pltpu.make_async_copy(
+                ref.at[:, :, lanes[side]],
+                planes_in.at[number, side],
+                plane_sem.at[2 * number + side],
+            )
+            for side in range(2)
+        ]
+        for number, ref in enumerate((control_ref, innov_ref))
+    ]
+    for copy in plane_in[0]:
         copy.start()
     load_half(1)
     for copy in plane_in[1]:
@@ -397,6 +399,23 @@
         if place < 3:
             to_own.append(remote(sums.at[y_rows(y, rx)], y_in.at[place], ring[place][1]))
 
+    for copy in small_in:
+        copy.wait()
+    for ref in (cells, misfit):
+        ref[0] = jnp.zeros(ref.shape[1:], F32)
+        ref[GROWN - 1] = jnp.zeros(ref.shape[1:], F32)
+    for row in (1, GROWN - 2):
+        field_b[row] = jnp.zeros(field_b.shape[1:], F32)
+    for lev_at in range(lev_dev):
+        sigma[lev_at : lev_at + 1, :] = jnp.full((1, 256), std_ref[lev_at], F32)
+    for j in range(3):
+        weights[j, GROWN - 1] = jnp.zeros((8, 128), F32)
+    col = lax.broadcasted_iota(jnp.int32, (128, 256), 0)
+    col_at, col_w = col_index_ref[...], col_weight_ref[...]
+    matrix = jnp.where(col == col_at, 1.0 - col_w, jnp.where(col == col_at + 1, col_w, 0.0))
+    hi, lo = halves(matrix)
+    col_mat[0], col_mat[1] = hi, lo
+
     count_load.wait()
     widen(0)
     amp_in[0].wait()
@@ -414,7 +433,7 @@
     settle(1)
     settle(2)
 
-    for copy in small_in + plane_in[0]:
+    for copy in plane_in[0]:
         copy.wait()
 
     def load_rows(i, carry):
@@ -464,13 +483,6 @@
     add(x_rows(other_y, x), x_in.at[0, 0], x_in.at[0, 1], x_in.at[0, 2])
     pair_x = remote(sums.at[x_rows(other_y, x)], pair_x_in, to_y)
 
-    for ref in (cells, misfit):
-        ref[0] = jnp.zeros(ref.shape[1:], F32)
-        ref[GROWN - 1] = jnp.zeros(ref.shape[1:], F32)
-    for row in (1, GROWN - 2):
-        field_b[row] = jnp.zeros(field_b.shape[1:], F32)
-    for lev_at in range(lev_dev):
-        sigma[lev_at : lev_at + 1, :] = jnp.full((1, 256), std_ref[lev_at], F32)
     for copy in halo_sends[:2]:
         copy.wait_recv()
 
@@ -510,14 +522,6 @@
     lax.fori_loop(15, GROWN - 1, coefficients, 0, unroll=4)
     inner = pl.ds(1, GROWN - 2)
     centre[inner] = centre[inner] - row_faces[pl.ds(0, GROWN - 2)]
-    for j in range(3):
-        weights[j, GROWN - 1] = jnp.zeros((8, 128), F32)
-    col = lax.broadcasted_iota(jnp.int32, (128, 256), 0)
-    col_at, col_w = col_index_ref[...], col_weight_ref[...]
-    matrix = jnp.where(col == col_at, 1.0 - col_w, jnp.where(col == col_at + 1, col_w, 0.0))
-    hi, lo = halves(matrix)
-    col_mat[0], col_mat[1] = hi, lo
-
     def sweep(src, dst, first=0, last=7):
         def rows_of_four(step, carry):
             e = EDGE - 2 + 4 * step

time: 50.9 us -> 51.8 us (1.018)
  Pallas kernels: 50.1 us -> 51 us
    pallas_call x1, Pallas kernels: 45.7 us -> 46.6 us  [exchange(): pl.pallas_call(functools.partial(exchange_kernel, sizes), in_specs=[anywh...]
where the time goes in v8:
time: 51.8 us; the launch traced here: 51.7 us
  Pallas kernels  51 us (98%)
  between operations  0.64 us (1%)
    pallas_call x1, Pallas kernels, exchange(): pl.pallas_call(functools.partial(exchange_kernel, sizes), in_specs=[anywh...  46.6 us
    pallas_call x1, Pallas kernels, backward(): pl.pallas_call(backward_kernel, in_specs=[vmem] * 7, out_specs=[anywhere]...  4.39 us

profile of v8, /device:TPU:1, one launch (start us, length us, event | category | flops | bytes accessed | tf_op | source)
XLA Modules:
  0.0 51.7 jit_solution(1219398261828203957)
XLA Ops:
  0.6 46.6 %exchange.1 = (f32[5,32,104,128]{3,2,1,0:T(8,128)S(1)}, f32[5,48,104,128]{3,2,1,0:T(8,128)S(1)}, f32[2,96,24,128]{3,2,1,0:T(8,128)S(1)}, f32[2,2,24,24,128]{4,3,...) custom-call(f32[32,48]{1,0:T(8,128)} %bitcast.3, ...), custom_call_target="tpu_custom_call" | custom-call | tf_op jit(solution)/shard_map/exchange/pallas_call | solution.py:736
  47.3 4.4 %backward_modes.1 = (f32[5,32,96,128]{3,2,1,0:T(8,128)}, f32[24,24,256]{2,1,0:T(8,128)}, f32[24,24,256]{2,1,0:T(8,128)}) custom-call(bf16[32,144]{1,0:T(8,128)(2,1)S(1)} %get-tuple-element.13.lhs_ref, s32[96,128]{1,0:T(8,128)S(1)} %get-tuple-element.14.count_ref, f32[5,32,104,128]{3,2,1,0:T(8,128)S(1)} %get-tuple-element.15.amp_ref, ...), custom_call_target="tpu_custom_call" | custom-call | tf_op jit(solution)/shard_map/backward_modes/pallas_call | solution.py:123
